TPU v7x, 32 devices: a whole 2x2x4 slice. The times are simulated.
32 devices in a mesh: row: 8 (over z, x), col: 4 (over y, core).
Axes of the slice: x: 2, y: 2, z: 4, core: 2. Of those that a mesh axis runs over, the one named last changes fastest.
Arguments:
- acts: bfloat16 [512, 5120], P('col', 'row'), may hold values from -60 to 60
- out_grads: bfloat16 [512, 13824], P('row', 'col'), may hold values from -0.1237436867076458 to 0.1237436867076458
- momentum: float32 [5120, 13824], P('row', 'col'), may hold values from -200 to 200
- weight: float32 [5120, 13824], P('row', 'col'), may hold values from -0.078125 to 0.078125
Outputs:
- momentum_new: float32 [5120, 13824], P('row', 'col')
- update: bfloat16 [5120, 13824], P('row', 'col')
- weight_new: float32 [5120, 13824], P('row', 'col')
All inputs are finite; a program needn't handle non-finite values.
Results may differ from a plain program's by a relative error of at most 0.014.
Values may be sent and summed in bfloat16 or wider, within the bound.
No kernel may reach another device: no remote copies, remote signals or barrier semaphores. Data moves between devices by JAX's collectives and lax.ppermute only.
A program may use at most 192 MiB of HBM per device.

v0:
```python
import math

import jax
import jax.numpy as jnp
from jax import lax
from jax.sharding import PartitionSpec as P

D = 5120


def body(acts, out_grads, momentum, weight):
    token_acts = lax.all_gather(acts, "col", axis=0, tiled=True)
    slab_rows = token_acts
    gradient = lax.dot_general(
        slab_rows,
        lax.all_gather(out_grads, "row", axis=0, tiled=True),
        (((0,), (0,)), ((), ())),
        preferred_element_type=jnp.float32,
    )
    momentum_new = 0.95 * momentum + gradient
    blended = gradient + 0.95 * momentum_new
    rounded = blended.astype(jnp.bfloat16)
    col_panel = lax.all_gather(rounded, "row", axis=0, tiled=True)
    slab_rows = col_panel
    gram_tile = lax.psum_scatter(
        lax.dot_general(
            slab_rows, rounded, (((1,), (1,)), ((), ())), preferred_element_type=jnp.float32
        ).astype(jnp.bfloat16),
        "col",
        scatter_dimension=0,
        tiled=True,
    )
    gram_cols = lax.all_gather(gram_tile, "col", axis=0, tiled=True)
    gram_rows = lax.all_gather(gram_tile, "row", axis=1, tiled=True)
    gram_square = jnp.dot(gram_rows, gram_cols, preferred_element_type=jnp.float32)
    total_sum = lax.psum(jnp.sum(gram_square * gram_square), ("row", "col"))
    schatten = jnp.sqrt(total_sum + 1e-06)
    square_root = jnp.sqrt(schatten)
    fourth_root = jnp.sqrt(square_root)
    poly_tile = (
        -4.775 * gram_tile.astype(jnp.float32) / square_root + 2.0315 * gram_square / schatten
    ).astype(jnp.bfloat16)
    poly_cols = lax.all_gather(poly_tile, "col", axis=0, tiled=True)
    product = lax.dot_general(
        poly_cols, col_panel, (((0,), (0,)), ((), ())), preferred_element_type=jnp.float32
    )
    orthogonal = (3.4445 * rounded.astype(jnp.float32) + product) / fourth_root
    factor = math.sqrt(D)
    update = (factor * orthogonal).astype(jnp.bfloat16)
    weight_new = 0.998 * weight - 0.02 * factor * orthogonal
    return (momentum_new, update, weight_new)


def solution(mesh):
    in_specs = (P("col", "row"), P("row", "col"), P("row", "col"), P("row", "col"))
    out_specs = (P("row", "col"), P("row", "col"), P("row", "col"))
    return jax.shard_map(body, mesh=mesh, in_specs=in_specs, out_specs=out_specs, check_vma=False)
```

profile of v0, /device:TPU:27, one launch (start us, length us, event | category | flops | bytes accessed | tf_op | source)
XLA Modules:
  0.0 1243.7 jit_solution(14039994435617294925)
XLA Ops:
  7.2 0.0 all-gather.6.cloned.1.call-start
  7.2 0.7 all-gather.6.cloned.1.call-update
  7.9 0.0 all-gather.8.cloned.1.call-start
  7.9 8.6 all_gather.18
  16.6 57.4 %all-gather.6.cloned.1.call-done = bf16[512,3456]{1,0:T(8,128)(2,1)} async-done(((bf16[64,3456]{1,0:T(8,128)(2,1)}), bf16[512,3456]{1,0:T(8,128)(2,1)}) %all-gather.6.cloned.1.call-update) | async-done | bytes 3538960 | tf_op jit(solution)/shard_map/all_gather | solution.py:16
  74.0 12.9 %add_convert_fusion = (bf16[640,3456]{1,0:T(8,128)(2,1)}, f32[640,3456]{1,0:T(8,128)}) fusion(f32[640,3456]{1,0:T(8,128)} %param.6, bf16[512,640]{1,0:T(8,128)(2,1)S(1)} %all_gather.18, bf16[512,3456]{1,0:T(8,128)(2,1)} %all-gather.6.cloned.1.call-done), kind=kOutput, calls=%fused_computation.3 | convolution fusion | flops 2275983360 | bytes 26312704 | tf_op jit(solution)/shard_map/dot_general | solution.py:14
  86.9 0.0 all-gather.8.cloned.1.call-update
  87.0 0.0 reduce-scatter.2.cloned.1.call-start
  87.0 672.1 %all-gather.8.cloned.1.call-done = bf16[5120,3456]{1,0:T(8,128)(2,1)} async-done(((bf16[640,3456]{1,0:T(8,128)(2,1)}), bf16[5120,3456]{1,0:T(8,128)(2,1)}) %all-gather.8.cloned.1.call-update) | async-done | bytes 35389456 | tf_op jit(solution)/shard_map/all_gather | solution.py:23
  759.1 34.4 %convolution_convert_fusion = bf16[5120,640]{1,0:T(8,128)(2,1)} fusion(bf16[5120,3456]{1,0:T(8,128)(2,1)} %all-gather.8.cloned.1.call-done, bf16[640,3456]{1,0:T(8,128)(2,1)} %get-tuple-element.3), kind=kOutput, calls=%fused_computation.5 | convolution fusion | flops 22652518400 | bytes 46366720 | tf_op jit(solution)/shard_map/dot_general | solution.py:26
  793.6 0.0 reduce-scatter.2.cloned.1.call-update
  793.6 0.0 all-gather.12.cloned.1.call-start
  793.6 61.2 %reduce-scatter.2.cloned.1.call-done = bf16[1280,640]{1,0:T(8,128)(2,1)} async-done(((bf16[5120,640]{1,0:T(8,128)(2,1)}), bf16[1280,640]{1,0:T(8,128)(2,1)}) %reduce-scatter.2.cloned.1.call-update) | async-done | bytes 1638416 | tf_op jit(solution)/shard_map/reduce_scatter | solution.py:25
  854.8 0.0 all-gather.12.cloned.1.call-update
  854.8 0.0 all-gather.10.cloned.1.call-start
  854.8 0.5 all-gather.10.cloned.1.call-update
  855.4 0.0 copy-start
  855.4 0.0 all-gather.14.cloned.1.call-start
  855.4 49.2 %all-gather.12.cloned.1.call-done = bf16[5120,640]{1,0:T(8,128)(2,1)} async-done(((bf16[1280,640]{1,0:T(8,128)(2,1)}), bf16[5120,640]{1,0:T(8,128)(2,1)}) %all-gather.12.cloned.1.call-update) | async-done | bytes 6553616 | tf_op jit(solution)/shard_map/all_gather | solution.py:33
  904.6 182.1 %all-gather.10.cloned.1.call-done = bf16[1280,5120]{1,0:T(8,128)(2,1)} async-done(((bf16[1280,640]{1,0:T(8,128)(2,1)}), bf16[1280,5120]{1,0:T(8,128)(2,1)}) %all-gather.10.cloned.1.call-update) | async-done | bytes 13107216 | tf_op jit(solution)/shard_map/all_gather | solution.py:34
  1086.7 16.7 %multiply_reduce_fusion = (f32[]{:T(128)}, f32[1280,640]{1,0:T(8,128)}) fusion(bf16[1280,5120]{1,0:T(8,128)(2,1)} %all-gather.10.cloned.1.call-done, bf16[5120,640]{1,0:T(8,128)(2,1)} %all-gather.12.cloned.1.call-done), kind=kOutput, calls=%fused_computation.7 | convolution fusion | flops 8390246400 | bytes 22937604 | tf_op jit(solution)/shard_map/dot_general | solution.py:35
  1103.4 40.7 %psum.7 = f32[]{:T(128)} all-reduce(f32[]{:T(128)} %get-tuple-element.7), channel_id=1, replica_groups=mesh['row'=8,'col'=4] {'row','col'}, use_global_device_ids=true, to_apply=%region_2.0 | all-reduce | flops 1 | bytes 8 | tf_op jit(solution)/shard_map/psum | solution.py:36
  1144.8 0.0 copy-done
  1144.8 3.8 add_convert_fusion.1
  1148.6 0.0 all-gather.14.cloned.1.call-update
  1148.7 50.1 %all-gather.14.cloned.1.call-done = bf16[5120,640]{1,0:T(8,128)(2,1)} async-done(((bf16[1280,640]{1,0:T(8,128)(2,1)}), bf16[5120,640]{1,0:T(8,128)(2,1)}) %all-gather.14.cloned.1.call-update) | async-done | bytes 6553616 | tf_op jit(solution)/shard_map/all_gather | solution.py:43
  1198.8 38.1 %multiply_subtract_fusion = (f32[640,3456]{1,0:T(8,128)}, bf16[640,3456]{1,0:T(8,128)(2,1)}) fusion(f32[640,3456]{1,0:T(8,128)} %param.7, f32[]{:T(128)S(6)} %sqrt.11, bf16[5120,640]{1,0:T(8,128)(2,1)} %all-gather.14.cloned.1.call-done, bf16[5120,3456]{1,0:T(8,128)(2,1)} %all-gather.8.cloned.1.call-done, bf16[640,3456]{1,0:T(8,128)(2,1)} %get-tuple-element.3), kind=kOutput, calls=%fused_computation | convolution fusion | flops 22669148160 | bytes 68485120 | tf_op jit(solution)/shard_map/dot_general | solution.py:44
Async XLA Ops:
  7.2 66.8 %all-gather.6.cloned.1.call-start = ((), (), s32[]{:S(2)}) async-start(), calls=%async_computation.1 | async-start | bytes 3981312 | tf_op jit(solution)/shard_map/all_gather | solution.py:16
  7.9 751.2 %all-gather.8.cloned.1.call-start = ((), (), s32[]{:S(2)}) async-start(), calls=%async_computation.2 | async-start | bytes 39813120 | tf_op jit(solution)/shard_map/all_gather | solution.py:23
  87.0 767.8 %reduce-scatter.2.cloned.1.call-start = ((), (), s32[]{:S(2)}) async-start(), calls=%async_computation.3 | async-start | bytes 8192000 | tf_op jit(solution)/shard_map/reduce_scatter | solution.py:25
  793.6 111.0 %all-gather.12.cloned.1.call-start = ((), (), s32[]{:S(2)}) async-start(), calls=%async_computation.5 | async-start | bytes 8192000 | tf_op jit(solution)/shard_map/all_gather | solution.py:33
  854.8 231.9 %all-gather.10.cloned.1.call-start = ((), (), s32[]{:S(2)}) async-start(), calls=%async_computation.4 | async-start | bytes 14745600 | tf_op jit(solution)/shard_map/all_gather | solution.py:34
  855.4 289.4 %copy-start = (bf16[1280,640]{1,0:T(8,128)(2,1)S(1)}, bf16[1280,640]{1,0:T(8,128)(2,1)}, u32[]{:S(2)}) copy-start(bf16[1280,640]{1,0:T(8,128)(2,1)} %reduce-scatter.2.cloned.1.call-done) | copy-start | bytes 4915204
  855.4 343.4 %all-gather.14.cloned.1.call-start = ((), (), s32[]{:S(2)}) async-start(), calls=%async_computation.6 | async-start | bytes 8192000 | tf_op jit(solution)/shard_map/all_gather | solution.py:43
Sparse Core Ops, SparseCore 0:
  10.2 63.7 all-gather.5
  87.1 672.0 all-gather.7
  793.7 61.0 reduce-scatter.1
  856.3 48.2 all-gather.11
  906.9 179.6 all-gather.9
  1148.8 50.0 all-gather.13
where the time goes:
time: 1250 us; the launch traced here: 1240 us
  waiting for transfers between devices  1070 us (86%)
  matrix products  102 us (8%)
  blocking collectives  49.3 us (4%)
  between operations  14.9 us (1%)
    all_gather x1, waiting for transfers between devices, body(): col_panel = lax.all_gather(rounded, 'row', axis=0, tiled=True)  672 us
    all_gather x1, waiting for transfers between devices, body(): gram_rows = lax.all_gather(gram_tile, 'row', axis=1, tiled=True)  182 us
    reduce_scatter x1, waiting for transfers between devices, body(): lax.psum_scatter(lax.dot_general(slab_rows, rounded, (((1,), (1,)), ((),...  61.2 us
    all_gather x1, waiting for transfers between devices, body(): lax.all_gather(out_grads, 'row', axis=0, tiled=True)  57.4 us
    all_gather x1, waiting for transfers between devices, body(): poly_cols = lax.all_gather(poly_tile, 'col', axis=0, tiled=True)  50.1 us
    all_gather x1, waiting for transfers between devices, body(): gram_cols = lax.all_gather(gram_tile, 'col', axis=0, tiled=True)  49.2 us
    psum x1, blocking collectives, body(): total_sum = lax.psum(jnp.sum(gram_square * gram_square), ('row', 'col'))  40.7 us
    dot_general x1, matrix products, body(): lax.dot_general(poly_cols, col_panel, (((0,), (0,)), ((), ())), preferred...  38.1 us
  transfers between devices with their start and end apart: 6, of which 6 were waited for; matrix products, arithmetic and copies ran while one was open for 0% of the time, Pallas kernels for 0%

commit v1 on v0

v1 whole, which is shorter than its diff:
```python
import functools
import math

import jax
import jax.numpy as jnp
from jax import lax
from jax.experimental import pallas as pl
from jax.experimental.pallas import tpu as pltpu
from jax.sharding import PartitionSpec as P

F32 = jnp.float32
BF16 = jnp.bfloat16


def general_body(acts, out_grads, momentum, weight):
    token_acts = lax.all_gather(acts, "col", axis=0, tiled=True)
    token_grads = lax.all_gather(out_grads, "row", axis=0, tiled=True)
    gradient = lax.dot_general(token_acts, token_grads, (((0,), (0,)), ((), ())), preferred_element_type=F32)
    momentum_new = 0.95 * momentum + gradient
    blended = gradient + 0.95 * momentum_new
    rounded = blended.astype(BF16)
    col_panel = lax.all_gather(rounded, "row", axis=0, tiled=True)
    gram_tile = lax.psum_scatter(
        lax.dot_general(col_panel, rounded, (((1,), (1,)), ((), ())), preferred_element_type=F32).astype(BF16),
        "col",
        scatter_dimension=0,
        tiled=True,
    )
    gram_cols = lax.all_gather(gram_tile, "col", axis=0, tiled=True)
    gram_rows = lax.all_gather(gram_tile, "row", axis=1, tiled=True)
    gram_square = jnp.dot(gram_rows, gram_cols, preferred_element_type=F32)
    total_sum = lax.psum(jnp.sum(gram_square * gram_square), ("row", "col"))
    schatten = jnp.sqrt(total_sum + 1e-06)
    square_root = jnp.sqrt(schatten)
    fourth_root = jnp.sqrt(square_root)
    poly_tile = (-4.775 * gram_tile.astype(F32) / square_root + 2.0315 * gram_square / schatten).astype(BF16)
    poly_cols = lax.all_gather(poly_tile, "col", axis=0, tiled=True)
    product = lax.dot_general(poly_cols, col_panel, (((0,), (0,)), ((), ())), preferred_element_type=F32)
    orthogonal = (3.4445 * rounded.astype(F32) + product) / fourth_root
    factor = math.sqrt(col_panel.shape[0])
    update = (factor * orthogonal).astype(BF16)
    weight_new = 0.998 * weight - 0.02 * factor * orthogonal
    return (momentum_new, update, weight_new)


BLOCKS = 8
TILES = 9
PARTS = 3


def row_shift(value, step):
    return lax.ppermute(value, "row", [(i, (i + step) % BLOCKS) for i in range(BLOCKS)])


def swap(value, axis, bit):
    size = 8 if axis == "row" else 4
    return lax.ppermute(value, axis, [(i, i ^ bit) for i in range(size)])


def take(value, dim, index):
    return lax.dynamic_index_in_dim(value, index, dim, keepdims=False)


def halve(value, dim, mine, axis, bit):
    received = swap(take(value, dim, 1 - mine), axis, bit)
    return (take(value, dim, mine).astype(F32) + received.astype(F32)).astype(BF16)


def tile_blocks(step):
    part = step // 12
    group = (step % 12) // 3
    tile = part * 3 + step % 3
    second = (tile >= 5).astype(jnp.int32)
    row = lax.rem(group + tile - second, 8)
    column = lax.rem(group + 4 * second, 8)
    return row, column


def product_kernel(group_ref, x_ref, t0_ref, t1_ref, t2_ref, y_ref, z_ref, dot_ref, ybf_ref):
    second_pass = pl.program_id(0)
    step = pl.program_id(1)
    row, column = tile_blocks(step)
    group = group_ref[0]
    a = lax.rem(row - group + 8, 8)
    b = lax.rem(column - group + 8, 8)

    @pl.when((second_pass == 0) & (step == 0))
    def _():
        y_ref[...] = jnp.zeros_like(y_ref)
        z_ref[...] = jnp.zeros_like(z_ref)

    def apply(tile_ref, source, target):
        target[b] += jnp.dot(source[a], tile_ref[0], preferred_element_type=F32)

        @pl.when(a != b)
        def _():
            target[a] += lax.dot_general(source[b], tile_ref[0], (((1,), (1,)), ((), ())), preferred_element_type=F32)

    for part, tile_ref in enumerate((t0_ref, t1_ref, t2_ref)):
        @pl.when((step // 12 == part) & (second_pass == 0))
        def _():
            apply(tile_ref, x_ref, y_ref)

        @pl.when((step // 12 == part) & (second_pass == 1))
        def _():
            apply(tile_ref, ybf_ref, z_ref)

    @pl.when((second_pass == 0) & (step == 35))
    def _():
        ybf_ref[...] = y_ref[...].astype(BF16)

    @pl.when((second_pass == 1) & (step == 35))
    def _():
        dot_ref[...] = jnp.sum(y_ref[...] * z_ref[...], axis=0).sum(axis=0, keepdims=True)


def products(group, x, tiles):
    blocks, width, rows = x.shape
    def tile_spec(part):
        return pl.BlockSpec((1, rows, rows), lambda p, i, g: (jnp.clip(i - 12 * part, 0, 11), 0, 0))
    whole = pl.BlockSpec((blocks, width, rows), lambda p, i, g: (0, 0, 0))
    return pl.pallas_call(
        product_kernel,
        out_shape=(
            jax.ShapeDtypeStruct(x.shape, F32),
            jax.ShapeDtypeStruct(x.shape, F32),
            jax.ShapeDtypeStruct((1, rows), F32),
        ),
        grid_spec=pltpu.PrefetchScalarGridSpec(
            num_scalar_prefetch=1,
            grid=(2, 36),
            in_specs=[whole, tile_spec(0), tile_spec(1), tile_spec(2)],
            out_specs=(whole, whole, pl.BlockSpec((1, rows), lambda p, i, g: (0, 0))),
            scratch_shapes=[pltpu.VMEM(x.shape, BF16)],
        ),
        compiler_params=pltpu.CompilerParams(
            dimension_semantics=("arbitrary", "arbitrary"), vmem_limit_bytes=60 * 2**20
        ),
        cost_estimate=pl.CostEstimate(
            flops=2 * 2 * 64 * width * rows * rows, bytes_accessed=2 * 36 * rows * rows * 2, transcendentals=0
        ),
    )(group, x, *tiles)


def gather_part(mine, order, place):
    dims = {"x": 0, "k": 1, "y": 3, "zh": 4, "zl": 5}
    moves = {"x": ("row", 1), "zl": ("row", 2), "zh": ("row", 4), "y": ("col", 2), "k": ("col", 1)}
    count, e, rows = mine.shape
    start = [place["x"], place["k"], 0, place["y"], place["zh"], place["zl"], 0, 0]
    buffer = jnp.zeros((2, 2, count, 2, 2, 2, e, rows), BF16)
    current = mine.reshape(1, 1, count, 1, 1, 1, e, rows)
    buffer = lax.dynamic_update_slice(buffer, current, start)
    for name in order:
        dim = dims[name]
        received = swap(current, *moves[name])
        there = list(start)
        there[dim] = 1 - place[name]
        buffer = lax.dynamic_update_slice(buffer, received, there)
        start[dim] = 0
        sizes = list(current.shape)
        sizes[dim] = 2
        current = lax.dynamic_slice(buffer, start, sizes)
    return current


def fast_body(acts, out_grads, momentum, weight):
    row, col = lax.axis_index("row"), lax.axis_index("col")
    z, x, y, core = row // 2, row % 2, col // 2, col % 2
    place = {"x": x, "k": core, "y": y, "zh": z // 2, "zl": z % 2}
    rows, cols = momentum.shape
    quarter = cols // 4
    half = quarter // 2
    e = rows // 8
    group = 2 * x + core

    token_acts = lax.all_gather(acts, "col", axis=0, tiled=True)
    token_grads = lax.all_gather(out_grads, "row", axis=0, tiled=True)
    gradient = lax.dot_general(token_acts, token_grads, (((0,), (0,)), ((), ())), preferred_element_type=F32)
    momentum_new = 0.95 * momentum + gradient
    rounded = (gradient + 0.95 * momentum_new).astype(BF16)
    pieces = rounded.T.reshape(4, quarter, rows)

    panel = jnp.zeros((BLOCKS, 2, quarter, rows), BF16)
    for step in range(4):
        piece = take(pieces, 0, (z + step) % 4)
        if step:
            piece = row_shift(piece, 2 * step)
        source = 2 * ((z - step + 4) % 4)
        beside = swap(piece, "row", 1)
        for block, value in ((source + x, piece), (source + 1 - x, beside)):
            j = (block - group + 8) % 8
            panel = lax.dynamic_update_slice(panel, value[None, None], (j, 0, 0, 0))
            panel = lax.dynamic_update_slice(panel, swap(value, "col", 1)[None, None], (j, 1, 0, 0))
    deep = panel.reshape(BLOCKS, 2 * quarter, rows)

    def tile(i, j):
        return lax.dot_general(deep[i], deep[j], (((0,), (0,)), ((), ())), preferred_element_type=F32).astype(BF16)

    first = jnp.stack([tile(i, 0) for i in range(5)]).reshape(5, 2, 2, 2, e, rows)
    last = jnp.stack([tile(i, 4) for i in range(4, 8)]).reshape(4, 2, 2, 2, e, rows)
    first = halve(first, 1, y, "col", 2)
    last = halve(last, 3, place["zl"], "row", 2)
    first = halve(first, 2, place["zl"], "row", 2)
    last = halve(last, 2, place["zh"], "row", 4)
    first = halve(first, 1, place["zh"], "row", 4)
    last = halve(last, 1, y, "col", 2)
    mine = jnp.concatenate([first, last])

    orders = (("zh", "zl", "y", "x", "k"), ("y", "x", "zh", "zl", "k"), ("x", "zh", "zl", "y", "k"))
    tiles = [
        gather_part(mine[3 * part : 3 * part + 3], order, place).reshape(12, rows, rows)
        for part, order in enumerate(orders)
    ]

    own = lax.dynamic_slice(panel, (0, 0, x * half, 0), (BLOCKS, 1, half, rows))[:, 0]
    one, three, lanes = products(group.astype(jnp.int32).reshape(1), own, tiles)
    total_sum = lax.psum(jnp.sum(lanes), ("row", "col"))
    schatten = jnp.sqrt(total_sum + 1e-06)
    square_root = jnp.sqrt(schatten)
    fourth_root = jnp.sqrt(square_root)
    factor = math.sqrt(rows * BLOCKS)
    update_t = (
        (3.4445 * own.astype(F32) - (4.775 / square_root) * one + (2.0315 / schatten) * three) * (factor / fourth_root)
    ).astype(BF16)

    home = jnp.zeros((BLOCKS, half, rows), BF16)
    for step in range(BLOCKS):
        value = take(update_t, 0, (row + step - group + 8) % 8)
        if step:
            value = row_shift(value, step)
        home = lax.dynamic_update_slice(home, value[None], ((row - step + 8) % 8, 0, 0))
    update = home.reshape(cols, rows).T
    weight_new = 0.998 * weight - 0.02 * update.astype(F32)
    return (momentum_new, update, weight_new)


def solution(mesh):
    spec = P("row", "col")
    in_specs = (P("col", "row"), spec, spec, spec)
    fast = mesh.shape["row"] == 8 and mesh.shape["col"] == 4
    body = fast_body if fast else general_body
    return jax.shard_map(body, mesh=mesh, in_specs=in_specs, out_specs=(spec, spec, spec), check_vma=False)
```

time: 1250 us -> 900 us (0.72)
  waiting for transfers between devices: 1070 us -> 471 us
  local copies, waits for them, and re-layouts: 0.01 us -> 137 us
  Pallas kernels: 0 us -> 114 us
  matrix products: 102 us -> 31.2 us
  starting transfers between devices: 0.23 us -> 49.3 us
  other arithmetic: 3.82 us -> 27.2 us
    all_gather x5 -> x1, waiting for transfers between devices: 1010 us -> 57.4 us  [fast_body(): token_grads = lax.all_gather(out_grads, 'row', axis=0, tiled=True)]
    ppermute x0 -> x43, waiting for transfers between devices: none -> 413 us  [the longest x33 273 us: swap(): return lax.ppermute(value, axis, [(i, i ^ bit) for i in range(size)])]
    pallas_call x0 -> x1, Pallas kernels: none -> 114 us  [products(): pl.pallas_call(product_kernel, out_shape=(jax.ShapeDtypeStruct(x.shape, F...]
    dot_general x4 -> x10, matrix products: 102 us -> 31.2 us  [the longest x9 18.3 us: tile(): lax.dot_general(deep[i], deep[j], (((0,), (0,)), ((), ())), preferred_ele...]
    reduce_scatter x1 -> x0, waiting for transfers between devices: 61.2 us -> none  [body(): lax.psum_scatter(lax.dot_general(slab_rows, rounded, (((1,), (1,)), ((),...]
    ppermute x0 -> x43, starting transfers between devices: none -> 49.3 us  [the longest x33 39.7 us: swap(): return lax.ppermute(value, axis, [(i, i ^ bit) for i in range(size)])]
    dynamic_update_slice x0 -> x40, local copies, waits for them, and re-layouts: none -> 43.4 us  [the longest x15 27.1 us: gather_part(): buffer = lax.dynamic_update_slice(buffer, received, there)]
    unnamed x2 -> x25, local copies, waits for them, and re-layouts: 0.01 us -> 34.7 us
  transfers between devices with their start and end apart: 6 -> 44, of which waited for: 6 -> 20; matrix products, arithmetic and copies ran while one was open for 0% -> 11% of each run, Pallas kernels for 0% -> 0%
where the time goes in v1:
time: 900 us; the launch traced here: 892 us
  waiting for transfers between devices  471 us (52%)
  local copies, waits for them, and re-layouts  137 us (15%)
  Pallas kernels  114 us (13%)
  starting transfers between devices  49.3 us (5%)
  blocking collectives  46.7 us (5%)
  matrix products  31.2 us (3%)
  other arithmetic  27.2 us (3%)
  between operations  15.8 us (2%)
    ppermute x33, waiting for transfers between devices, swap(): return lax.ppermute(value, axis, [(i, i ^ bit) for i in range(size)])  273 us
    ppermute x10, waiting for transfers between devices, row_shift(): lax.ppermute(value, 'row', [(i, (i + step) % BLOCKS) for i in range(BLOCK...  140 us
    pallas_call x1, Pallas kernels, products(): pl.pallas_call(product_kernel, out_shape=(jax.ShapeDtypeStruct(x.shape, F...  114 us
    all_gather x1, waiting for transfers between devices, fast_body(): token_grads = lax.all_gather(out_grads, 'row', axis=0, tiled=True)  57.4 us
    ppermute x33, starting transfers between devices, swap(): return lax.ppermute(value, axis, [(i, i ^ bit) for i in range(size)])  39.7 us
    psum x1, blocking collectives, fast_body(): total_sum = lax.psum(jnp.sum(lanes), ('row', 'col'))  38.1 us
    unnamed x25, local copies, waits for them, and re-layouts  34.7 us
    dynamic_update_slice x15, local copies, waits for them, and re-layouts, gather_part(): buffer = lax.dynamic_update_slice(buffer, received, there)  27.1 us
  transfers between devices with their start and end apart: 44, of which 20 were waited for; matrix products, arithmetic and copies ran while one was open for 11% of the time, Pallas kernels for 0%

profile of v1, /device:TPU:27, one launch (start us, length us, event | category | flops | bytes accessed | tf_op | source)
XLA Modules:
  0.0 892.3 jit_solution(16470111752575302789)
XLA Ops:
  8.0 8.6 all_gather.6
  16.6 57.4 %all-gather.2.cloned.1.call-done = bf16[512,3456]{1,0:T(8,128)(2,1)} async-done(((bf16[64,3456]{1,0:T(8,128)(2,1)}), bf16[512,3456]{1,0:T(8,128)(2,1)}) %all-gather.2.cloned.1.call-update) | async-done | bytes 3538960 | tf_op jit(solution)/shard_map/all_gather | solution.py:177
  74.0 12.9 %fusion = (bf16[3456,640]{0,1:T(8,128)(2,1)}, f32[640,3456]{1,0:T(8,128)}) fusion(f32[640,3456]{1,0:T(8,128)} %param.6, bf16[512,640]{1,0:T(8,128)(2,1)S(1)} %all_gather.6, bf16[512,3456]{1,0:T(8,128)(2,1)} %all-gather.2.cloned.1.call-done), kind=kOutput, calls=%fused_computation.4 | convolution fusion | flops 2275983360 | bytes 26312704 | tf_op jit(solution)/shard_map/dot_general | solution.py:178
  86.9 7.2 copy.24
  103.5 20.3 %collective-permute-done.1 = bf16[864,640]{1,0:T(8,128)(2,1)} collective-permute-done((bf16[864,640]{1,0:T(8,128)(2,1)}, bf16[864,640]{1,0:T(8,128)(2,1)}, u32[]{:S(2)}, u32[]{:S(2)}) %collective-permute-start.1) | collective-permute-done | bytes 1105952 | tf_op jit(solution)/shard_map/ppermute | solution.py:57
  131.3 63.6 %collective-permute-done.7 = bf16[864,640]{1,0:T(8,128)(2,1)S(1)} collective-permute-done((bf16[864,640]{1,0:T(8,128)(2,1)}, bf16[864,640]{1,0:T(8,128)(2,1)S(1)}, u32[]{:S(2)}, u32[]{:S(2)}) %collective-permute-start.7) | collective-permute-done | bytes 1105952 | tf_op jit(solution)/shard_map/ppermute | solution.py:52
  204.6 13.5 %collective-permute-done.9 = bf16[864,640]{1,0:T(8,128)(2,1)S(1)} collective-permute-done((bf16[864,640]{1,0:T(8,128)(2,1)S(1)}, bf16[864,640]{1,0:T(8,128)(2,1)S(1)}, u32[]{:S(2)}, u32[]{:S(2)}) %collective-permute-start.9) | collective-permute-done | bytes 1105952 | tf_op jit(solution)/shard_map/ppermute | solution.py:57
  218.1 6.6 collective-permute-start.10
  224.7 17.1 %collective-permute-done.13 = bf16[864,640]{1,0:T(8,128)(2,1)S(1)} collective-permute-done((bf16[864,640]{1,0:T(8,128)(2,1)S(1)}, bf16[864,640]{1,0:T(8,128)(2,1)S(1)}, u32[]{:S(2)}, u32[]{:S(2)}) %collective-permute-start.13) | collective-permute-done | bytes 1105952 | tf_op jit(solution)/shard_map/ppermute | solution.py:57
  274.4 34.2 %collective-permute-done.23 = bf16[4,2,2,80,640]{4,3,0,1,2:T(8,128)(2,1)} collective-permute-done((bf16[4,2,2,80,640]{4,3,0,1,2:T(8,128)(2,1)}, bf16[4,2,2,80,640]{4,3,0,1,2:T(8,128)(2,1)}, u32[]{:S(2)}, u32[]{:S(2)}) %collective-permute-start.23) | collective-permute-done | bytes 1638432 | tf_op jit(solution)/shard_map/ppermute | solution.py:57
  312.2 7.5 collective-permute-done.15
  323.1 27.7 %collective-permute-done.24 = bf16[4,2,80,640]{3,2,0,1:T(8,128)(2,1)} collective-permute-done((bf16[4,2,80,640]{3,2,0,1:T(8,128)(2,1)S(1)}, bf16[4,2,80,640]{3,2,0,1:T(8,128)(2,1)}, u32[]{:S(2)}, u32[]{:S(2)}) %collective-permute-start.24) | collective-permute-done | bytes 819232 | tf_op jit(solution)/shard_map/ppermute | solution.py:57
  353.5 9.3 %collective-permute-done.25 = bf16[4,80,640]{2,1,0:T(8,128)(2,1)S(1)} collective-permute-done((bf16[4,80,640]{2,1,0:T(8,128)(2,1)S(1)}, bf16[4,80,640]{2,1,0:T(8,128)(2,1)S(1)}, u32[]{:S(2)}, u32[]{:S(2)}) %collective-permute-start.25) | collective-permute-done | bytes 409632 | tf_op jit(solution)/shard_map/ppermute | solution.py:57
  373.8 30.3 %collective-permute-done.17 = bf16[5,80,640]{2,1,0:T(8,128)(2,1)S(1)} collective-permute-done((bf16[5,80,640]{2,1,0:T(8,128)(2,1)S(1)}, bf16[5,80,640]{2,1,0:T(8,128)(2,1)S(1)}, u32[]{:S(2)}, u32[]{:S(2)}) %collective-permute-start.17) | collective-permute-done | bytes 512032 | tf_op jit(solution)/shard_map/ppermute | solution.py:57
  412.7 14.4 %collective-permute-done.18 = bf16[1,1,3,1,1,1,80,640]{7,6,2,5,4,3,1,0:T(8,128)(2,1)S(1)} collective-permute-done((bf16[1,1,3,1,1,1,80,640]{7,6,2,5,4,3,1,0:T(8,128)(2,1)S(1)}, bf16[1,1,3,1,1,1,80,640]{7,6,2,5,4,3,1,0:T(8,128)(2,1)S(1)}, u32[]{:S(2)}, u32[]{:S(2)}) %collective-permute-start.18) | collective-permute-done | bytes 307232 | tf_op jit(solution)/shard_map/ppermute | solution.py:57
  433.4 8.9 collective-permute-done.19
  447.4 38.7 %collective-permute-done.33 = bf16[2,1,3,1,2,1,80,640]{7,6,5,4,3,2,1,0:T(8,128)(2,1)S(1)} collective-permute-done((bf16[2,1,3,1,2,1,80,640]{7,6,5,4,3,2,1,0:T(8,128)(2,1)S(1)}, bf16[2,1,3,1,2,1,80,640]{7,6,5,4,3,2,1,0:T(8,128)(2,1)S(1)}, u32[]{:S(2)}, u32[]{:S(2)}) %collective-permute-start.33) | collective-permute-done | bytes 1228832 | tf_op jit(solution)/shard_map/ppermute | solution.py:57
  491.2 10.7 %collective-permute-done.28 = bf16[2,1,3,2,1,1,80,640]{7,6,5,4,3,2,1,0:T(8,128)(2,1)S(1)} collective-permute-done((bf16[2,1,3,2,1,1,80,640]{7,6,5,4,3,2,1,0:T(8,128)(2,1)S(1)}, bf16[2,1,3,2,1,1,80,640]{7,6,5,4,3,2,1,0:T(8,128)(2,1)S(1)}, u32[]{:S(2)}, u32[]{:S(2)}) %collective-permute-start.28) | collective-permute-done | bytes 1228832 | tf_op jit(solution)/shard_map/ppermute | solution.py:57
  505.1 37.8 %collective-permute-done.34 = bf16[2,1,3,1,2,2,80,640]{7,6,5,4,3,2,1,0:T(8,128)(2,1)S(1)} collective-permute-done((bf16[2,1,3,1,2,2,80,640]{7,6,5,4,3,2,1,0:T(8,128)(2,1)S(1)}, bf16[2,1,3,1,2,2,80,640]{7,6,5,4,3,2,1,0:T(8,128)(2,1)S(1)}, u32[]{:S(2)}, u32[]{:S(2)}) %collective-permute-start.34) | collective-permute-done | bytes 2457632 | tf_op jit(solution)/shard_map/ppermute | solution.py:57
  544.5 5.2 constant_dynamic-slice_fusion
  572.6 5.4 constant_dynamic-update-slice_fusion
  581.4 8.7 constant_dynamic-update-slice_fusion.6
  590.1 114.4 %shard_map.67 = (f32[8,432,640]{2,1,0:T(8,128)}, f32[8,432,640]{2,1,0:T(8,128)}, f32[1,640]{1,0:T(1,128)}) custom-call(s32[1]{0:T(128)} %bitcast.23.group_ref, bf16[8,432,640]{2,1,0:T(8,128)(2,1)} %dynamic-slice_bitcast_fusion.x_ref, bf16[12,640,640]{2,1,0:T(8,128)(2,1)} %bitcast.208, bf16[12,640,640]{2,1,0:T(8,128)(2,1)} %bitcast.67.t1_ref, ...), custom_call_target="tpu_custom_call" | custom-call | flops 45298483200 | bytes 58982400 | tf_op jit(solution)/shard_map/pallas_call | solution.py:122
  705.8 38.1 %psum.7 = f32[]{:T(128)} all-reduce(f32[]{:T(128)} %reduce_sum.9), channel_id=1, replica_groups=mesh['row'=8,'col'=4] {'row','col'}, use_global_device_ids=true, to_apply=%region_1.2 | all-reduce | flops 1 | bytes 8 | tf_op jit(solution)/shard_map/psum | solution.py:217
  744.7 8.5 multiply_convert_fusion
  761.2 10.4 %copy.36 = f32[640,3456]{0,1:T(8,128)} copy(f32[640,3456]{1,0:T(8,128)} %param.7) | data formatting | bytes 17694720 | tf_op args[3]
  776.3 5.7 collective-permute-done.37
  782.8 10.7 %collective-permute-done.38 = bf16[432,640]{1,0:T(8,128)(2,1)S(1)} collective-permute-done((bf16[432,640]{1,0:T(8,128)(2,1)}, bf16[432,640]{1,0:T(8,128)(2,1)S(1)}, u32[]{:S(2)}, u32[]{:S(2)}) %collective-permute-start.38) | collective-permute-done | bytes 552992 | tf_op jit(solution)/shard_map/ppermute | solution.py:52
  794.4 60.2 %collective-permute-done.39 = bf16[432,640]{1,0:T(8,128)(2,1)S(1)} collective-permute-done((bf16[432,640]{1,0:T(8,128)(2,1)}, bf16[432,640]{1,0:T(8,128)(2,1)S(1)}, u32[]{:S(2)}, u32[]{:S(2)}) %collective-permute-start.39) | collective-permute-done | bytes 552992 | tf_op jit(solution)/shard_map/ppermute | solution.py:52
  858.1 7.2 copy.37
  865.3 9.6 %multiply_subtract_fusion = f32[640,3456]{0,1:T(8,128)} fusion(f32[640,3456]{0,1:T(8,128)} %copy.36, bf16[8,432,640]{2,1,0:T(8,128)(2,1)} %bitcast_dynamic-update-slice_fusion.16), kind=kLoop, calls=%fused_computation | loop fusion | flops 8847360 | bytes 22118400 | tf_op jit(solution)/shard_map/sub | solution.py:233
  874.9 10.3 %copy.38 = f32[640,3456]{1,0:T(8,128)} copy(f32[640,3456]{0,1:T(8,128)} %multiply_subtract_fusion) | data formatting | bytes 17694720
  (177 shorter events, 155.4 us)
Async XLA Ops:
  7.2 66.8 %all-gather.2.cloned.1.call-start = ((), (), s32[]{:S(2)}) async-start(), calls=%async_computation | async-start | bytes 3981312 | tf_op jit(solution)/shard_map/all_gather | solution.py:177
  98.2 25.7 %collective-permute-start.1 = (bf16[864,640]{1,0:T(8,128)(2,1)}, bf16[864,640]{1,0:T(8,128)(2,1)}, u32[]{:S(2)}, u32[]{:S(2)}) collective-permute-start(bf16[864,640]{1,0:T(8,128)(2,1)} %get-tuple-element.25), channel_id=1, source_target_pairs={{0,4},{4,0},{8,12},{12,8},{16,20},{20,16},{24,28},{28,24},{1,5},{5... | collective-permute-start | bytes 3317768 | tf_op jit(solution)/shard_map/ppermute | solution.py:57
  99.4 25.9 %collective-permute-start.3 = (bf16[864,640]{1,0:T(8,128)(2,1)S(1)}, bf16[864,640]{1,0:T(8,128)(2,1)S(1)}, u32[]{:S(2)}, u32[]{:S(2)}) collective-permute-start(bf16[864,640]{1,0:T(8,128)(2,1)S(1)} %get-tuple-element.27), channel_id=1, source_target_pairs={{0,8},{4,12},{8,16},{12,20},{16,24},{20,28},{24,0},{28,4},{1,9},{5... | collective-permute-start | bytes 3317768 | tf_op jit(solution)/shard_map/ppermute | solution.py:52
  100.1 29.9 %collective-permute-start = (bf16[864,640]{1,0:T(8,128)(2,1)}, bf16[864,640]{1,0:T(8,128)(2,1)}, u32[]{:S(2)}, u32[]{:S(2)}) collective-permute-start(bf16[864,640]{1,0:T(8,128)(2,1)} %get-tuple-element.25), channel_id=1, source_target_pairs={{0,1},{1,0},{2,3},{3,2},{4,5},{5,4},{6,7},{7,6},{8,9},{9,8},{10,11... | collective-permute-start | bytes 3317768 | tf_op jit(solution)/shard_map/ppermute | solution.py:57
  102.3 92.6 %collective-permute-start.7 = (bf16[864,640]{1,0:T(8,128)(2,1)}, bf16[864,640]{1,0:T(8,128)(2,1)S(1)}, u32[]{:S(2)}, u32[]{:S(2)}) collective-permute-start(bf16[864,640]{1,0:T(8,128)(2,1)} %get-tuple-element.26), channel_id=1, source_target_pairs={{0,16},{4,20},{8,24},{12,28},{16,0},{20,4},{24,8},{28,12},{1,17},{... | collective-permute-start | bytes 3317768 | tf_op jit(solution)/shard_map/ppermute | solution.py:52
  102.9 92.2 %collective-permute-start.11 = (bf16[864,640]{1,0:T(8,128)(2,1)}, bf16[864,640]{1,0:T(8,128)(2,1)S(1)}, u32[]{:S(2)}, u32[]{:S(2)}) collective-permute-start(bf16[864,640]{1,0:T(8,128)(2,1)} %get-tuple-element.24), channel_id=1, source_target_pairs={{0,24},{4,28},{8,0},{12,4},{16,8},{20,12},{24,16},{28,20},{1,25},{... | collective-permute-start | bytes 3317768 | tf_op jit(solution)/shard_map/ppermute | solution.py:52
  123.9 75.3 %collective-permute-start.2 = (bf16[864,640]{1,0:T(8,128)(2,1)}, bf16[864,640]{1,0:T(8,128)(2,1)}, u32[]{:S(2)}, u32[]{:S(2)}) collective-permute-start(bf16[864,640]{1,0:T(8,128)(2,1)} %collective-permute-done.1), channel_id=1, source_target_pairs={{0,1},{1,0},{2,3},{3,2},{4,5},{5,4},{6,7},{7,6},{8,9},{9,8},{10,11... | collective-permute-start | bytes 3317768 | tf_op jit(solution)/shard_map/ppermute | solution.py:57
  125.3 77.1 %collective-permute-start.5 = (bf16[864,640]{1,0:T(8,128)(2,1)S(1)}, bf16[864,640]{1,0:T(8,128)(2,1)}, u32[]{:S(2)}, u32[]{:S(2)}) collective-permute-start(bf16[864,640]{1,0:T(8,128)(2,1)S(1)} %collective-permute-done.3), channel_id=1, source_target_pairs={{0,4},{4,0},{8,12},{12,8},{16,20},{20,16},{24,28},{28,24},{1,5},{5... | collective-permute-start | bytes 3317768 | tf_op jit(solution)/shard_map/ppermute | solution.py:57
  130.0 74.1 %collective-permute-start.4 = (bf16[864,640]{1,0:T(8,128)(2,1)S(1)}, bf16[864,640]{1,0:T(8,128)(2,1)S(1)}, u32[]{:S(2)}, u32[]{:S(2)}) collective-permute-start(bf16[864,640]{1,0:T(8,128)(2,1)S(1)} %collective-permute-done.3), channel_id=1, source_target_pairs={{0,1},{1,0},{2,3},{3,2},{4,5},{5,4},{6,7},{7,6},{8,9},{9,8},{10,11... | collective-permute-start | bytes 3317768 | tf_op jit(solution)/shard_map/ppermute | solution.py:57
  194.8 23.3 %collective-permute-start.9 = (bf16[864,640]{1,0:T(8,128)(2,1)S(1)}, bf16[864,640]{1,0:T(8,128)(2,1)S(1)}, u32[]{:S(2)}, u32[]{:S(2)}) collective-permute-start(bf16[864,640]{1,0:T(8,128)(2,1)S(1)} %collective-permute-done.7), channel_id=1, source_target_pairs={{0,4},{4,0},{8,12},{12,8},{16,20},{20,16},{24,28},{28,24},{1,5},{5... | collective-permute-start | bytes 3317768 | tf_op jit(solution)/shard_map/ppermute | solution.py:57
  195.1 46.7 %collective-permute-start.13 = (bf16[864,640]{1,0:T(8,128)(2,1)S(1)}, bf16[864,640]{1,0:T(8,128)(2,1)S(1)}, u32[]{:S(2)}, u32[]{:S(2)}) collective-permute-start(bf16[864,640]{1,0:T(8,128)(2,1)S(1)} %collective-permute-done.11), channel_id=1, source_target_pairs={{0,4},{4,0},{8,12},{12,8},{16,20},{20,16},{24,28},{28,24},{1,5},{5... | collective-permute-start | bytes 3317768 | tf_op jit(solution)/shard_map/ppermute | solution.py:57
  199.2 48.2 %collective-permute-start.8 = (bf16[864,640]{1,0:T(8,128)(2,1)S(1)}, bf16[864,640]{1,0:T(8,128)(2,1)S(1)}, u32[]{:S(2)}, u32[]{:S(2)}) collective-permute-start(bf16[864,640]{1,0:T(8,128)(2,1)S(1)} %collective-permute-done.7), channel_id=1, source_target_pairs={{0,1},{1,0},{2,3},{3,2},{4,5},{5,4},{6,7},{7,6},{8,9},{9,8},{10,11... | collective-permute-start | bytes 3317768 | tf_op jit(solution)/shard_map/ppermute | solution.py:57
  202.4 44.6 %collective-permute-start.6 = (bf16[864,640]{1,0:T(8,128)(2,1)}, bf16[864,640]{1,0:T(8,128)(2,1)S(1)}, u32[]{:S(2)}, u32[]{:S(2)}) collective-permute-start(bf16[864,640]{1,0:T(8,128)(2,1)} %collective-permute-done.5), channel_id=1, source_target_pairs={{0,1},{1,0},{2,3},{3,2},{4,5},{5,4},{6,7},{7,6},{8,9},{9,8},{10,11... | collective-permute-start | bytes 3317768 | tf_op jit(solution)/shard_map/ppermute | solution.py:57
  204.1 44.1 %collective-permute-start.12 = (bf16[864,640]{1,0:T(8,128)(2,1)S(1)}, bf16[864,640]{1,0:T(8,128)(2,1)S(1)}, u32[]{:S(2)}, u32[]{:S(2)}) collective-permute-start(bf16[864,640]{1,0:T(8,128)(2,1)S(1)} %collective-permute-done.11), channel_id=1, source_target_pairs={{0,1},{1,0},{2,3},{3,2},{4,5},{5,4},{6,7},{7,6},{8,9},{9,8},{10,11... | collective-permute-start | bytes 3317768 | tf_op jit(solution)/shard_map/ppermute | solution.py:57
  218.1 29.7 %collective-permute-start.10 = (bf16[864,640]{1,0:T(8,128)(2,1)S(1)}, bf16[864,640]{1,0:T(8,128)(2,1)S(1)}, u32[]{:S(2)}, u32[]{:S(2)}) collective-permute-start(bf16[864,640]{1,0:T(8,128)(2,1)S(1)} %collective-permute-done.9), channel_id=1, source_target_pairs={{0,1},{1,0},{2,3},{3,2},{4,5},{5,4},{6,7},{7,6},{8,9},{9,8},{10,11... | collective-permute-start | bytes 3317768 | tf_op jit(solution)/shard_map/ppermute | solution.py:57
  270.8 37.7 %collective-permute-start.23 = (bf16[4,2,2,80,640]{4,3,0,1,2:T(8,128)(2,1)}, bf16[4,2,2,80,640]{4,3,0,1,2:T(8,128)(2,1)}, u32[]{:S(2)}, u32[]{:S(2)}) collective-permute-start(bf16[4,2,2,80,640]{4,3,0,1,2:T(8,128)(2,1)} %bitcast.205), channel_id=1, source_target_pairs={{0,8},{4,12},{8,0},{12,4},{16,24},{20,28},{24,16},{28,20},{1,9},{5... | collective-permute-start | bytes 4915208 | tf_op jit(solution)/shard_map/ppermute | solution.py:57
  273.2 46.5 %collective-permute-start.15 = (bf16[5,2,2,80,640]{4,3,0,1,2:T(8,128)(2,1)}, bf16[5,2,2,80,640]{4,3,0,1,2:T(8,128)(2,1)}, u32[]{:S(2)}, u32[]{:S(2)}) collective-permute-start(bf16[5,2,2,80,640]{4,3,0,1,2:T(8,128)(2,1)} %bitcast.204), channel_id=1, source_target_pairs={{0,2},{1,3},{2,0},{3,1},{4,6},{5,7},{6,4},{7,5},{8,10},{9,11},{10,... | collective-permute-start | bytes 6144008 | tf_op jit(solution)/shard_map/ppermute | solution.py:57
  312.1 38.8 %collective-permute-start.24 = (bf16[4,2,80,640]{3,2,0,1:T(8,128)(2,1)S(1)}, bf16[4,2,80,640]{3,2,0,1:T(8,128)(2,1)}, u32[]{:S(2)}, u32[]{:S(2)}) collective-permute-start(bf16[4,2,80,640]{3,2,0,1:T(8,128)(2,1)S(1)} %dynamic-slice_bitcast_fusion.6), channel_id=1, source_target_pairs={{0,16},{4,20},{8,24},{12,28},{16,0},{20,4},{24,8},{28,12},{1,17},{... | collective-permute-start | bytes 2457608 | tf_op jit(solution)/shard_map/ppermute | solution.py:57
  321.9 41.4 %collective-permute-start.16 = (bf16[5,2,80,640]{3,2,0,1:T(8,128)(2,1)S(1)}, bf16[5,2,80,640]{3,2,0,1:T(8,128)(2,1)S(1)}, u32[]{:S(2)}, u32[]{:S(2)}) collective-permute-start(bf16[5,2,80,640]{3,2,0,1:T(8,128)(2,1)S(1)} %dynamic-slice_bitcast_fusion.4), channel_id=1, source_target_pairs={{0,8},{4,12},{8,0},{12,4},{16,24},{20,28},{24,16},{28,20},{1,9},{5... | collective-permute-start | bytes 3072008 | tf_op jit(solution)/shard_map/ppermute | solution.py:57
  363.6 40.4 %collective-permute-start.17 = (bf16[5,80,640]{2,1,0:T(8,128)(2,1)S(1)}, bf16[5,80,640]{2,1,0:T(8,128)(2,1)S(1)}, u32[]{:S(2)}, u32[]{:S(2)}) collective-permute-start(bf16[5,80,640]{2,1,0:T(8,128)(2,1)S(1)} %dynamic-slice_bitcast_fusion.14), channel_id=1, source_target_pairs={{0,16},{4,20},{8,24},{12,28},{16,0},{20,4},{24,8},{28,12},{1,17},{... | collective-permute-start | bytes 1536008 | tf_op jit(solution)/shard_map/ppermute | solution.py:57
  372.3 55.1 %collective-permute-start.32 = (bf16[2,1,3,1,1,1,80,640]{7,6,5,4,3,2,1,0:T(8,128)(2,1)S(1)}, bf16[2,1,3,1,1,1,80,640]{7,6,5,4,3,2,1,0:T(8,128)(2,1)S(1)}, u32[]{:S(2)}, u32[]{:S(2)}) collective-permute-start(bf16[2,1,3,1,1,1,80,640]{7,6,5,4,3,2,1,0:T(8,128)(2,1)S(1)} %constant_dynamic-slice_fusion.3), channel_id=1, source_target_pairs={{0,16},{4,20},{8,24},{12,28},{16,0},{20,4},{24,8},{28,12},{1,17},{... | collective-permute-start | bytes 1843208 | tf_op jit(solution)/shard_map/ppermute | solution.py:57
  431.9 54.3 %collective-permute-start.33 = (bf16[2,1,3,1,2,1,80,640]{7,6,5,4,3,2,1,0:T(8,128)(2,1)S(1)}, bf16[2,1,3,1,2,1,80,640]{7,6,5,4,3,2,1,0:T(8,128)(2,1)S(1)}, u32[]{:S(2)}, u32[]{:S(2)}) collective-permute-start(bf16[2,1,3,1,2,1,80,640]{7,6,5,4,3,2,1,0:T(8,128)(2,1)S(1)} %constant_dynamic-slice_fusion.2), channel_id=1, source_target_pairs={{0,8},{4,12},{8,0},{12,4},{16,24},{20,28},{24,16},{28,20},{1,9},{5... | collective-permute-start | bytes 3686408 | tf_op jit(solution)/shard_map/ppermute | solution.py:57
  442.5 47.8 %collective-permute-start.20 = (bf16[1,1,3,1,2,2,80,640]{7,6,5,4,3,2,1,0:T(8,128)(2,1)S(1)}, bf16[1,1,3,1,2,2,80,640]{7,6,5,4,3,2,1,0:T(8,128)(2,1)S(1)}, u32[]{:S(2)}, u32[]{:S(2)}) collective-permute-start(bf16[1,1,3,1,2,2,80,640]{7,6,5,4,3,2,1,0:T(8,128)(2,1)S(1)} %constant_dynamic-slice_fusion.12), channel_id=1, source_target_pairs={{0,2},{1,3},{2,0},{3,1},{4,6},{5,7},{6,4},{7,5},{8,10},{9,11},{10,... | collective-permute-start | bytes 3686408 | tf_op jit(solution)/shard_map/ppermute | solution.py:57
  447.4 54.5 %collective-permute-start.28 = (bf16[2,1,3,2,1,1,80,640]{7,6,5,4,3,2,1,0:T(8,128)(2,1)S(1)}, bf16[2,1,3,2,1,1,80,640]{7,6,5,4,3,2,1,0:T(8,128)(2,1)S(1)}, u32[]{:S(2)}, u32[]{:S(2)}) collective-permute-start(bf16[2,1,3,2,1,1,80,640]{7,6,5,4,3,2,1,0:T(8,128)(2,1)S(1)} %constant_dynamic-slice_fusion.6), channel_id=1, source_target_pairs={{0,16},{4,20},{8,24},{12,28},{16,0},{20,4},{24,8},{28,12},{1,17},{... | collective-permute-start | bytes 3686408 | tf_op jit(solution)/shard_map/ppermute | solution.py:57
  489.2 53.6 %collective-permute-start.34 = (bf16[2,1,3,1,2,2,80,640]{7,6,5,4,3,2,1,0:T(8,128)(2,1)S(1)}, bf16[2,1,3,1,2,2,80,640]{7,6,5,4,3,2,1,0:T(8,128)(2,1)S(1)}, u32[]{:S(2)}, u32[]{:S(2)}) collective-permute-start(bf16[2,1,3,1,2,2,80,640]{7,6,5,4,3,2,1,0:T(8,128)(2,1)S(1)} %constant_dynamic-slice_fusion.1), channel_id=1, source_target_pairs={{0,2},{1,3},{2,0},{3,1},{4,6},{5,7},{6,4},{7,5},{8,10},{9,11},{10,... | collective-permute-start | bytes 7372808 | tf_op jit(solution)/shard_map/ppermute | solution.py:57
  490.7 61.2 %collective-permute-start.21 = (bf16[1,1,3,2,2,2,80,640]{7,6,5,4,3,2,1,0:T(8,128)(2,1)S(1)}, bf16[1,1,3,2,2,2,80,640]{7,6,5,4,3,2,1,0:T(8,128)(2,1)S(1)}, u32[]{:S(2)}, u32[]{:S(2)}) collective-permute-start(bf16[1,1,3,2,2,2,80,640]{7,6,5,4,3,2,1,0:T(8,128)(2,1)S(1)} %constant_dynamic-slice_fusion.11), channel_id=1, source_target_pairs={{0,4},{4,0},{8,12},{12,8},{16,20},{20,16},{24,28},{28,24},{1,5},{5... | collective-permute-start | bytes 7372808 | tf_op jit(solution)/shard_map/ppermute | solution.py:57
  505.0 52.8 %collective-permute-start.29 = (bf16[2,1,3,2,2,1,80,640]{7,6,5,4,3,2,1,0:T(8,128)(2,1)S(1)}, bf16[2,1,3,2,2,1,80,640]{7,6,5,4,3,2,1,0:T(8,128)(2,1)S(1)}, u32[]{:S(2)}, u32[]{:S(2)}) collective-permute-start(bf16[2,1,3,2,2,1,80,640]{7,6,5,4,3,2,1,0:T(8,128)(2,1)S(1)} %constant_dynamic-slice_fusion.5), channel_id=1, source_target_pairs={{0,8},{4,12},{8,0},{12,4},{16,24},{20,28},{24,16},{28,20},{1,9},{5... | collective-permute-start | bytes 7372808 | tf_op jit(solution)/shard_map/ppermute | solution.py:57
  760.3 33.2 %collective-permute-start.38 = (bf16[432,640]{1,0:T(8,128)(2,1)}, bf16[432,640]{1,0:T(8,128)(2,1)S(1)}, u32[]{:S(2)}, u32[]{:S(2)}) collective-permute-start(bf16[432,640]{1,0:T(8,128)(2,1)} %get-tuple-element.20), channel_id=1, source_target_pairs={{0,12},{4,16},{8,20},{12,24},{16,28},{20,0},{24,4},{28,8},{1,13},{... | collective-permute-start | bytes 1658888 | tf_op jit(solution)/shard_map/ppermute | solution.py:52
  771.6 83.1 %collective-permute-start.39 = (bf16[432,640]{1,0:T(8,128)(2,1)}, bf16[432,640]{1,0:T(8,128)(2,1)S(1)}, u32[]{:S(2)}, u32[]{:S(2)}) collective-permute-start(bf16[432,640]{1,0:T(8,128)(2,1)} %get-tuple-element.19), channel_id=1, source_target_pairs={{0,16},{4,20},{8,24},{12,28},{16,0},{20,4},{24,8},{28,12},{1,17},{... | collective-permute-start | bytes 1658888 | tf_op jit(solution)/shard_map/ppermute | solution.py:52
  772.6 82.9 %collective-permute-start.40 = (bf16[432,640]{1,0:T(8,128)(2,1)S(1)}, bf16[432,640]{1,0:T(8,128)(2,1)S(1)}, u32[]{:S(2)}, u32[]{:S(2)}) collective-permute-start(bf16[432,640]{1,0:T(8,128)(2,1)S(1)} %get-tuple-element.18), channel_id=1, source_target_pairs={{0,20},{4,24},{8,28},{12,0},{16,4},{20,8},{24,12},{28,16},{1,21},{... | collective-permute-start | bytes 1658888 | tf_op jit(solution)/shard_map/ppermute | solution.py:52
  773.1 83.3 %collective-permute-start.41 = (bf16[432,640]{1,0:T(8,128)(2,1)S(1)}, bf16[432,640]{1,0:T(8,128)(2,1)S(1)}, u32[]{:S(2)}, u32[]{:S(2)}) collective-permute-start(bf16[432,640]{1,0:T(8,128)(2,1)S(1)} %get-tuple-element.17), channel_id=1, source_target_pairs={{0,24},{4,28},{8,0},{12,4},{16,8},{20,12},{24,16},{28,20},{1,25},{... | collective-permute-start | bytes 1658888 | tf_op jit(solution)/shard_map/ppermute | solution.py:52
  781.9 75.3 %collective-permute-start.42 = (bf16[432,640]{1,0:T(8,128)(2,1)S(1)}, bf16[432,640]{1,0:T(8,128)(2,1)S(1)}, u32[]{:S(2)}, u32[]{:S(2)}) collective-permute-start(bf16[432,640]{1,0:T(8,128)(2,1)S(1)} %get-tuple-element.16), channel_id=1, source_target_pairs={{0,28},{4,0},{8,4},{12,8},{16,12},{20,16},{24,20},{28,24},{1,29},{... | collective-permute-start | bytes 1658888 | tf_op jit(solution)/shard_map/ppermute | solution.py:52
  (20 other events, 291.1 us)
Sparse Core Ops, SparseCore 0:
  10.2 63.7 all-gather.1

commit v2 on v0

v2 whole, which is shorter than its diff:
```python
import functools
import math

import jax
import jax.numpy as jnp
from jax import lax
from jax.experimental import pallas as pl
from jax.experimental.pallas import tpu as pltpu
from jax.sharding import PartitionSpec as P

F32 = jnp.float32
BF16 = jnp.bfloat16


def general_body(acts, out_grads, momentum, weight):
    token_acts = lax.all_gather(acts, "col", axis=0, tiled=True)
    token_grads = lax.all_gather(out_grads, "row", axis=0, tiled=True)
    gradient = lax.dot_general(token_acts, token_grads, (((0,), (0,)), ((), ())), preferred_element_type=F32)
    momentum_new = 0.95 * momentum + gradient
    blended = gradient + 0.95 * momentum_new
    rounded = blended.astype(BF16)
    col_panel = lax.all_gather(rounded, "row", axis=0, tiled=True)
    gram_tile = lax.psum_scatter(
        lax.dot_general(col_panel, rounded, (((1,), (1,)), ((), ())), preferred_element_type=F32).astype(BF16),
        "col",
        scatter_dimension=0,
        tiled=True,
    )
    gram_cols = lax.all_gather(gram_tile, "col", axis=0, tiled=True)
    gram_rows = lax.all_gather(gram_tile, "row", axis=1, tiled=True)
    gram_square = jnp.dot(gram_rows, gram_cols, preferred_element_type=F32)
    total_sum = lax.psum(jnp.sum(gram_square * gram_square), ("row", "col"))
    schatten = jnp.sqrt(total_sum + 1e-06)
    square_root = jnp.sqrt(schatten)
    fourth_root = jnp.sqrt(square_root)
    poly_tile = (-4.775 * gram_tile.astype(F32) / square_root + 2.0315 * gram_square / schatten).astype(BF16)
    poly_cols = lax.all_gather(poly_tile, "col", axis=0, tiled=True)
    product = lax.dot_general(poly_cols, col_panel, (((0,), (0,)), ((), ())), preferred_element_type=F32)
    orthogonal = (3.4445 * rounded.astype(F32) + product) / fourth_root
    factor = math.sqrt(col_panel.shape[0])
    update = (factor * orthogonal).astype(BF16)
    weight_new = 0.998 * weight - 0.02 * factor * orthogonal
    return (momentum_new, update, weight_new)


BLOCKS = 8
PIECES = 5
MOVES = {"x": ("row", 1), "zl": ("row", 2), "zh": ("row", 4), "y": ("col", 2), "k": ("col", 1)}
REDUCE = (("y", "zl"), ("zl", "y"), ("zl", "y"))
GATHER = (("zl", "y", "x"), ("zl", "x", "y"), ("x", "y", "zl"))


def row_shift(value, step):
    return lax.ppermute(value, "row", [(i, (i + step) % BLOCKS) for i in range(BLOCKS)])


def swap(value, name):
    axis, bit = MOVES[name]
    size = 8 if axis == "row" else 4
    return lax.ppermute(value, axis, [(i, i ^ bit) for i in range(size)])


def take(value, dim, index):
    return lax.dynamic_index_in_dim(value, index, dim, keepdims=False)


def reduce_part(tiles, order, place):
    left = ["y", "zl"]
    for name in order:
        dim = 1 + left.index(name)
        left.remove(name)
        received = swap(take(tiles, dim, 1 - place[name]), name)
        tiles = (take(tiles, dim, place[name]).astype(F32) + received.astype(F32)).astype(BF16)
    return (tiles.astype(F32) + swap(tiles, "zh").astype(F32)).astype(BF16)


def gather_part(mine, order):
    mine = jnp.stack([mine, swap(mine, order[0])])
    held = [mine]
    for name in order[1:]:
        held = held + [swap(value, name) for value in held]
    return held + [swap(jnp.stack(held), "k")]


def entry_kernel(acts_ref, momentum_ref, *refs):
    grads_refs, (new_ref, turned_ref) = refs[:-2], refs[-2:]
    grads = jnp.concatenate([ref[...] for ref in grads_refs])
    gradient = jnp.dot(acts_ref[...], grads, preferred_element_type=F32)
    momentum_new = 0.95 * momentum_ref[...] + gradient
    new_ref[...] = momentum_new
    turned_ref[...] = (gradient + 0.95 * momentum_new).T.astype(BF16)


def entry(acts_t, momentum, grads):
    rows, cols = momentum.shape
    tokens = acts_t.shape[1]
    width = cols // 9
    across = pl.BlockSpec((rows, width), lambda i: (0, i))
    return pl.pallas_call(
        entry_kernel,
        out_shape=(jax.ShapeDtypeStruct((rows, cols), F32), jax.ShapeDtypeStruct((cols, rows), BF16)),
        grid=(9,),
        in_specs=[pl.BlockSpec((rows, tokens), lambda i: (0, 0)), across]
        + [pl.BlockSpec((value.shape[0], width), lambda i: (0, i)) for value in grads],
        out_specs=(across, pl.BlockSpec((width, rows), lambda i: (i, 0))),
        compiler_params=pltpu.CompilerParams(vmem_limit_bytes=40 * 2**20),
        cost_estimate=pl.CostEstimate(
            flops=2 * rows * cols * tokens, bytes_accessed=rows * cols * 10 + tokens * cols * 2, transcendentals=0
        ),
    )(acts_t, momentum, *grads)


def finish_kernel(home_ref, weight_ref, update_ref, new_ref):
    update = home_ref[...].astype(F32).T
    update_ref[...] = update.astype(BF16)
    new_ref[...] = 0.998 * weight_ref[...] - 0.02 * update


def finish(home, weight):
    rows, cols = weight.shape
    width = cols // 9
    across = pl.BlockSpec((rows, width), lambda i: (0, i))
    return pl.pallas_call(
        finish_kernel,
        out_shape=(jax.ShapeDtypeStruct((rows, cols), BF16), jax.ShapeDtypeStruct((rows, cols), F32)),
        grid=(9,),
        in_specs=[pl.BlockSpec((width, rows), lambda i: (i, 0)), across],
        out_specs=(across, across),
        compiler_params=pltpu.CompilerParams(vmem_limit_bytes=40 * 2**20),
        cost_estimate=pl.CostEstimate(flops=4 * rows * cols, bytes_accessed=rows * cols * 12, transcendentals=0),
    )(home, weight)


def apply_near(source, tiles, total, blocks, first, last):
    rows = total.shape[2]
    depth = (last - first) * rows

    def near(b, _):
        start = pl.multiple_of((b + first) * rows, 128)
        own = pl.multiple_of(b * rows, 128)
        total[b] += jnp.dot(
            source[:, pl.ds(start, depth)],
            tiles[b, first:last].reshape(depth, rows),
            preferred_element_type=F32,
        )
        for d in range(max(first, 1), last):
            total[lax.rem(b + d, BLOCKS)] += lax.dot_general(
                source[:, pl.ds(own, rows)],
                tiles[b, d].reshape(rows, rows),
                (((1,), (1,)), ((), ())),
                preferred_element_type=F32,
            )
        return 0

    lax.fori_loop(*blocks, near, 0)


def apply_far(source, fours, total):
    rows = total.shape[2]

    def far(b, _):
        start = pl.multiple_of(b * rows, 128)
        other = pl.multiple_of((b + 4) * rows, 128)
        tile = fours[b].reshape(rows, rows)
        total[b] += jnp.dot(source[:, pl.ds(other, rows)], tile, preferred_element_type=F32)
        total[b + 4] += lax.dot_general(
            source[:, pl.ds(start, rows)], tile, (((1,), (1,)), ((), ())), preferred_element_type=F32
        )
        return 0

    lax.fori_loop(0, BLOCKS // 2, far, 0)


def load_tiles(place, part, pieces, tiles, fours, sem):
    for index in range(8):
        for inner in range(2):
            flips = (inner, index & 1, (index >> 1) & 1, index >> 2)
            there = {
                name: 1 - place[name] if flip else place[name] for name, flip in zip(GATHER[part] + ("k",), flips)
            }
            b = 2 * there["x"] + there["k"]
            e = 2 * there["y"] + there["zl"]
            piece = pieces[index].at[inner] if index < 4 else pieces[4].at[index - 4, inner]
            if part < 2:
                pltpu.make_async_copy(piece, tiles.at[b + 4 * part, pl.ds(0, 3), e], sem.at[part]).start()
            else:
                pltpu.make_async_copy(piece.at[0], tiles.at[b, 3, e], sem.at[2]).start()
                pltpu.make_async_copy(piece.at[1], tiles.at[b + 4, 3, e], sem.at[2]).start()
                pltpu.make_async_copy(piece.at[2], fours.at[b, e], sem.at[3]).start()
    if part < 2:
        block = tiles.at[pl.ds(4 * part, 4), pl.ds(0, 3)]
        return [pltpu.make_async_copy(block, block, sem.at[part])]
    block = tiles.at[:, 3]
    return [pltpu.make_async_copy(block, block, sem.at[2]), pltpu.make_async_copy(fours, fours, sem.at[3])]


def load_columns(place, panel_ref, source, sem):
    width = source.shape[0]
    rows = panel_ref.shape[3]
    group = 2 * place["x"] + place["k"]
    copies = []
    for b in range(BLOCKS + 3):
        j = lax.rem(b - group + 2 * BLOCKS, BLOCKS)
        block = panel_ref.at[j, 0, pl.ds(pl.multiple_of(place["x"] * width, 16), width)]
        copies.append(pltpu.make_async_copy(block, source.at[:, pl.ds(b * rows, rows)], sem.at[b]))
        copies[-1].start()
    return copies


def places_of(place_ref):
    return {name: place_ref[i] for i, name in enumerate(("x", "k", "y", "zh", "zl"))}


def product_kernel(place_ref, panel_ref, *refs):
    parts, (y_ref, z_ref, dot_ref), scratch = refs[: 3 * PIECES], refs[3 * PIECES : 3 * PIECES + 3], refs[3 * PIECES + 3 :]
    source, tiles, fours, total, tile_sem, x_sem, out_sem = scratch
    rows = total.shape[2]
    place = places_of(place_ref)
    columns = load_columns(place, panel_ref, source, x_sem)
    arrivals = [
        load_tiles(place, part, parts[PIECES * part : PIECES * part + PIECES], tiles, fours, tile_sem)
        for part in range(3)
    ]
    total[...] = jnp.zeros_like(total)
    for wait in columns + arrivals[0]:
        wait.wait()
    apply_near(source, tiles, total, (0, 4), 0, 3)
    for wait in arrivals[1]:
        wait.wait()
    apply_near(source, tiles, total, (4, 8), 0, 3)
    for wait in arrivals[2]:
        wait.wait()
    apply_near(source, tiles, total, (0, BLOCKS), 3, 4)
    apply_far(source, fours, total)
    out = pltpu.make_async_copy(total, y_ref, out_sem)
    out.start()
    for b in range(BLOCKS + 3):
        source[:, b * rows : (b + 1) * rows] = total[b % BLOCKS].astype(BF16)
    out.wait()
    total[...] = jnp.zeros_like(total)
    apply_near(source, tiles, total, (0, BLOCKS), 0, 4)
    apply_far(source, fours, total)
    out = pltpu.make_async_copy(total, z_ref, out_sem)
    out.start()
    lanes = jnp.zeros((1, rows), F32)
    for b in range(BLOCKS):
        lanes += jnp.sum(source[:, b * rows : (b + 1) * rows].astype(F32) * total[b], axis=0, keepdims=True)
    dot_ref[...] = jnp.broadcast_to(lanes, dot_ref.shape)
    out.wait()


def products(place, panel, parts):
    blocks, _, quarter, rows = panel.shape
    width = quarter // 2
    e = rows // 4
    anywhere = pl.BlockSpec(memory_space=pl.ANY)
    whole = jax.ShapeDtypeStruct((blocks, width, rows), F32)
    return pl.pallas_call(
        product_kernel,
        out_shape=(whole, whole, jax.ShapeDtypeStruct((8, rows), F32)),
        in_specs=[pl.BlockSpec(memory_space=pltpu.SMEM)] + [anywhere] * (1 + len(parts)),
        out_specs=(anywhere, anywhere, pl.BlockSpec(memory_space=pltpu.VMEM)),
        scratch_shapes=[
            pltpu.VMEM((width, (blocks + 3) * rows), BF16),
            pltpu.VMEM((blocks, 4, 4, e, rows), BF16),
            pltpu.VMEM((blocks // 2, 4, e, rows), BF16),
            pltpu.VMEM((blocks, width, rows), F32),
            pltpu.SemaphoreType.DMA((4,)),
            pltpu.SemaphoreType.DMA((blocks + 3,)),
            pltpu.SemaphoreType.DMA,
        ],
        compiler_params=pltpu.CompilerParams(vmem_limit_bytes=60 * 2**20),
        cost_estimate=pl.CostEstimate(
            flops=2 * 2 * 64 * width * rows * rows, bytes_accessed=2 * 36 * rows * rows, transcendentals=0
        ),
    )(place, panel, *parts)


def fast_body(acts, out_grads, momentum, weight):
    row, col = lax.axis_index("row"), lax.axis_index("col")
    z, x, y, core = row // 2, row % 2, col // 2, col % 2
    place = {"x": x, "k": core, "y": y, "zh": z // 2, "zl": z % 2}
    rows, cols = momentum.shape
    quarter = cols // 4
    half = quarter // 2
    e = rows // 4
    group = 2 * x + core

    along = {0: out_grads, 2: swap(out_grads, "zl"), 4: swap(out_grads, "zh")}
    along[6] = swap(along[4], "zl")
    along |= {bits + 1: swap(value, "x") for bits, value in along.items()}
    token_acts = jnp.zeros((4, *acts.shape), BF16)
    for bit in range(4):
        value = lax.ppermute(acts, "col", [(i, i ^ bit) for i in range(4)]) if bit else acts
        token_acts = lax.dynamic_update_slice(token_acts, value[None], (col ^ bit, 0, 0))
    token_acts = token_acts.reshape(BLOCKS, -1, rows)
    acts_t = jnp.concatenate([take(token_acts, 0, row ^ bits) for bits in along]).T
    momentum_new, turned = entry(acts_t, momentum, list(along.values()))
    pieces = turned.reshape(4, quarter, rows)

    panel = jnp.zeros((BLOCKS, 2, quarter, rows), BF16)
    for step in range(4):
        piece = take(pieces, 0, (z + step) % 4)
        if step:
            piece = row_shift(piece, 2 * step)
        source = 2 * ((z - step + 4) % 4)
        beside = swap(piece, "x")
        for block, value in ((source + x, piece), (source + 1 - x, beside)):
            j = (block - group + 8) % 8
            panel = lax.dynamic_update_slice(panel, value[None, None], (j, 0, 0, 0))
            panel = lax.dynamic_update_slice(panel, swap(value, "k")[None, None], (j, 1, 0, 0))
    deep = panel.reshape(BLOCKS, 2 * quarter, rows)

    def tile(deep, i, j):
        return lax.dot_general(deep[i], deep[j], (((0,), (0,)), ((), ())), preferred_element_type=F32).astype(BF16)

    wanted = (((0, 0), (1, 0), (2, 0)), ((4, 4), (5, 4), (6, 4)), ((3, 0), (7, 4), (4, 0)))
    parts = []
    for which in range(3):
        tiles = jnp.stack([tile(deep, i, j) for i, j in wanted[which]]).reshape(3, 2, 2, e, rows)
        deep, tiles = lax.optimization_barrier((deep, tiles))
        parts += gather_part(reduce_part(tiles, REDUCE[which], place), GATHER[which])

    places = jnp.stack([place[name] for name in ("x", "k", "y", "zh", "zl")]).astype(jnp.int32)
    one, two, lanes = products(places, panel, parts)
    total_sum = jnp.broadcast_to(jnp.sum(lanes[0]), (8, 128))
    total_sum = total_sum + sum(row_shift(total_sum, step) for step in range(1, 8))
    total_sum = total_sum + sum(
        lax.ppermute(total_sum, "col", [(i, i ^ bit) for i in range(4)]) for bit in range(1, 4)
    )
    schatten = jnp.sqrt(total_sum[0, 0] + 1e-06)
    square_root = jnp.sqrt(schatten)
    scale = math.sqrt(rows * BLOCKS) / jnp.sqrt(square_root)

    home = jnp.zeros((BLOCKS, half, rows), BF16)
    own = lax.dynamic_slice(panel, (0, 0, x * half, 0), (BLOCKS, 1, half, rows))[:, 0]
    for step in range(BLOCKS):
        there = (row + step) % 8
        value = (
            3.4445 * take(own, 0, (there - group + 8) % 8).astype(F32)
            - (4.775 / square_root) * take(one, 0, there)
            + (2.0315 / schatten) * take(two, 0, there)
        )
        value = (scale * value).astype(BF16)
        if step:
            value = row_shift(value, step)
        home = lax.dynamic_update_slice(home, value[None], ((row - step + 8) % 8, 0, 0))
    update, weight_new = finish(home.reshape(cols, rows), weight)
    return (momentum_new, update, weight_new)


def solution(mesh):
    spec = P("row", "col")
    in_specs = (P("col", "row"), spec, spec, spec)
    fast = mesh.shape["row"] == 8 and mesh.shape["col"] == 4
    body = fast_body if fast else general_body
    return jax.shard_map(body, mesh=mesh, in_specs=in_specs, out_specs=(spec, spec, spec), check_vma=False)
```

time: 1250 us -> 757 us (0.61)
  waiting for transfers between devices: 1070 us -> 488 us
  Pallas kernels: 0 us -> 108 us
  matrix products: 102 us -> 18.5 us
  starting transfers between devices: 0.23 us -> 62.9 us
  blocking collectives: 49.3 us -> 0 us
  local copies, waits for them, and re-layouts: 0.01 us -> 37.5 us
  other arithmetic: 3.82 us -> 31.7 us
    all_gather x5 -> x0, waiting for transfers between devices: 1010 us -> none  [the longest x1 672 us: body(): col_panel = lax.all_gather(rounded, 'row', axis=0, tiled=True)]
    ppermute x0 -> x66, waiting for transfers between devices: none -> 488 us  [the longest x43 331 us: swap(): return lax.ppermute(value, axis, [(i, i ^ bit) for i in range(size)])]
    pallas_call x0 -> x3, Pallas kernels: none -> 108 us  [the longest x1 89.8 us: products(): pl.pallas_call(product_kernel, out_shape=(whole, whole, jax.ShapeDtypeStr...]
    dot_general x4 -> x9, matrix products: 102 us -> 18.5 us  [tile(): lax.dot_general(deep[i], deep[j], (((0,), (0,)), ((), ())), preferred_ele...]
    ppermute x0 -> x66, starting transfers between devices: none -> 62.9 us  [the longest x43 41.2 us: swap(): return lax.ppermute(value, axis, [(i, i ^ bit) for i in range(size)])]
    reduce_scatter x1 -> x0, waiting for transfers between devices: 61.2 us -> none  [body(): lax.psum_scatter(lax.dot_general(slab_rows, rounded, (((1,), (1,)), ((),...]
    psum x1 -> x0, blocking collectives: 40.7 us -> none  [body(): total_sum = lax.psum(jnp.sum(gram_square * gram_square), ('row', 'col'))]
    convert_element_type x1 -> x11, other arithmetic: 3.82 us -> 17 us  [the longest x2 10.7 us: fast_body(): value = (scale * value).astype(BF16)]
  transfers between devices with their start and end apart: 6 -> 66, of which waited for: 6 -> 33; matrix products, arithmetic and copies ran while one was open for 0% -> 7% of each run, Pallas kernels for 0% -> 0%
where the time goes in v2:
time: 757 us; the launch traced here: 749 us
  waiting for transfers between devices  488 us (64%)
  Pallas kernels  108 us (14%)
  starting transfers between devices  62.9 us (8%)
  local copies, waits for them, and re-layouts  37.5 us (5%)
  other arithmetic  31.7 us (4%)
  matrix products  18.5 us (2%)
    ppermute x43, waiting for transfers between devices, swap(): return lax.ppermute(value, axis, [(i, i ^ bit) for i in range(size)])  331 us
    ppermute x17, waiting for transfers between devices, row_shift(): lax.ppermute(value, 'row', [(i, (i + step) % BLOCKS) for i in range(BLOCK...  155 us
    pallas_call x1, Pallas kernels, products(): pl.pallas_call(product_kernel, out_shape=(whole, whole, jax.ShapeDtypeStr...  89.8 us
    ppermute x43, starting transfers between devices, swap(): return lax.ppermute(value, axis, [(i, i ^ bit) for i in range(size)])  41.2 us
    dot_general x9, matrix products, tile(): lax.dot_general(deep[i], deep[j], (((0,), (0,)), ((), ())), preferred_ele...  18.5 us
  transfers between devices with their start and end apart: 66, of which 33 were waited for; matrix products, arithmetic and copies ran while one was open for 7% of the time, Pallas kernels for 0%

profile of v2, /device:TPU:27, one launch (start us, length us, event | category | flops | bytes accessed | tf_op | source)
XLA Modules:
  0.0 748.9 jit_solution(10389189793969048162)
XLA Ops:
  3.5 19.8 %collective-permute-done.4.refs_2_ = bf16[64,3456]{1,0:T(8,128)(2,1)S(1)} collective-permute-done((bf16[64,3456]{1,0:T(8,128)(2,1)}, bf16[64,3456]{1,0:T(8,128)(2,1)S(1)}, u32[]{:S(2)}, u32[]{:S(2)}) %collective-permute-start.4) | collective-permute-done | bytes 442400 | tf_op jit(solution)/shard_map/ppermute | solution.py:60
  26.2 8.3 %collective-permute-done.5.refs_3_ = bf16[64,3456]{1,0:T(8,128)(2,1)S(1)} collective-permute-done((bf16[64,3456]{1,0:T(8,128)(2,1)S(1)}, bf16[64,3456]{1,0:T(8,128)(2,1)S(1)}, u32[]{:S(2)}, u32[]{:S(2)}) %collective-permute-start.5) | collective-permute-done | bytes 442400 | tf_op jit(solution)/shard_map/ppermute | solution.py:60
  45.3 9.6 %collective-permute-done.7.refs_5_ = bf16[64,3456]{1,0:T(8,128)(2,1)} collective-permute-done((bf16[64,3456]{1,0:T(8,128)(2,1)S(1)}, bf16[64,3456]{1,0:T(8,128)(2,1)}, u32[]{:S(2)}, u32[]{:S(2)}) %collective-permute-start.7) | collective-permute-done | bytes 442400 | tf_op jit(solution)/shard_map/ppermute | solution.py:60
  54.8 9.5 %collective-permute-done.9.refs_7_ = bf16[64,3456]{1,0:T(8,128)(2,1)} collective-permute-done((bf16[64,3456]{1,0:T(8,128)(2,1)S(1)}, bf16[64,3456]{1,0:T(8,128)(2,1)}, u32[]{:S(2)}, u32[]{:S(2)}) %collective-permute-start.9) | collective-permute-done | bytes 442400 | tf_op jit(solution)/shard_map/ppermute | solution.py:60
  64.3 11.2 %shard_map.67 = (f32[640,3456]{1,0:T(8,128)}, bf16[3456,640]{1,0:T(8,128)(2,1)S(1)}) custom-call(bf16[640,512]{1,0:T(8,128)(2,1)S(1)} %bitcast.318, f32[640,3456]{1,0:T(8,128)} %momentum_ref.1, bf16[64,3456]{1,0:T(8,128)(2,1)S(1)} %copy-done.2, bf16[64,3456]{1,0:T(8,128)(2,1)S(1)} %collective-permute-done.3.refs_1_, ...), custom_call_target="tpu_custom_call" | custom-call | flops 2264924160 | bytes 25657344 | tf_op jit(solution)/shard_map/pallas_call | solution.py:99
  83.5 19.9 %collective-permute-done.11 = bf16[864,640]{1,0:T(8,128)(2,1)} collective-permute-done((bf16[864,640]{1,0:T(8,128)(2,1)}, bf16[864,640]{1,0:T(8,128)(2,1)}, u32[]{:S(2)}, u32[]{:S(2)}) %collective-permute-start.11) | collective-permute-done | bytes 1105952 | tf_op jit(solution)/shard_map/ppermute | solution.py:60
  111.3 63.4 %collective-permute-done.17 = bf16[864,640]{1,0:T(8,128)(2,1)S(1)} collective-permute-done((bf16[864,640]{1,0:T(8,128)(2,1)}, bf16[864,640]{1,0:T(8,128)(2,1)S(1)}, u32[]{:S(2)}, u32[]{:S(2)}) %collective-permute-start.17) | collective-permute-done | bytes 1105952 | tf_op jit(solution)/shard_map/ppermute | solution.py:54
  184.9 12.8 %collective-permute-done.19 = bf16[864,640]{1,0:T(8,128)(2,1)S(1)} collective-permute-done((bf16[864,640]{1,0:T(8,128)(2,1)S(1)}, bf16[864,640]{1,0:T(8,128)(2,1)S(1)}, u32[]{:S(2)}, u32[]{:S(2)}) %collective-permute-start.19) | collective-permute-done | bytes 1105952 | tf_op jit(solution)/shard_map/ppermute | solution.py:60
  197.7 7.3 collective-permute-start.20
  205.0 16.4 %collective-permute-done.23 = bf16[864,640]{1,0:T(8,128)(2,1)S(1)} collective-permute-done((bf16[864,640]{1,0:T(8,128)(2,1)S(1)}, bf16[864,640]{1,0:T(8,128)(2,1)S(1)}, u32[]{:S(2)}, u32[]{:S(2)}) %collective-permute-start.23) | collective-permute-done | bytes 1105952 | tf_op jit(solution)/shard_map/ppermute | solution.py:60
  221.4 3.9 collective-permute-start.24
  255.1 24.0 %collective-permute-done.41 = bf16[3,2,160,640]{3,2,0,1:T(8,128)(2,1)} collective-permute-done((bf16[3,2,160,640]{3,2,0,1:T(8,128)(2,1)}, bf16[3,2,160,640]{3,2,0,1:T(8,128)(2,1)}, u32[]{:S(2)}, u32[]{:S(2)}) %collective-permute-start.41) | collective-permute-done | bytes 1228832 | tf_op jit(solution)/shard_map/ppermute | solution.py:60
  283.8 21.7 %collective-permute-done.33 = bf16[3,2,160,640]{3,2,0,1:T(8,128)(2,1)} collective-permute-done((bf16[3,2,160,640]{3,2,0,1:T(8,128)(2,1)}, bf16[3,2,160,640]{3,2,0,1:T(8,128)(2,1)}, u32[]{:S(2)}, u32[]{:S(2)}) %collective-permute-start.33) | collective-permute-done | bytes 1228832 | tf_op jit(solution)/shard_map/ppermute | solution.py:60
  310.9 11.3 %collective-permute-done.34 = bf16[3,160,640]{2,1,0:T(8,128)(2,1)S(1)} collective-permute-done((bf16[3,160,640]{2,1,0:T(8,128)(2,1)S(1)}, bf16[3,160,640]{2,1,0:T(8,128)(2,1)S(1)}, u32[]{:S(2)}, u32[]{:S(2)}) %collective-permute-start.34) | collective-permute-done | bytes 614432 | tf_op jit(solution)/shard_map/ppermute | solution.py:60
  322.4 17.6 %collective-permute-done.43 = bf16[3,160,640]{2,1,0:T(8,128)(2,1)S(1)} collective-permute-done((bf16[3,160,640]{2,1,0:T(8,128)(2,1)S(1)}, bf16[3,160,640]{2,1,0:T(8,128)(2,1)S(1)}, u32[]{:S(2)}, u32[]{:S(2)}) %collective-permute-start.43) | collective-permute-done | bytes 614432 | tf_op jit(solution)/shard_map/ppermute | solution.py:60
  341.9 36.3 %collective-permute-done.35 = bf16[3,160,640]{2,1,0:T(8,128)(2,1)S(1)} collective-permute-done((bf16[3,160,640]{2,1,0:T(8,128)(2,1)S(1)}, bf16[3,160,640]{2,1,0:T(8,128)(2,1)S(1)}, u32[]{:S(2)}, u32[]{:S(2)}) %collective-permute-start.35) | collective-permute-done | bytes 614432 | tf_op jit(solution)/shard_map/ppermute | solution.py:60
  379.1 12.4 %collective-permute-done.27 = bf16[3,160,640]{2,1,0:T(8,128)(2,1)S(1)} collective-permute-done((bf16[3,160,640]{2,1,0:T(8,128)(2,1)S(1)}, bf16[3,160,640]{2,1,0:T(8,128)(2,1)S(1)}, u32[]{:S(2)}, u32[]{:S(2)}) %collective-permute-start.27) | collective-permute-done | bytes 614432 | tf_op jit(solution)/shard_map/ppermute | solution.py:60
  391.7 12.9 %collective-permute-done.36 = bf16[3,160,640]{2,1,0:T(8,128)(2,1)S(1)} collective-permute-done((bf16[3,160,640]{2,1,0:T(8,128)(2,1)S(1)}, bf16[3,160,640]{2,1,0:T(8,128)(2,1)S(1)}, u32[]{:S(2)}, u32[]{:S(2)}) %collective-permute-start.36) | collective-permute-done | bytes 614432 | tf_op jit(solution)/shard_map/ppermute | solution.py:60
  406.1 11.6 %collective-permute-done.28 = bf16[3,160,640]{2,1,0:T(8,128)(2,1)S(1)} collective-permute-done((bf16[3,160,640]{2,1,0:T(8,128)(2,1)S(1)}, bf16[3,160,640]{2,1,0:T(8,128)(2,1)S(1)}, u32[]{:S(2)}, u32[]{:S(2)}) %collective-permute-start.28) | collective-permute-done | bytes 614432 | tf_op jit(solution)/shard_map/ppermute | solution.py:60
  419.6 13.3 %collective-permute-done.37.refs_6_ = bf16[2,3,160,640]{3,2,1,0:T(8,128)(2,1)S(1)} collective-permute-done((bf16[2,3,160,640]{3,2,1,0:T(8,128)(2,1)S(1)}, bf16[2,3,160,640]{3,2,1,0:T(8,128)(2,1)S(1)}, u32[]{:S(2)}, u32[]{:S(2)}) %collective-permute-start.37) | collective-permute-done | bytes 1228832 | tf_op jit(solution)/shard_map/ppermute | solution.py:60
  433.1 11.0 %collective-permute-done.46.refs_12_ = bf16[2,3,160,640]{3,2,1,0:T(8,128)(2,1)S(1)} collective-permute-done((bf16[2,3,160,640]{3,2,1,0:T(8,128)(2,1)S(1)}, bf16[2,3,160,640]{3,2,1,0:T(8,128)(2,1)S(1)}, u32[]{:S(2)}, u32[]{:S(2)}) %collective-permute-start.46) | collective-permute-done | bytes 1228832 | tf_op jit(solution)/shard_map/ppermute | solution.py:60
  447.3 23.1 %collective-permute-done.47.refs_13_ = bf16[2,3,160,640]{3,2,1,0:T(8,128)(2,1)S(1)} collective-permute-done((bf16[2,3,160,640]{3,2,1,0:T(8,128)(2,1)S(1)}, bf16[2,3,160,640]{3,2,1,0:T(8,128)(2,1)S(1)}, u32[]{:S(2)}, u32[]{:S(2)}) %collective-permute-start.47) | collective-permute-done | bytes 1228832 | tf_op jit(solution)/shard_map/ppermute | solution.py:60
  474.1 24.6 %collective-permute-done.39.refs_8_ = bf16[2,3,160,640]{3,2,1,0:T(8,128)(2,1)S(1)} collective-permute-done((bf16[2,3,160,640]{3,2,1,0:T(8,128)(2,1)S(1)}, bf16[2,3,160,640]{3,2,1,0:T(8,128)(2,1)S(1)}, u32[]{:S(2)}, u32[]{:S(2)}) %collective-permute-start.39) | collective-permute-done | bytes 1228832 | tf_op jit(solution)/shard_map/ppermute | solution.py:60
  507.0 4.4 collective-permute-done.40.refs_9_
  511.4 7.0 collective-permute-done.32.refs_4_
  518.4 89.8 %shard_map.68 = (f32[8,432,640]{2,1,0:T(8,128)}, f32[8,432,640]{2,1,0:T(8,128)}, f32[8,640]{1,0:T(8,128)}) custom-call(s32[5]{0:T(128)} %stack.131.place_ref, bf16[8,2,864,640]{3,2,1,0:T(8,128)(2,1)} %copy-done.3, bf16[2,3,160,640]{3,2,1,0:T(8,128)(2,1)} %copy-done.11, bf16[2,3,160,640]{3,2,1,0:T(8,128)(2,1)} %copy-done.15, ...), custom_call_target="tpu_custom_call" | custom-call | flops 45298483200 | bytes 29491200 | tf_op jit(solution)/shard_map/pallas_call | solution.py:258
  633.1 7.8 %fusion.66 = (bf16[432,640]{1,0:T(8,128)(2,1)S(1)}, bf16[432,640]{1,0:T(8,128)(2,1)S(1)}, bf16[432,640]{1,0:T(8,128)(2,1)S(1)}, bf16[432,640]{1,0:T(8,128)(2,1)S...) fusion(f32[8,432,640]{2,1,0:T(8,128)} %get-tuple-element.24, s32[]{:T(128)S(6)} %select_n.421, ...), kind=kLoop, calls=%fused_computation.72 | loop fusion | flops 13271040 | bytes 19906624 | tf_op jit(solution)/shard_map/convert_element_type | solution.py:344
  649.8 7.2 collective-permute-done.60
  658.1 10.8 %collective-permute-done.61 = bf16[432,640]{1,0:T(8,128)(2,1)S(1)} collective-permute-done((bf16[432,640]{1,0:T(8,128)(2,1)S(1)}, bf16[432,640]{1,0:T(8,128)(2,1)S(1)}, u32[]{:S(2)}, u32[]{:S(2)}) %collective-permute-start.61) | collective-permute-done | bytes 552992 | tf_op jit(solution)/shard_map/ppermute | solution.py:54
  669.0 60.0 %collective-permute-done.62 = bf16[432,640]{1,0:T(8,128)(2,1)S(1)} collective-permute-done((bf16[432,640]{1,0:T(8,128)(2,1)S(1)}, bf16[432,640]{1,0:T(8,128)(2,1)S(1)}, u32[]{:S(2)}, u32[]{:S(2)}) %collective-permute-start.62) | collective-permute-done | bytes 552992 | tf_op jit(solution)/shard_map/ppermute | solution.py:54
  729.1 8.5 %collective-permute-done.63 = bf16[432,640]{1,0:T(8,128)(2,1)S(1)} collective-permute-done((bf16[432,640]{1,0:T(8,128)(2,1)S(1)}, bf16[432,640]{1,0:T(8,128)(2,1)S(1)}, u32[]{:S(2)}, u32[]{:S(2)}) %collective-permute-start.63) | collective-permute-done | bytes 552992 | tf_op jit(solution)/shard_map/ppermute | solution.py:54
  741.4 7.1 shard_map.69
  (230 shorter events, 141.9 us)
Async XLA Ops:
  2.9 31.8 %collective-permute-start.2 = (bf16[128,640]{1,0:T(8,128)(2,1)}, bf16[128,640]{1,0:T(8,128)(2,1)S(1)}, u32[]{:S(2)}, u32[]{:S(2)}) collective-permute-start(bf16[128,640]{1,0:T(8,128)(2,1)} %param.4), channel_id=1, source_target_pairs={{0,3},{1,2},{2,1},{3,0},{4,7},{5,6},{6,5},{7,4},{8,11},{9,10},{10,... | collective-permute-start | bytes 491528 | tf_op jit(solution)/shard_map/ppermute | solution.py:294
  34.5 29.8 %collective-permute-start.9 = (bf16[64,3456]{1,0:T(8,128)(2,1)S(1)}, bf16[64,3456]{1,0:T(8,128)(2,1)}, u32[]{:S(2)}, u32[]{:S(2)}) collective-permute-start(bf16[64,3456]{1,0:T(8,128)(2,1)S(1)} %collective-permute-done.5.refs_3_), channel_id=1, source_target_pairs={{0,4},{4,0},{8,12},{12,8},{16,20},{20,16},{24,28},{28,24},{1,5},{5... | collective-permute-start | bytes 1327112 | tf_op jit(solution)/shard_map/ppermute | solution.py:60
  79.2 30.2 %collective-permute-start.10 = (bf16[864,640]{1,0:T(8,128)(2,1)}, bf16[864,640]{1,0:T(8,128)(2,1)}, u32[]{:S(2)}, u32[]{:S(2)}) collective-permute-start(bf16[864,640]{1,0:T(8,128)(2,1)} %get-tuple-element.34), channel_id=1, source_target_pairs={{0,1},{1,0},{2,3},{3,2},{4,5},{5,4},{6,7},{7,6},{8,9},{9,8},{10,11... | collective-permute-start | bytes 3317768 | tf_op jit(solution)/shard_map/ppermute | solution.py:60
  81.4 93.3 %collective-permute-start.17 = (bf16[864,640]{1,0:T(8,128)(2,1)}, bf16[864,640]{1,0:T(8,128)(2,1)S(1)}, u32[]{:S(2)}, u32[]{:S(2)}) collective-permute-start(bf16[864,640]{1,0:T(8,128)(2,1)} %get-tuple-element.35), channel_id=1, source_target_pairs={{0,16},{4,20},{8,24},{12,28},{16,0},{20,4},{24,8},{28,12},{1,17},{... | collective-permute-start | bytes 3317768 | tf_op jit(solution)/shard_map/ppermute | solution.py:54
  83.5 92.4 %collective-permute-start.21 = (bf16[864,640]{1,0:T(8,128)(2,1)}, bf16[864,640]{1,0:T(8,128)(2,1)S(1)}, u32[]{:S(2)}, u32[]{:S(2)}) collective-permute-start(bf16[864,640]{1,0:T(8,128)(2,1)} %get-tuple-element.33), channel_id=1, source_target_pairs={{0,24},{4,28},{8,0},{12,4},{16,8},{20,12},{24,16},{28,20},{1,25},{... | collective-permute-start | bytes 3317768 | tf_op jit(solution)/shard_map/ppermute | solution.py:54
  103.4 75.7 %collective-permute-start.12 = (bf16[864,640]{1,0:T(8,128)(2,1)}, bf16[864,640]{1,0:T(8,128)(2,1)}, u32[]{:S(2)}, u32[]{:S(2)}) collective-permute-start(bf16[864,640]{1,0:T(8,128)(2,1)} %collective-permute-done.11), channel_id=1, source_target_pairs={{0,1},{1,0},{2,3},{3,2},{4,5},{5,4},{6,7},{7,6},{8,9},{9,8},{10,11... | collective-permute-start | bytes 3317768 | tf_op jit(solution)/shard_map/ppermute | solution.py:60
  105.8 76.9 %collective-permute-start.15 = (bf16[864,640]{1,0:T(8,128)(2,1)S(1)}, bf16[864,640]{1,0:T(8,128)(2,1)}, u32[]{:S(2)}, u32[]{:S(2)}) collective-permute-start(bf16[864,640]{1,0:T(8,128)(2,1)S(1)} %collective-permute-done.13), channel_id=1, source_target_pairs={{0,4},{4,0},{8,12},{12,8},{16,20},{20,16},{24,28},{28,24},{1,5},{5... | collective-permute-start | bytes 3317768 | tf_op jit(solution)/shard_map/ppermute | solution.py:60
  109.4 75.0 %collective-permute-start.14 = (bf16[864,640]{1,0:T(8,128)(2,1)S(1)}, bf16[864,640]{1,0:T(8,128)(2,1)S(1)}, u32[]{:S(2)}, u32[]{:S(2)}) collective-permute-start(bf16[864,640]{1,0:T(8,128)(2,1)S(1)} %collective-permute-done.13), channel_id=1, source_target_pairs={{0,1},{1,0},{2,3},{3,2},{4,5},{5,4},{6,7},{7,6},{8,9},{9,8},{10,11... | collective-permute-start | bytes 3317768 | tf_op jit(solution)/shard_map/ppermute | solution.py:60
  175.9 45.4 %collective-permute-start.23 = (bf16[864,640]{1,0:T(8,128)(2,1)S(1)}, bf16[864,640]{1,0:T(8,128)(2,1)S(1)}, u32[]{:S(2)}, u32[]{:S(2)}) collective-permute-start(bf16[864,640]{1,0:T(8,128)(2,1)S(1)} %collective-permute-done.21), channel_id=1, source_target_pairs={{0,4},{4,0},{8,12},{12,8},{16,20},{20,16},{24,28},{28,24},{1,5},{5... | collective-permute-start | bytes 3317768 | tf_op jit(solution)/shard_map/ppermute | solution.py:60
  179.1 48.2 %collective-permute-start.18 = (bf16[864,640]{1,0:T(8,128)(2,1)S(1)}, bf16[864,640]{1,0:T(8,128)(2,1)S(1)}, u32[]{:S(2)}, u32[]{:S(2)}) collective-permute-start(bf16[864,640]{1,0:T(8,128)(2,1)S(1)} %collective-permute-done.17), channel_id=1, source_target_pairs={{0,1},{1,0},{2,3},{3,2},{4,5},{5,4},{6,7},{7,6},{8,9},{9,8},{10,11... | collective-permute-start | bytes 3317768 | tf_op jit(solution)/shard_map/ppermute | solution.py:60
  182.6 44.2 %collective-permute-start.16 = (bf16[864,640]{1,0:T(8,128)(2,1)}, bf16[864,640]{1,0:T(8,128)(2,1)S(1)}, u32[]{:S(2)}, u32[]{:S(2)}) collective-permute-start(bf16[864,640]{1,0:T(8,128)(2,1)} %collective-permute-done.15), channel_id=1, source_target_pairs={{0,1},{1,0},{2,3},{3,2},{4,5},{5,4},{6,7},{7,6},{8,9},{9,8},{10,11... | collective-permute-start | bytes 3317768 | tf_op jit(solution)/shard_map/ppermute | solution.py:60
  184.4 43.7 %collective-permute-start.22 = (bf16[864,640]{1,0:T(8,128)(2,1)S(1)}, bf16[864,640]{1,0:T(8,128)(2,1)S(1)}, u32[]{:S(2)}, u32[]{:S(2)}) collective-permute-start(bf16[864,640]{1,0:T(8,128)(2,1)S(1)} %collective-permute-done.21), channel_id=1, source_target_pairs={{0,1},{1,0},{2,3},{3,2},{4,5},{5,4},{6,7},{7,6},{8,9},{9,8},{10,11... | collective-permute-start | bytes 3317768 | tf_op jit(solution)/shard_map/ppermute | solution.py:60
  197.7 30.0 %collective-permute-start.20 = (bf16[864,640]{1,0:T(8,128)(2,1)S(1)}, bf16[864,640]{1,0:T(8,128)(2,1)S(1)}, u32[]{:S(2)}, u32[]{:S(2)}) collective-permute-start(bf16[864,640]{1,0:T(8,128)(2,1)S(1)} %collective-permute-done.19), channel_id=1, source_target_pairs={{0,1},{1,0},{2,3},{3,2},{4,5},{5,4},{6,7},{7,6},{8,9},{9,8},{10,11... | collective-permute-start | bytes 3317768 | tf_op jit(solution)/shard_map/ppermute | solution.py:60
  251.3 54.1 %collective-permute-start.33 = (bf16[3,2,160,640]{3,2,0,1:T(8,128)(2,1)}, bf16[3,2,160,640]{3,2,0,1:T(8,128)(2,1)}, u32[]{:S(2)}, u32[]{:S(2)}) collective-permute-start(bf16[3,2,160,640]{3,2,0,1:T(8,128)(2,1)} %dynamic-slice_bitcast_fusion.1), channel_id=1, source_target_pairs={{0,8},{4,12},{8,0},{12,4},{16,24},{20,28},{24,16},{28,20},{1,9},{5... | collective-permute-start | bytes 3686408 | tf_op jit(solution)/shard_map/ppermute | solution.py:60
  253.9 55.0 %collective-permute-start.25 = (bf16[3,2,160,640]{3,2,0,1:T(8,128)(2,1)}, bf16[3,2,160,640]{3,2,0,1:T(8,128)(2,1)}, u32[]{:S(2)}, u32[]{:S(2)}) collective-permute-start(bf16[3,2,160,640]{3,2,0,1:T(8,128)(2,1)} %dynamic-slice_bitcast_fusion.2), channel_id=1, source_target_pairs={{0,2},{1,3},{2,0},{3,1},{4,6},{5,7},{6,4},{7,5},{8,10},{9,11},{10,... | collective-permute-start | bytes 3686408 | tf_op jit(solution)/shard_map/ppermute | solution.py:60
  308.9 31.1 %collective-permute-start.43 = (bf16[3,160,640]{2,1,0:T(8,128)(2,1)S(1)}, bf16[3,160,640]{2,1,0:T(8,128)(2,1)S(1)}, u32[]{:S(2)}, u32[]{:S(2)}) collective-permute-start(bf16[3,160,640]{2,1,0:T(8,128)(2,1)S(1)} %fusion.62), channel_id=1, source_target_pairs={{0,16},{4,20},{8,24},{12,28},{16,0},{20,4},{24,8},{28,12},{1,17},{... | collective-permute-start | bytes 1843208 | tf_op jit(solution)/shard_map/ppermute | solution.py:60
  310.7 31.0 %collective-permute-start.26 = (bf16[3,160,640]{2,1,0:T(8,128)(2,1)S(1)}, bf16[3,160,640]{2,1,0:T(8,128)(2,1)S(1)}, u32[]{:S(2)}, u32[]{:S(2)}) collective-permute-start(bf16[3,160,640]{2,1,0:T(8,128)(2,1)S(1)} %dynamic-slice_bitcast_fusion.9), channel_id=1, source_target_pairs={{0,8},{4,12},{8,0},{12,4},{16,24},{20,28},{24,16},{28,20},{1,9},{5... | collective-permute-start | bytes 1843208 | tf_op jit(solution)/shard_map/ppermute | solution.py:60
  322.3 55.9 %collective-permute-start.35 = (bf16[3,160,640]{2,1,0:T(8,128)(2,1)S(1)}, bf16[3,160,640]{2,1,0:T(8,128)(2,1)S(1)}, u32[]{:S(2)}, u32[]{:S(2)}) collective-permute-start(bf16[3,160,640]{2,1,0:T(8,128)(2,1)S(1)} %fusion.63), channel_id=1, source_target_pairs={{0,16},{4,20},{8,24},{12,28},{16,0},{20,4},{24,8},{28,12},{1,17},{... | collective-permute-start | bytes 1843208 | tf_op jit(solution)/shard_map/ppermute | solution.py:60
  340.4 38.1 %collective-permute-start.44 = (bf16[3,160,640]{2,1,0:T(8,128)(2,1)S(1)}, bf16[3,160,640]{2,1,0:T(8,128)(2,1)S(1)}, u32[]{:S(2)}, u32[]{:S(2)}) collective-permute-start(bf16[3,160,640]{2,1,0:T(8,128)(2,1)S(1)} %add_convert_fusion), channel_id=1, source_target_pairs={{0,4},{4,0},{8,12},{12,8},{16,20},{20,16},{24,28},{28,24},{1,5},{5... | collective-permute-start | bytes 1843208 | tf_op jit(solution)/shard_map/ppermute | solution.py:60
  341.8 49.6 %collective-permute-start.27 = (bf16[3,160,640]{2,1,0:T(8,128)(2,1)S(1)}, bf16[3,160,640]{2,1,0:T(8,128)(2,1)S(1)}, u32[]{:S(2)}, u32[]{:S(2)}) collective-permute-start(bf16[3,160,640]{2,1,0:T(8,128)(2,1)S(1)} %fusion.64), channel_id=1, source_target_pairs={{0,16},{4,20},{8,24},{12,28},{16,0},{20,4},{24,8},{28,12},{1,17},{... | collective-permute-start | bytes 1843208 | tf_op jit(solution)/shard_map/ppermute | solution.py:60
  378.7 39.6 %collective-permute-start.45 = (bf16[2,3,160,640]{3,2,1,0:T(8,128)(2,1)S(1)}, bf16[2,3,160,640]{3,2,1,0:T(8,128)(2,1)S(1)}, u32[]{:S(2)}, u32[]{:S(2)}) collective-permute-start(bf16[2,3,160,640]{3,2,1,0:T(8,128)(2,1)S(1)} %get-tuple-element.38.refs_10_), channel_id=1, source_target_pairs={{0,2},{1,3},{2,0},{3,1},{4,6},{5,7},{6,4},{7,5},{8,10},{9,11},{10,... | collective-permute-start | bytes 3686408 | tf_op jit(solution)/shard_map/ppermute | solution.py:60
  406.1 38.0 %collective-permute-start.46 = (bf16[2,3,160,640]{3,2,1,0:T(8,128)(2,1)S(1)}, bf16[2,3,160,640]{3,2,1,0:T(8,128)(2,1)S(1)}, u32[]{:S(2)}, u32[]{:S(2)}) collective-permute-start(bf16[2,3,160,640]{3,2,1,0:T(8,128)(2,1)S(1)} %get-tuple-element.38.refs_10_), channel_id=1, source_target_pairs={{0,8},{4,12},{8,0},{12,4},{16,24},{20,28},{24,16},{28,20},{1,9},{5... | collective-permute-start | bytes 3686408 | tf_op jit(solution)/shard_map/ppermute | solution.py:60
  418.3 52.1 %collective-permute-start.47 = (bf16[2,3,160,640]{3,2,1,0:T(8,128)(2,1)S(1)}, bf16[2,3,160,640]{3,2,1,0:T(8,128)(2,1)S(1)}, u32[]{:S(2)}, u32[]{:S(2)}) collective-permute-start(bf16[2,3,160,640]{3,2,1,0:T(8,128)(2,1)S(1)} %collective-permute-done.45.refs_11_), channel_id=1, source_target_pairs={{0,8},{4,12},{8,0},{12,4},{16,24},{20,28},{24,16},{28,20},{1,9},{5... | collective-permute-start | bytes 3686408 | tf_op jit(solution)/shard_map/ppermute | solution.py:60
  418.3 55.7 %collective-permute-start.38 = (bf16[2,3,160,640]{3,2,1,0:T(8,128)(2,1)S(1)}, bf16[2,3,160,640]{3,2,1,0:T(8,128)(2,1)S(1)}, u32[]{:S(2)}, u32[]{:S(2)}) collective-permute-start(bf16[2,3,160,640]{3,2,1,0:T(8,128)(2,1)S(1)} %get-tuple-element.40.refs_5_), channel_id=1, source_target_pairs={{0,2},{1,3},{2,0},{3,1},{4,6},{5,7},{6,4},{7,5},{8,10},{9,11},{10,... | collective-permute-start | bytes 3686408 | tf_op jit(solution)/shard_map/ppermute | solution.py:60
  432.9 65.8 %collective-permute-start.39 = (bf16[2,3,160,640]{3,2,1,0:T(8,128)(2,1)S(1)}, bf16[2,3,160,640]{3,2,1,0:T(8,128)(2,1)S(1)}, u32[]{:S(2)}, u32[]{:S(2)}) collective-permute-start(bf16[2,3,160,640]{3,2,1,0:T(8,128)(2,1)S(1)} %collective-permute-done.37.refs_6_), channel_id=1, source_target_pairs={{0,2},{1,3},{2,0},{3,1},{4,6},{5,7},{6,4},{7,5},{8,10},{9,11},{10,... | collective-permute-start | bytes 3686408 | tf_op jit(solution)/shard_map/ppermute | solution.py:60
  444.1 59.1 %collective-permute-start.30 = (bf16[2,3,160,640]{3,2,1,0:T(8,128)(2,1)S(1)}, bf16[2,3,160,640]{3,2,1,0:T(8,128)(2,1)S(1)}, u32[]{:S(2)}, u32[]{:S(2)}) collective-permute-start(bf16[2,3,160,640]{3,2,1,0:T(8,128)(2,1)S(1)} %get-tuple-element.42.refs_0_), channel_id=1, source_target_pairs={{0,4},{4,0},{8,12},{12,8},{16,20},{20,16},{24,28},{28,24},{1,5},{5... | collective-permute-start | bytes 3686408 | tf_op jit(solution)/shard_map/ppermute | solution.py:60
  446.0 57.2 %collective-permute-start.31 = (bf16[2,3,160,640]{3,2,1,0:T(8,128)(2,1)S(1)}, bf16[2,3,160,640]{3,2,1,0:T(8,128)(2,1)S(1)}, u32[]{:S(2)}, u32[]{:S(2)}) collective-permute-start(bf16[2,3,160,640]{3,2,1,0:T(8,128)(2,1)S(1)} %collective-permute-done.29.refs_1_), channel_id=1, source_target_pairs={{0,4},{4,0},{8,12},{12,8},{16,20},{20,16},{24,28},{28,24},{1,5},{5... | collective-permute-start | bytes 3686408 | tf_op jit(solution)/shard_map/ppermute | solution.py:60
  473.5 33.5 %collective-permute-start.48 = (bf16[4,2,3,160,640]{4,3,2,1,0:T(8,128)(2,1)}, bf16[4,2,3,160,640]{4,3,2,1,0:T(8,128)(2,1)}, u32[]{:S(2)}, u32[]{:S(2)}) collective-permute-start(bf16[4,2,3,160,640]{4,3,2,1,0:T(8,128)(2,1)} %pad_maximum_fusion.2), channel_id=1, source_target_pairs={{0,1},{1,0},{2,3},{3,2},{4,5},{5,4},{6,7},{7,6},{8,9},{9,8},{10,11... | collective-permute-start | bytes 14745608 | tf_op jit(solution)/shard_map/ppermute | solution.py:60
  642.5 86.5 %collective-permute-start.62 = (bf16[432,640]{1,0:T(8,128)(2,1)S(1)}, bf16[432,640]{1,0:T(8,128)(2,1)S(1)}, u32[]{:S(2)}, u32[]{:S(2)}) collective-permute-start(bf16[432,640]{1,0:T(8,128)(2,1)S(1)} %get-tuple-element.30), channel_id=1, source_target_pairs={{0,16},{4,20},{8,24},{12,28},{16,0},{20,4},{24,8},{28,12},{1,17},{... | collective-permute-start | bytes 1658888 | tf_op jit(solution)/shard_map/ppermute | solution.py:54
  645.9 91.7 %collective-permute-start.63 = (bf16[432,640]{1,0:T(8,128)(2,1)S(1)}, bf16[432,640]{1,0:T(8,128)(2,1)S(1)}, u32[]{:S(2)}, u32[]{:S(2)}) collective-permute-start(bf16[432,640]{1,0:T(8,128)(2,1)S(1)} %get-tuple-element.29), channel_id=1, source_target_pairs={{0,20},{4,24},{8,28},{12,0},{16,4},{20,8},{24,12},{28,16},{1,21},{... | collective-permute-start | bytes 1658888 | tf_op jit(solution)/shard_map/ppermute | solution.py:54
  648.4 89.3 %collective-permute-start.64 = (bf16[432,640]{1,0:T(8,128)(2,1)S(1)}, bf16[432,640]{1,0:T(8,128)(2,1)S(1)}, u32[]{:S(2)}, u32[]{:S(2)}) collective-permute-start(bf16[432,640]{1,0:T(8,128)(2,1)S(1)} %get-tuple-element.28), channel_id=1, source_target_pairs={{0,24},{4,28},{8,0},{12,4},{16,8},{20,12},{24,16},{28,20},{1,25},{... | collective-permute-start | bytes 1658888 | tf_op jit(solution)/shard_map/ppermute | solution.py:54
  657.0 80.8 %collective-permute-start.65 = (bf16[432,640]{1,0:T(8,128)(2,1)S(1)}, bf16[432,640]{1,0:T(8,128)(2,1)S(1)}, u32[]{:S(2)}, u32[]{:S(2)}) collective-permute-start(bf16[432,640]{1,0:T(8,128)(2,1)S(1)} %get-tuple-element.27), channel_id=1, source_target_pairs={{0,28},{4,0},{8,4},{12,8},{16,12},{20,16},{24,20},{28,24},{1,29},{... | collective-permute-start | bytes 1658888 | tf_op jit(solution)/shard_map/ppermute | solution.py:54
  (55 other events, 1014.1 us)

commit v3 on v2

--- a/solution.py
+++ b/solution.py
@@ -44,10 +44,11 @@
 
 
 BLOCKS = 8
+STRIPS = ((0, 4), (4, 9))
 PIECES = 5
 MOVES = {"x": ("row", 1), "zl": ("row", 2), "zh": ("row", 4), "y": ("col", 2), "k": ("col", 1)}
 REDUCE = (("y", "zl"), ("zl", "y"), ("zl", "y"))
-GATHER = (("zl", "y", "x"), ("zl", "x", "y"), ("x", "y", "zl"))
+GATHER = (("x", "y", "zl"), ("zl", "y", "x"), ("zl", "x", "y"))
 
 
 def row_shift(value, step):
@@ -64,26 +65,41 @@
     return lax.dynamic_index_in_dim(value, index, dim, keepdims=False)
 
 
-def reduce_part(tiles, order, place):
-    left = ["y", "zl"]
-    for name in order:
-        dim = 1 + left.index(name)
-        left.remove(name)
-        received = swap(take(tiles, dim, 1 - place[name]), name)
-        tiles = (take(tiles, dim, place[name]).astype(F32) + received.astype(F32)).astype(BF16)
-    return (tiles.astype(F32) + swap(tiles, "zh").astype(F32)).astype(BF16)
-
-
-def gather_part(mine, order):
-    mine = jnp.stack([mine, swap(mine, order[0])])
-    held = [mine]
-    for name in order[1:]:
-        held = held + [swap(value, name) for value in held]
-    return held + [swap(jnp.stack(held), "k")]
+def halve(tiles, dim, name, place):
+    received = swap(take(tiles, dim, 1 - place[name]), name)
+    return (take(tiles, dim, place[name]).astype(F32) + received.astype(F32)).astype(BF16)
+
+
+def after(value, *others):
+    return lax.optimization_barrier((value, *others))
+
+
+def reduce_and_gather(tiles, place):
+    a, b, c = tiles
+
+    def step(part, which, number):
+        name = REDUCE[which][number]
+        return halve(part, 2 if name == "zl" and number == 0 else 1, name, place)
+
+    a, b = step(a, 0, 0), step(b, 1, 0)
+    c, a = after(c, a)
+    a, b, c = step(a, 0, 1), step(b, 1, 1), step(c, 2, 0)
+    a = (a.astype(F32) + swap(a, "zh").astype(F32)).astype(BF16)
+    c = step(c, 2, 1)
+    b = (b.astype(F32) + swap(b, "zh").astype(F32)).astype(BF16)
+    c = (c.astype(F32) + swap(c, "zh").astype(F32)).astype(BF16)
+    parts = []
+    for mine, order in zip((a, b, c), GATHER):
+        mine = jnp.stack([mine, swap(mine, order[0])])
+        held = [mine]
+        for name in order[1:]:
+            held = held + [swap(value, name) for value in held]
+        parts += held + [swap(jnp.stack(held), "k")]
+    return parts
 
 
 def entry_kernel(acts_ref, momentum_ref, *refs):
-    grads_refs, (new_ref, turned_ref) = refs[:-2], refs[-2:]
+    grads_refs, (new_ref, turned_ref) = refs[:BLOCKS], refs[-2:]
     grads = jnp.concatenate([ref[...] for ref in grads_refs])
     gradient = jnp.dot(acts_ref[...], grads, preferred_element_type=F32)
     momentum_new = 0.95 * momentum_ref[...] + gradient
@@ -91,23 +107,28 @@
     turned_ref[...] = (gradient + 0.95 * momentum_new).T.astype(BF16)
 
 
-def entry(acts_t, momentum, grads):
+def entry(acts_t, momentum, grads, first, held):
     rows, cols = momentum.shape
     tokens = acts_t.shape[1]
     width = cols // 9
-    across = pl.BlockSpec((rows, width), lambda i: (0, i))
+    count = grads[0].shape[1] // width
+    across = pl.BlockSpec((rows, width), lambda i: (0, first + i))
     return pl.pallas_call(
         entry_kernel,
-        out_shape=(jax.ShapeDtypeStruct((rows, cols), F32), jax.ShapeDtypeStruct((cols, rows), BF16)),
-        grid=(9,),
+        out_shape=(jax.ShapeDtypeStruct((rows, cols), F32), jax.ShapeDtypeStruct((count * width, rows), BF16)),
+        grid=(count,),
         in_specs=[pl.BlockSpec((rows, tokens), lambda i: (0, 0)), across]
-        + [pl.BlockSpec((value.shape[0], width), lambda i: (0, i)) for value in grads],
+        + [pl.BlockSpec((value.shape[0], width), lambda i: (0, i)) for value in grads]
+        + [pl.BlockSpec(memory_space=pl.ANY)] * len(held),
         out_specs=(across, pl.BlockSpec((width, rows), lambda i: (i, 0))),
+        input_output_aliases={2 + len(grads): 0} if held else {},
         compiler_params=pltpu.CompilerParams(vmem_limit_bytes=40 * 2**20),
         cost_estimate=pl.CostEstimate(
-            flops=2 * rows * cols * tokens, bytes_accessed=rows * cols * 10 + tokens * cols * 2, transcendentals=0
+            flops=2 * rows * count * width * tokens,
+            bytes_accessed=rows * count * width * 10 + tokens * count * width * 2,
+            transcendentals=0,
         ),
-    )(acts_t, momentum, *grads)
+    )(acts_t, momentum, *grads, *held)
 
 
 def finish_kernel(home_ref, weight_ref, update_ref, new_ref):
@@ -196,14 +217,18 @@
 
 def load_columns(place, panel_ref, source, sem):
     width = source.shape[0]
-    rows = panel_ref.shape[3]
-    group = 2 * place["x"] + place["k"]
+    rows = panel_ref.shape[2]
+    group = 2 * place["x"]
     copies = []
     for b in range(BLOCKS + 3):
         j = lax.rem(b - group + 2 * BLOCKS, BLOCKS)
-        block = panel_ref.at[j, 0, pl.ds(pl.multiple_of(place["x"] * width, 16), width)]
-        copies.append(pltpu.make_async_copy(block, source.at[:, pl.ds(b * rows, rows)], sem.at[b]))
-        copies[-1].start()
+        for which, (first, last) in enumerate(STRIPS):
+            ninth = width // 9
+            start = pl.multiple_of((2 * first + place["x"] * (last - first)) * ninth, 16)
+            block = panel_ref.at[j, pl.ds(start, (last - first) * ninth)]
+            there = source.at[pl.ds(first * ninth, (last - first) * ninth), pl.ds(b * rows, rows)]
+            copies.append(pltpu.make_async_copy(block, there, sem.at[len(STRIPS) * b + which]))
+            copies[-1].start()
     return copies
 
 
@@ -250,7 +275,7 @@
 
 
 def products(place, panel, parts):
-    blocks, _, quarter, rows = panel.shape
+    blocks, quarter, rows = panel.shape
     width = quarter // 2
     e = rows // 4
     anywhere = pl.BlockSpec(memory_space=pl.ANY)
@@ -266,7 +291,7 @@
             pltpu.VMEM((blocks // 2, 4, e, rows), BF16),
             pltpu.VMEM((blocks, width, rows), F32),
             pltpu.SemaphoreType.DMA((4,)),
-            pltpu.SemaphoreType.DMA((blocks + 3,)),
+            pltpu.SemaphoreType.DMA((len(STRIPS) * (blocks + 3),)),
             pltpu.SemaphoreType.DMA,
         ],
         compiler_params=pltpu.CompilerParams(vmem_limit_bytes=60 * 2**20),
@@ -284,32 +309,38 @@
     quarter = cols // 4
     half = quarter // 2
     e = rows // 4
-    group = 2 * x + core
-
-    along = {0: out_grads, 2: swap(out_grads, "zl"), 4: swap(out_grads, "zh")}
-    along[6] = swap(along[4], "zl")
-    along |= {bits + 1: swap(value, "x") for bits, value in along.items()}
+    group = 2 * x
+
     token_acts = jnp.zeros((4, *acts.shape), BF16)
     for bit in range(4):
         value = lax.ppermute(acts, "col", [(i, i ^ bit) for i in range(4)]) if bit else acts
         token_acts = lax.dynamic_update_slice(token_acts, value[None], (col ^ bit, 0, 0))
     token_acts = token_acts.reshape(BLOCKS, -1, rows)
-    acts_t = jnp.concatenate([take(token_acts, 0, row ^ bits) for bits in along]).T
-    momentum_new, turned = entry(acts_t, momentum, list(along.values()))
-    pieces = turned.reshape(4, quarter, rows)
-
-    panel = jnp.zeros((BLOCKS, 2, quarter, rows), BF16)
-    for step in range(4):
-        piece = take(pieces, 0, (z + step) % 4)
-        if step:
-            piece = row_shift(piece, 2 * step)
-        source = 2 * ((z - step + 4) % 4)
-        beside = swap(piece, "x")
-        for block, value in ((source + x, piece), (source + 1 - x, beside)):
-            j = (block - group + 8) % 8
-            panel = lax.dynamic_update_slice(panel, value[None, None], (j, 0, 0, 0))
-            panel = lax.dynamic_update_slice(panel, swap(value, "k")[None, None], (j, 1, 0, 0))
-    deep = panel.reshape(BLOCKS, 2 * quarter, rows)
+    acts_t = jnp.concatenate([take(token_acts, 0, row ^ bits) for bits in (0, 2, 4, 6, 1, 3, 5, 7)]).T
+
+    panel = jnp.zeros((BLOCKS, quarter, rows), BF16)
+    ninth = cols // 9
+    held = ()
+    for first, last in STRIPS:
+        along = {0: out_grads[:, first * ninth : last * ninth]}
+        along |= {2: swap(along[0], "zl"), 4: swap(along[0], "zh")}
+        along[6] = swap(along[4], "zl")
+        along |= {bits + 1: swap(value, "x") for bits, value in along.items()}
+        momentum_new, turned = entry(acts_t, momentum, list(along.values()), first, held)
+        held = (momentum_new,)
+        share = (last - first) * ninth // 4
+        start = first * ninth // 4
+        pieces = turned.reshape(4, share, rows)
+        for step in range(4):
+            piece = take(pieces, 0, (z + step) % 4)
+            if step:
+                piece = row_shift(piece, 2 * step)
+            source = 2 * ((z - step + 4) % 4)
+            beside = swap(piece, "x")
+            for block, value in ((source + x, piece), (source + 1 - x, beside)):
+                j = (block - group + 8) % 8
+                panel = lax.dynamic_update_slice(panel, value[None], (j, start, 0))
+    deep = panel
 
     def tile(deep, i, j):
         return lax.dot_general(deep[i], deep[j], (((0,), (0,)), ((), ())), preferred_element_type=F32).astype(BF16)
@@ -317,9 +348,13 @@
     wanted = (((0, 0), (1, 0), (2, 0)), ((4, 4), (5, 4), (6, 4)), ((3, 0), (7, 4), (4, 0)))
     parts = []
     for which in range(3):
-        tiles = jnp.stack([tile(deep, i, j) for i, j in wanted[which]]).reshape(3, 2, 2, e, rows)
-        deep, tiles = lax.optimization_barrier((deep, tiles))
-        parts += gather_part(reduce_part(tiles, REDUCE[which], place), GATHER[which])
+        if which == 2:
+            deep, parts[0] = after(deep, parts[0])
+        tiles = [tile(deep, (i + k) % BLOCKS, j + k) for k in range(2) for i, j in wanted[which]]
+        tiles = jnp.stack(tiles).reshape(2, 3, 2, 2, e, rows)
+        deep, tiles = after(deep, tiles)
+        parts.append(halve(tiles, 0, "k", place))
+    parts = reduce_and_gather(parts, place)
 
     places = jnp.stack([place[name] for name in ("x", "k", "y", "zh", "zl")]).astype(jnp.int32)
     one, two, lanes = products(places, panel, parts)
@@ -332,8 +367,13 @@
     square_root = jnp.sqrt(schatten)
     scale = math.sqrt(rows * BLOCKS) / jnp.sqrt(square_root)
 
-    home = jnp.zeros((BLOCKS, half, rows), BF16)
-    own = lax.dynamic_slice(panel, (0, 0, x * half, 0), (BLOCKS, 1, half, rows))[:, 0]
+    home = jnp.zeros((cols, rows), BF16)
+    own = []
+    for first, last in STRIPS:
+        share = (last - first) * ninth // 8
+        start = 2 * (first * ninth // 8) + x * share
+        own.append(lax.dynamic_slice(panel, (0, start, 0), (BLOCKS, share, rows)))
+    own = jnp.concatenate(own, axis=1)
     for step in range(BLOCKS):
         there = (row + step) % 8
         value = (
@@ -344,8 +384,12 @@
         value = (scale * value).astype(BF16)
         if step:
             value = row_shift(value, step)
-        home = lax.dynamic_update_slice(home, value[None], ((row - step + 8) % 8, 0, 0))
-    update, weight_new = finish(home.reshape(cols, rows), weight)
+        for first, last in STRIPS:
+            share = (last - first) * ninth // 8
+            low = first * ninth // 8
+            there = first * ninth + (row - step + 8) % 8 * share
+            home = lax.dynamic_update_slice(home, value[low : low + share], (there, 0))
+    update, weight_new = finish(home, weight)
     return (momentum_new, update, weight_new)
 
 

time: 757 us -> 723 us (0.955)
  waiting for transfers between devices: 488 us -> 422 us
  local copies, waits for them, and re-layouts: 37.5 us -> 59.1 us
  matrix products: 18.5 us -> 30.8 us
    ppermute x43 -> x49, waiting for transfers between devices: 331 us -> 266 us  [swap(): return lax.ppermute(value, axis, [(i, i ^ bit) for i in range(size)])]
    dot_general x9 -> x18, matrix products: 18.5 us -> 30.8 us  [tile(): lax.dot_general(deep[i], deep[j], (((0,), (0,)), ((), ())), preferred_ele...]
    unnamed x42 -> x64, local copies, waits for them, and re-layouts: 5.53 us -> 15 us
    ppermute x17 -> x20, starting transfers between devices: 14.1 us -> 19.1 us  [row_shift(): lax.ppermute(value, 'row', [(i, (i + step) % BLOCKS) for i in range(BLOCK...]
    ppermute x43 -> x49, starting transfers between devices: 41.2 us -> 36.2 us  [swap(): return lax.ppermute(value, axis, [(i, i ^ bit) for i in range(size)])]
    dynamic_update_slice x23 -> x30, local copies, waits for them, and re-layouts: 12 us -> 15.6 us  [the longest x14 15 us: fast_body(): panel = lax.dynamic_update_slice(panel, value[None], (j, start, 0))]
    ppermute x17 -> x20, waiting for transfers between devices: 155 us -> 155 us  [row_shift(): lax.ppermute(value, 'row', [(i, (i + step) % BLOCKS) for i in range(BLOCK...]
  transfers between devices with their start and end apart: 66 -> 75, of which waited for: 33 -> 31; matrix products, arithmetic and copies ran while one was open for 7% -> 12% of each run, Pallas kernels for 0% -> 1%
where the time goes in v3:
time: 723 us; the launch traced here: 717 us
  waiting for transfers between devices  422 us (58%)
  Pallas kernels  106 us (15%)
  starting transfers between devices  62.8 us (9%)
  local copies, waits for them, and re-layouts  59.1 us (8%)
  other arithmetic  33.5 us (5%)
  matrix products  30.8 us (4%)
    ppermute x49, waiting for transfers between devices, swap(): return lax.ppermute(value, axis, [(i, i ^ bit) for i in range(size)])  266 us
    ppermute x20, waiting for transfers between devices, row_shift(): lax.ppermute(value, 'row', [(i, (i + step) % BLOCKS) for i in range(BLOCK...  155 us
    pallas_call x1, Pallas kernels, products(): pl.pallas_call(product_kernel, out_shape=(whole, whole, jax.ShapeDtypeStr...  89.6 us
    ppermute x49, starting transfers between devices, swap(): return lax.ppermute(value, axis, [(i, i ^ bit) for i in range(size)])  36.2 us
    dot_general x18, matrix products, tile(): lax.dot_general(deep[i], deep[j], (((0,), (0,)), ((), ())), preferred_ele...  30.8 us
    ppermute x20, starting transfers between devices, row_shift(): lax.ppermute(value, 'row', [(i, (i + step) % BLOCKS) for i in range(BLOCK...  19.1 us
    unnamed x64, local copies, waits for them, and re-layouts  15 us
    dynamic_update_slice x14, local copies, waits for them, and re-layouts, fast_body(): panel = lax.dynamic_update_slice(panel, value[None], (j, start, 0))  15 us
  transfers between devices with their start and end apart: 75, of which 31 were waited for; matrix products, arithmetic and copies ran while one was open for 12% of the time, Pallas kernels for 1%

profile of v3, /device:TPU:27, one launch (start us, length us, event | category | flops | bytes accessed | tf_op | source)
XLA Modules:
  0.0 716.9 jit_solution(2767248410847678668)
XLA Ops:
  9.1 7.3 %collective-permute-done.11.refs_2_ = bf16[64,1536]{1,0:T(8,128)(2,1)S(1)} collective-permute-done((bf16[64,1536]{1,0:T(8,128)(2,1)S(1)}, bf16[64,1536]{1,0:T(8,128)(2,1)S(1)}, u32[]{:S(2)}, u32[]{:S(2)}) %collective-permute-start.11) | collective-permute-done | bytes 196640 | tf_op jit(solution)/shard_map/ppermute | solution.py:61
  19.5 7.9 %collective-permute-done.12.refs_3_ = bf16[64,1536]{1,0:T(8,128)(2,1)S(1)} collective-permute-done((bf16[64,1536]{1,0:T(8,128)(2,1)S(1)}, bf16[64,1536]{1,0:T(8,128)(2,1)S(1)}, u32[]{:S(2)}, u32[]{:S(2)}) %collective-permute-start.12) | collective-permute-done | bytes 196640 | tf_op jit(solution)/shard_map/ppermute | solution.py:61
  40.8 3.5 copy-done
  45.3 4.8 shard_map.67
  56.3 12.3 %collective-permute-done.9.refs_7_ = bf16[64,1920]{1,0:T(8,128)(2,1)S(1)} collective-permute-done((bf16[64,1920]{1,0:T(8,128)(2,1)S(1)}, bf16[64,1920]{1,0:T(8,128)(2,1)S(1)}, u32[]{:S(2)}, u32[]{:S(2)}) %collective-permute-start.9) | collective-permute-done | bytes 245792 | tf_op jit(solution)/shard_map/ppermute | solution.py:61
  68.6 3.5 copy-done.1
  72.1 4.8 shard_map.68
  77.2 18.4 %collective-permute-done.20 = bf16[384,640]{1,0:T(8,128)(2,1)} collective-permute-done((bf16[384,640]{1,0:T(8,128)(2,1)}, bf16[384,640]{1,0:T(8,128)(2,1)}, u32[]{:S(2)}, u32[]{:S(2)}) %collective-permute-start.20) | collective-permute-done | bytes 491552 | tf_op jit(solution)/shard_map/ppermute | solution.py:55
  107.0 8.9 %collective-permute-done.23 = bf16[384,640]{1,0:T(8,128)(2,1)S(1)} collective-permute-done((bf16[384,640]{1,0:T(8,128)(2,1)S(1)}, bf16[384,640]{1,0:T(8,128)(2,1)S(1)}, u32[]{:S(2)}, u32[]{:S(2)}) %collective-permute-start.23) | collective-permute-done | bytes 491552 | tf_op jit(solution)/shard_map/ppermute | solution.py:61
  122.1 7.3 %collective-permute-done.25 = bf16[480,640]{1,0:T(8,128)(2,1)S(1)} collective-permute-done((bf16[480,640]{1,0:T(8,128)(2,1)S(1)}, bf16[480,640]{1,0:T(8,128)(2,1)S(1)}, u32[]{:S(2)}, u32[]{:S(2)}) %collective-permute-start.25) | collective-permute-done | bytes 614432 | tf_op jit(solution)/shard_map/ppermute | solution.py:55
  129.5 39.9 %collective-permute-done.27 = bf16[480,640]{1,0:T(8,128)(2,1)S(1)} collective-permute-done((bf16[480,640]{1,0:T(8,128)(2,1)}, bf16[480,640]{1,0:T(8,128)(2,1)S(1)}, u32[]{:S(2)}, u32[]{:S(2)}) %collective-permute-start.27) | collective-permute-done | bytes 614432 | tf_op jit(solution)/shard_map/ppermute | solution.py:55
  174.3 5.5 collective-permute-done.28
  181.6 11.4 %collective-permute-done.30 = bf16[480,640]{1,0:T(8,128)(2,1)S(1)} collective-permute-done((bf16[480,640]{1,0:T(8,128)(2,1)S(1)}, bf16[480,640]{1,0:T(8,128)(2,1)S(1)}, u32[]{:S(2)}, u32[]{:S(2)}) %collective-permute-start.30) | collective-permute-done | bytes 614432 | tf_op jit(solution)/shard_map/ppermute | solution.py:61
  207.0 5.8 collective-permute-start.31
  249.6 21.5 %collective-permute-done.33 = bf16[3,2,160,640]{3,2,0,1:T(8,128)(2,1)} collective-permute-done((bf16[3,2,160,640]{3,2,0,1:T(8,128)(2,1)}, bf16[3,2,160,640]{3,2,0,1:T(8,128)(2,1)}, u32[]{:S(2)}, u32[]{:S(2)}) %collective-permute-start.33) | collective-permute-done | bytes 1228832 | tf_op jit(solution)/shard_map/ppermute | solution.py:61
  280.6 12.4 %collective-permute-done.43 = bf16[3,160,640]{2,1,0:T(8,128)(2,1)S(1)} collective-permute-done((bf16[3,160,640]{2,1,0:T(8,128)(2,1)S(1)}, bf16[3,160,640]{2,1,0:T(8,128)(2,1)S(1)}, u32[]{:S(2)}, u32[]{:S(2)}) %collective-permute-start.43) | collective-permute-done | bytes 614432 | tf_op jit(solution)/shard_map/ppermute | solution.py:61
  295.6 21.0 %collective-permute-done.50 = bf16[3,2,160,640]{3,2,0,1:T(8,128)(2,1)S(1)} collective-permute-done((bf16[3,2,160,640]{3,2,0,1:T(8,128)(2,1)S(1)}, bf16[3,2,160,640]{3,2,0,1:T(8,128)(2,1)S(1)}, u32[]{:S(2)}, u32[]{:S(2)}) %collective-permute-start.50) | collective-permute-done | bytes 1228832 | tf_op jit(solution)/shard_map/ppermute | solution.py:61
  318.2 11.6 %collective-permute-done.34 = bf16[3,160,640]{2,1,0:T(8,128)(2,1)S(1)} collective-permute-done((bf16[3,160,640]{2,1,0:T(8,128)(2,1)S(1)}, bf16[3,160,640]{2,1,0:T(8,128)(2,1)S(1)}, u32[]{:S(2)}, u32[]{:S(2)}) %collective-permute-start.34) | collective-permute-done | bytes 614432 | tf_op jit(solution)/shard_map/ppermute | solution.py:61
  333.2 28.7 %collective-permute-done.35 = bf16[3,160,640]{2,1,0:T(8,128)(2,1)S(1)} collective-permute-done((bf16[3,160,640]{2,1,0:T(8,128)(2,1)S(1)}, bf16[3,160,640]{2,1,0:T(8,128)(2,1)S(1)}, u32[]{:S(2)}, u32[]{:S(2)}) %collective-permute-start.35) | collective-permute-done | bytes 614432 | tf_op jit(solution)/shard_map/ppermute | solution.py:61
  363.8 22.5 %collective-permute-done.52 = bf16[3,160,640]{2,1,0:T(8,128)(2,1)S(1)} collective-permute-done((bf16[3,160,640]{2,1,0:T(8,128)(2,1)S(1)}, bf16[3,160,640]{2,1,0:T(8,128)(2,1)S(1)}, u32[]{:S(2)}, u32[]{:S(2)}) %collective-permute-start.52) | collective-permute-done | bytes 614432 | tf_op jit(solution)/shard_map/ppermute | solution.py:61
  388.1 13.3 %collective-permute-done.53 = bf16[3,160,640]{2,1,0:T(8,128)(2,1)S(1)} collective-permute-done((bf16[3,160,640]{2,1,0:T(8,128)(2,1)S(1)}, bf16[3,160,640]{2,1,0:T(8,128)(2,1)S(1)}, u32[]{:S(2)}, u32[]{:S(2)}) %collective-permute-start.53) | collective-permute-done | bytes 614432 | tf_op jit(solution)/shard_map/ppermute | solution.py:61
  403.5 13.2 %collective-permute-done.37.refs_1_ = bf16[2,3,160,640]{3,2,1,0:T(8,128)(2,1)S(1)} collective-permute-done((bf16[2,3,160,640]{3,2,1,0:T(8,128)(2,1)S(1)}, bf16[2,3,160,640]{3,2,1,0:T(8,128)(2,1)S(1)}, u32[]{:S(2)}, u32[]{:S(2)}) %collective-permute-start.37) | collective-permute-done | bytes 1228832 | tf_op jit(solution)/shard_map/ppermute | solution.py:61
  417.7 24.3 %collective-permute-done.54.refs_11_ = bf16[2,3,160,640]{3,2,1,0:T(8,128)(2,1)S(1)} collective-permute-done((bf16[2,3,160,640]{3,2,1,0:T(8,128)(2,1)S(1)}, bf16[2,3,160,640]{3,2,1,0:T(8,128)(2,1)S(1)}, u32[]{:S(2)}, u32[]{:S(2)}) %collective-permute-start.54) | collective-permute-done | bytes 1228832 | tf_op jit(solution)/shard_map/ppermute | solution.py:61
  442.4 25.9 %collective-permute-done.48.refs_8_ = bf16[2,3,160,640]{3,2,1,0:T(8,128)(2,1)S(1)} collective-permute-done((bf16[2,3,160,640]{3,2,1,0:T(8,128)(2,1)S(1)}, bf16[2,3,160,640]{3,2,1,0:T(8,128)(2,1)S(1)}, u32[]{:S(2)}, u32[]{:S(2)}) %collective-permute-start.48) | collective-permute-done | bytes 1228832 | tf_op jit(solution)/shard_map/ppermute | solution.py:61
  481.3 7.0 collective-permute-done.40.refs_4_
  488.3 7.0 collective-permute-done.57.refs_14_
  495.4 89.6 %shard_map.69 = (f32[8,432,640]{2,1,0:T(8,128)}, f32[8,432,640]{2,1,0:T(8,128)}, f32[8,640]{1,0:T(8,128)}) custom-call(s32[5]{0:T(128)} %stack.158.place_ref, bf16[8,864,640]{2,1,0:T(8,128)(2,1)} %bitcast_dynamic-update-slice_fusion.panel_ref, bf16[2,3,160,640]{3,2,1,0:T(8,128)(2,1)} %copy-done.13, bf16[2,3,160,640]{3,2,1,0:T(8,128)(2,1)} %copy-done.16, ...), custom_call_target="tpu_custom_call" | custom-call | flops 45298483200 | bytes 29491200 | tf_op jit(solution)/shard_map/pallas_call | solution.py:283
  622.5 16.8 %collective-permute-done.68 = bf16[432,640]{1,0:T(8,128)(2,1)S(1)} collective-permute-done((bf16[432,640]{1,0:T(8,128)(2,1)S(1)}, bf16[432,640]{1,0:T(8,128)(2,1)S(1)}, u32[]{:S(2)}, u32[]{:S(2)}) %collective-permute-start.68) | collective-permute-done | bytes 552992 | tf_op jit(solution)/shard_map/ppermute | solution.py:55
  639.4 10.5 %collective-permute-done.69 = bf16[432,640]{1,0:T(8,128)(2,1)S(1)} collective-permute-done((bf16[432,640]{1,0:T(8,128)(2,1)S(1)}, bf16[432,640]{1,0:T(8,128)(2,1)S(1)}, u32[]{:S(2)}, u32[]{:S(2)}) %collective-permute-start.69) | collective-permute-done | bytes 552992 | tf_op jit(solution)/shard_map/ppermute | solution.py:55
  649.9 9.0 %collective-permute-done.70 = bf16[432,640]{1,0:T(8,128)(2,1)S(1)} collective-permute-done((bf16[432,640]{1,0:T(8,128)(2,1)S(1)}, bf16[432,640]{1,0:T(8,128)(2,1)S(1)}, u32[]{:S(2)}, u32[]{:S(2)}) %collective-permute-start.70) | collective-permute-done | bytes 552992 | tf_op jit(solution)/shard_map/ppermute | solution.py:55
  659.0 50.1 %collective-permute-done.71 = bf16[432,640]{1,0:T(8,128)(2,1)S(1)} collective-permute-done((bf16[432,640]{1,0:T(8,128)(2,1)S(1)}, bf16[432,640]{1,0:T(8,128)(2,1)S(1)}, u32[]{:S(2)}, u32[]{:S(2)}) %collective-permute-start.71) | collective-permute-done | bytes 552992 | tf_op jit(solution)/shard_map/ppermute | solution.py:55
  709.6 7.1 shard_map.70
  (296 shorter events, 181.1 us)
Async XLA Ops:
  7.4 30.0 %collective-permute-start.4 = (bf16[64,1920]{1,0:T(8,128)(2,1)S(1)}, bf16[64,1920]{1,0:T(8,128)(2,1)S(1)}, u32[]{:S(2)}, u32[]{:S(2)}) collective-permute-start(bf16[64,1920]{1,0:T(8,128)(2,1)S(1)} %slice.124.refs_0_), channel_id=1, source_target_pairs={{0,16},{4,20},{8,24},{12,28},{16,0},{20,4},{24,8},{28,12},{1,17},{... | collective-permute-start | bytes 737288 | tf_op jit(solution)/shard_map/ppermute | solution.py:61
  52.2 43.5 %collective-permute-start.20 = (bf16[384,640]{1,0:T(8,128)(2,1)}, bf16[384,640]{1,0:T(8,128)(2,1)}, u32[]{:S(2)}, u32[]{:S(2)}) collective-permute-start(bf16[384,640]{1,0:T(8,128)(2,1)} %get-tuple-element.54), channel_id=1, source_target_pairs={{0,16},{4,20},{8,24},{12,28},{16,0},{20,4},{24,8},{28,12},{1,17},{... | collective-permute-start | bytes 1474568 | tf_op jit(solution)/shard_map/ppermute | solution.py:55
  54.8 41.0 %collective-permute-start.22 = (bf16[384,640]{1,0:T(8,128)(2,1)}, bf16[384,640]{1,0:T(8,128)(2,1)S(1)}, u32[]{:S(2)}, u32[]{:S(2)}) collective-permute-start(bf16[384,640]{1,0:T(8,128)(2,1)} %get-tuple-element.52), channel_id=1, source_target_pairs={{0,24},{4,28},{8,0},{12,4},{16,8},{20,12},{24,16},{28,20},{1,25},{... | collective-permute-start | bytes 1474568 | tf_op jit(solution)/shard_map/ppermute | solution.py:55
  54.8 42.3 %collective-permute-start.17 = (bf16[384,640]{1,0:T(8,128)(2,1)}, bf16[384,640]{1,0:T(8,128)(2,1)}, u32[]{:S(2)}, u32[]{:S(2)}) collective-permute-start(bf16[384,640]{1,0:T(8,128)(2,1)} %get-tuple-element.53), channel_id=1, source_target_pairs={{0,4},{4,0},{8,12},{12,8},{16,20},{20,16},{24,28},{28,24},{1,5},{5... | collective-permute-start | bytes 1474568 | tf_op jit(solution)/shard_map/ppermute | solution.py:61
  118.2 51.1 %collective-permute-start.27 = (bf16[480,640]{1,0:T(8,128)(2,1)}, bf16[480,640]{1,0:T(8,128)(2,1)S(1)}, u32[]{:S(2)}, u32[]{:S(2)}) collective-permute-start(bf16[480,640]{1,0:T(8,128)(2,1)} %get-tuple-element.49), channel_id=1, source_target_pairs={{0,16},{4,20},{8,24},{12,28},{16,0},{20,4},{24,8},{28,12},{1,17},{... | collective-permute-start | bytes 1843208 | tf_op jit(solution)/shard_map/ppermute | solution.py:55
  119.9 50.6 %collective-permute-start.24 = (bf16[480,640]{1,0:T(8,128)(2,1)}, bf16[480,640]{1,0:T(8,128)(2,1)S(1)}, u32[]{:S(2)}, u32[]{:S(2)}) collective-permute-start(bf16[480,640]{1,0:T(8,128)(2,1)} %get-tuple-element.48), channel_id=1, source_target_pairs={{0,4},{4,0},{8,12},{12,8},{16,20},{20,16},{24,28},{28,24},{1,5},{5... | collective-permute-start | bytes 1843208 | tf_op jit(solution)/shard_map/ppermute | solution.py:61
  120.5 51.7 %collective-permute-start.29 = (bf16[480,640]{1,0:T(8,128)(2,1)}, bf16[480,640]{1,0:T(8,128)(2,1)S(1)}, u32[]{:S(2)}, u32[]{:S(2)}) collective-permute-start(bf16[480,640]{1,0:T(8,128)(2,1)} %get-tuple-element.47), channel_id=1, source_target_pairs={{0,24},{4,28},{8,0},{12,4},{16,8},{20,12},{24,16},{28,20},{1,25},{... | collective-permute-start | bytes 1843208 | tf_op jit(solution)/shard_map/ppermute | solution.py:55
  129.5 43.1 %collective-permute-start.26 = (bf16[480,640]{1,0:T(8,128)(2,1)S(1)}, bf16[480,640]{1,0:T(8,128)(2,1)S(1)}, u32[]{:S(2)}, u32[]{:S(2)}) collective-permute-start(bf16[480,640]{1,0:T(8,128)(2,1)S(1)} %collective-permute-done.25), channel_id=1, source_target_pairs={{0,4},{4,0},{8,12},{12,8},{16,20},{20,16},{24,28},{28,24},{1,5},{5... | collective-permute-start | bytes 1843208 | tf_op jit(solution)/shard_map/ppermute | solution.py:61
  241.5 31.2 %collective-permute-start.32 = (bf16[3,2,2,160,640]{4,3,0,1,2:T(8,128)(2,1)}, bf16[3,2,2,160,640]{4,3,0,1,2:T(8,128)(2,1)}, u32[]{:S(2)}, u32[]{:S(2)}) collective-permute-start(bf16[3,2,2,160,640]{4,3,0,1,2:T(8,128)(2,1)} %copy_bitcast_fusion.1), channel_id=1, source_target_pairs={{0,1},{1,0},{2,3},{3,2},{4,5},{5,4},{6,7},{7,6},{8,9},{9,8},{10,11... | collective-permute-start | bytes 7372808 | tf_op jit(solution)/shard_map/ppermute | solution.py:61
  242.7 28.4 %collective-permute-start.33 = (bf16[3,2,160,640]{3,2,0,1:T(8,128)(2,1)}, bf16[3,2,160,640]{3,2,0,1:T(8,128)(2,1)}, u32[]{:S(2)}, u32[]{:S(2)}) collective-permute-start(bf16[3,2,160,640]{3,2,0,1:T(8,128)(2,1)} %dynamic-slice_bitcast_fusion.2), channel_id=1, source_target_pairs={{0,2},{1,3},{2,0},{3,1},{4,6},{5,7},{6,4},{7,5},{8,10},{9,11},{10,... | collective-permute-start | bytes 3686408 | tf_op jit(solution)/shard_map/ppermute | solution.py:61
  249.6 28.1 %collective-permute-start.42 = (bf16[3,2,160,640]{3,2,0,1:T(8,128)(2,1)}, bf16[3,2,160,640]{3,2,0,1:T(8,128)(2,1)}, u32[]{:S(2)}, u32[]{:S(2)}) collective-permute-start(bf16[3,2,160,640]{3,2,0,1:T(8,128)(2,1)} %dynamic-slice_bitcast_fusion.1), channel_id=1, source_target_pairs={{0,8},{4,12},{8,0},{12,4},{16,24},{20,28},{24,16},{28,20},{1,9},{5... | collective-permute-start | bytes 3686408 | tf_op jit(solution)/shard_map/ppermute | solution.py:61
  275.9 40.7 %collective-permute-start.50 = (bf16[3,2,160,640]{3,2,0,1:T(8,128)(2,1)S(1)}, bf16[3,2,160,640]{3,2,0,1:T(8,128)(2,1)S(1)}, u32[]{:S(2)}, u32[]{:S(2)}) collective-permute-start(bf16[3,2,160,640]{3,2,0,1:T(8,128)(2,1)S(1)} %dynamic-slice_bitcast_fusion), channel_id=1, source_target_pairs={{0,8},{4,12},{8,0},{12,4},{16,24},{20,28},{24,16},{28,20},{1,9},{5... | collective-permute-start | bytes 3686408 | tf_op jit(solution)/shard_map/ppermute | solution.py:61
  280.5 49.3 %collective-permute-start.34 = (bf16[3,160,640]{2,1,0:T(8,128)(2,1)S(1)}, bf16[3,160,640]{2,1,0:T(8,128)(2,1)S(1)}, u32[]{:S(2)}, u32[]{:S(2)}) collective-permute-start(bf16[3,160,640]{2,1,0:T(8,128)(2,1)S(1)} %dynamic-slice_bitcast_fusion.5), channel_id=1, source_target_pairs={{0,8},{4,12},{8,0},{12,4},{16,24},{20,28},{24,16},{28,20},{1,9},{5... | collective-permute-start | bytes 1843208 | tf_op jit(solution)/shard_map/ppermute | solution.py:61
  293.1 37.4 %collective-permute-start.44 = (bf16[3,160,640]{2,1,0:T(8,128)(2,1)S(1)}, bf16[3,160,640]{2,1,0:T(8,128)(2,1)S(1)}, u32[]{:S(2)}, u32[]{:S(2)}) collective-permute-start(bf16[3,160,640]{2,1,0:T(8,128)(2,1)S(1)} %fusion.43), channel_id=1, source_target_pairs={{0,16},{4,20},{8,24},{12,28},{16,0},{20,4},{24,8},{28,12},{1,17},{... | collective-permute-start | bytes 1843208 | tf_op jit(solution)/shard_map/ppermute | solution.py:61
  330.0 32.0 %collective-permute-start.35 = (bf16[3,160,640]{2,1,0:T(8,128)(2,1)S(1)}, bf16[3,160,640]{2,1,0:T(8,128)(2,1)S(1)}, u32[]{:S(2)}, u32[]{:S(2)}) collective-permute-start(bf16[3,160,640]{2,1,0:T(8,128)(2,1)S(1)} %fusion.44), channel_id=1, source_target_pairs={{0,16},{4,20},{8,24},{12,28},{16,0},{20,4},{24,8},{28,12},{1,17},{... | collective-permute-start | bytes 1843208 | tf_op jit(solution)/shard_map/ppermute | solution.py:61
  330.7 31.9 %collective-permute-start.45 = (bf16[3,160,640]{2,1,0:T(8,128)(2,1)S(1)}, bf16[3,160,640]{2,1,0:T(8,128)(2,1)S(1)}, u32[]{:S(2)}, u32[]{:S(2)}) collective-permute-start(bf16[3,160,640]{2,1,0:T(8,128)(2,1)S(1)} %add_convert_fusion.1), channel_id=1, source_target_pairs={{0,8},{4,12},{8,0},{12,4},{16,24},{20,28},{24,16},{28,20},{1,9},{5... | collective-permute-start | bytes 1843208 | tf_op jit(solution)/shard_map/ppermute | solution.py:61
  333.1 53.2 %collective-permute-start.52 = (bf16[3,160,640]{2,1,0:T(8,128)(2,1)S(1)}, bf16[3,160,640]{2,1,0:T(8,128)(2,1)S(1)}, u32[]{:S(2)}, u32[]{:S(2)}) collective-permute-start(bf16[3,160,640]{2,1,0:T(8,128)(2,1)S(1)} %fusion.42), channel_id=1, source_target_pairs={{0,16},{4,20},{8,24},{12,28},{16,0},{20,4},{24,8},{28,12},{1,17},{... | collective-permute-start | bytes 1843208 | tf_op jit(solution)/shard_map/ppermute | solution.py:61
  362.8 39.4 %collective-permute-start.46 = (bf16[2,3,160,640]{3,2,1,0:T(8,128)(2,1)S(1)}, bf16[2,3,160,640]{3,2,1,0:T(8,128)(2,1)S(1)}, u32[]{:S(2)}, u32[]{:S(2)}) collective-permute-start(bf16[2,3,160,640]{3,2,1,0:T(8,128)(2,1)S(1)} %get-tuple-element.60.refs_5_), channel_id=1, source_target_pairs={{0,2},{1,3},{2,0},{3,1},{4,6},{5,7},{6,4},{7,5},{8,10},{9,11},{10,... | collective-permute-start | bytes 3686408 | tf_op jit(solution)/shard_map/ppermute | solution.py:61
  386.7 30.0 %collective-permute-start.37 = (bf16[2,3,160,640]{3,2,1,0:T(8,128)(2,1)S(1)}, bf16[2,3,160,640]{3,2,1,0:T(8,128)(2,1)S(1)}, u32[]{:S(2)}, u32[]{:S(2)}) collective-permute-start(bf16[2,3,160,640]{3,2,1,0:T(8,128)(2,1)S(1)} %get-tuple-element.62.refs_0_), channel_id=1, source_target_pairs={{0,2},{1,3},{2,0},{3,1},{4,6},{5,7},{6,4},{7,5},{8,10},{9,11},{10,... | collective-permute-start | bytes 3686408 | tf_op jit(solution)/shard_map/ppermute | solution.py:61
  387.9 28.9 %collective-permute-start.47 = (bf16[2,3,160,640]{3,2,1,0:T(8,128)(2,1)S(1)}, bf16[2,3,160,640]{3,2,1,0:T(8,128)(2,1)S(1)}, u32[]{:S(2)}, u32[]{:S(2)}) collective-permute-start(bf16[2,3,160,640]{3,2,1,0:T(8,128)(2,1)S(1)} %get-tuple-element.60.refs_5_), channel_id=1, source_target_pairs={{0,4},{4,0},{8,12},{12,8},{16,20},{20,16},{24,28},{28,24},{1,5},{5... | collective-permute-start | bytes 3686408 | tf_op jit(solution)/shard_map/ppermute | solution.py:61
  401.6 40.3 %collective-permute-start.54 = (bf16[2,3,160,640]{3,2,1,0:T(8,128)(2,1)S(1)}, bf16[2,3,160,640]{3,2,1,0:T(8,128)(2,1)S(1)}, u32[]{:S(2)}, u32[]{:S(2)}) collective-permute-start(bf16[2,3,160,640]{3,2,1,0:T(8,128)(2,1)S(1)} %get-tuple-element.58.refs_10_), channel_id=1, source_target_pairs={{0,4},{4,0},{8,12},{12,8},{16,20},{20,16},{24,28},{28,24},{1,5},{5... | collective-permute-start | bytes 3686408 | tf_op jit(solution)/shard_map/ppermute | solution.py:61
  402.2 66.2 %collective-permute-start.48 = (bf16[2,3,160,640]{3,2,1,0:T(8,128)(2,1)S(1)}, bf16[2,3,160,640]{3,2,1,0:T(8,128)(2,1)S(1)}, u32[]{:S(2)}, u32[]{:S(2)}) collective-permute-start(bf16[2,3,160,640]{3,2,1,0:T(8,128)(2,1)S(1)} %collective-permute-done.46.refs_6_), channel_id=1, source_target_pairs={{0,4},{4,0},{8,12},{12,8},{16,20},{20,16},{24,28},{28,24},{1,5},{5... | collective-permute-start | bytes 3686408 | tf_op jit(solution)/shard_map/ppermute | solution.py:61
  403.2 70.0 %collective-permute-start.38 = (bf16[2,3,160,640]{3,2,1,0:T(8,128)(2,1)S(1)}, bf16[2,3,160,640]{3,2,1,0:T(8,128)(2,1)S(1)}, u32[]{:S(2)}, u32[]{:S(2)}) collective-permute-start(bf16[2,3,160,640]{3,2,1,0:T(8,128)(2,1)S(1)} %get-tuple-element.62.refs_0_), channel_id=1, source_target_pairs={{0,8},{4,12},{8,0},{12,4},{16,24},{20,28},{24,16},{28,20},{1,9},{5... | collective-permute-start | bytes 3686408 | tf_op jit(solution)/shard_map/ppermute | solution.py:61
  416.7 56.4 %collective-permute-start.39 = (bf16[2,3,160,640]{3,2,1,0:T(8,128)(2,1)S(1)}, bf16[2,3,160,640]{3,2,1,0:T(8,128)(2,1)S(1)}, u32[]{:S(2)}, u32[]{:S(2)}) collective-permute-start(bf16[2,3,160,640]{3,2,1,0:T(8,128)(2,1)S(1)} %collective-permute-done.37.refs_1_), channel_id=1, source_target_pairs={{0,8},{4,12},{8,0},{12,4},{16,24},{20,28},{24,16},{28,20},{1,9},{5... | collective-permute-start | bytes 3686408 | tf_op jit(solution)/shard_map/ppermute | solution.py:61
  416.7 59.6 %collective-permute-start.55 = (bf16[2,3,160,640]{3,2,1,0:T(8,128)(2,1)S(1)}, bf16[2,3,160,640]{3,2,1,0:T(8,128)(2,1)S(1)}, u32[]{:S(2)}, u32[]{:S(2)}) collective-permute-start(bf16[2,3,160,640]{3,2,1,0:T(8,128)(2,1)S(1)} %get-tuple-element.58.refs_10_), channel_id=1, source_target_pairs={{0,2},{1,3},{2,0},{3,1},{4,6},{5,7},{6,4},{7,5},{8,10},{9,11},{10,... | collective-permute-start | bytes 3686408 | tf_op jit(solution)/shard_map/ppermute | solution.py:61
  442.0 34.4 %collective-permute-start.56 = (bf16[2,3,160,640]{3,2,1,0:T(8,128)(2,1)S(1)}, bf16[2,3,160,640]{3,2,1,0:T(8,128)(2,1)S(1)}, u32[]{:S(2)}, u32[]{:S(2)}) collective-permute-start(bf16[2,3,160,640]{3,2,1,0:T(8,128)(2,1)S(1)} %collective-permute-done.54.refs_11_), channel_id=1, source_target_pairs={{0,2},{1,3},{2,0},{3,1},{4,6},{5,7},{6,4},{7,5},{8,10},{9,11},{10,... | collective-permute-start | bytes 3686408 | tf_op jit(solution)/shard_map/ppermute | solution.py:61
  611.3 97.9 %collective-permute-start.72 = (bf16[432,640]{1,0:T(8,128)(2,1)S(1)}, bf16[432,640]{1,0:T(8,128)(2,1)S(1)}, u32[]{:S(2)}, u32[]{:S(2)}) collective-permute-start(bf16[432,640]{1,0:T(8,128)(2,1)S(1)} %get-tuple-element.41), channel_id=1, source_target_pairs={{0,20},{4,24},{8,28},{12,0},{16,4},{20,8},{24,12},{28,16},{1,21},{... | collective-permute-start | bytes 1658888 | tf_op jit(solution)/shard_map/ppermute | solution.py:55
  618.2 31.7 %collective-permute-start.69 = (bf16[432,640]{1,0:T(8,128)(2,1)S(1)}, bf16[432,640]{1,0:T(8,128)(2,1)S(1)}, u32[]{:S(2)}, u32[]{:S(2)}) collective-permute-start(bf16[432,640]{1,0:T(8,128)(2,1)S(1)} %get-tuple-element.44), channel_id=1, source_target_pairs={{0,8},{4,12},{8,16},{12,20},{16,24},{20,28},{24,0},{28,4},{1,9},{5... | collective-permute-start | bytes 1658888 | tf_op jit(solution)/shard_map/ppermute | solution.py:55
  621.1 37.9 %collective-permute-start.70 = (bf16[432,640]{1,0:T(8,128)(2,1)S(1)}, bf16[432,640]{1,0:T(8,128)(2,1)S(1)}, u32[]{:S(2)}, u32[]{:S(2)}) collective-permute-start(bf16[432,640]{1,0:T(8,128)(2,1)S(1)} %get-tuple-element.43), channel_id=1, source_target_pairs={{0,12},{4,16},{8,20},{12,24},{16,28},{20,0},{24,4},{28,8},{1,13},{... | collective-permute-start | bytes 1658888 | tf_op jit(solution)/shard_map/ppermute | solution.py:55
  621.1 88.0 %collective-permute-start.71 = (bf16[432,640]{1,0:T(8,128)(2,1)S(1)}, bf16[432,640]{1,0:T(8,128)(2,1)S(1)}, u32[]{:S(2)}, u32[]{:S(2)}) collective-permute-start(bf16[432,640]{1,0:T(8,128)(2,1)S(1)} %get-tuple-element.42), channel_id=1, source_target_pairs={{0,16},{4,20},{8,24},{12,28},{16,0},{20,4},{24,8},{28,12},{1,17},{... | collective-permute-start | bytes 1658888 | tf_op jit(solution)/shard_map/ppermute | solution.py:55
  639.3 70.0 %collective-permute-start.73 = (bf16[432,640]{1,0:T(8,128)(2,1)S(1)}, bf16[432,640]{1,0:T(8,128)(2,1)S(1)}, u32[]{:S(2)}, u32[]{:S(2)}) collective-permute-start(bf16[432,640]{1,0:T(8,128)(2,1)S(1)} %get-tuple-element.40), channel_id=1, source_target_pairs={{0,24},{4,28},{8,0},{12,4},{16,8},{20,12},{24,16},{28,20},{1,25},{... | collective-permute-start | bytes 1658888 | tf_op jit(solution)/shard_map/ppermute | solution.py:55
  649.9 59.6 %collective-permute-start.74 = (bf16[432,640]{1,0:T(8,128)(2,1)S(1)}, bf16[432,640]{1,0:T(8,128)(2,1)S(1)}, u32[]{:S(2)}, u32[]{:S(2)}) collective-permute-start(bf16[432,640]{1,0:T(8,128)(2,1)S(1)} %get-tuple-element.39), channel_id=1, source_target_pairs={{0,28},{4,0},{8,4},{12,8},{16,12},{20,16},{24,20},{28,24},{1,29},{... | collective-permute-start | bytes 1658888 | tf_op jit(solution)/shard_map/ppermute | solution.py:55
  (75 other events, 1340.1 us)

commit v4 on v3

--- a/solution.py
+++ b/solution.py
@@ -176,6 +176,31 @@
     lax.fori_loop(*blocks, near, 0)
 
 
+def apply_all(source, tiles, total):
+    rows = total.shape[2]
+
+    def straight(b, _):
+        start = pl.multiple_of(b * rows, 128)
+        total[b] = jnp.dot(
+            source[:, pl.ds(start, 4 * rows)], tiles[b].reshape(4 * rows, rows), preferred_element_type=F32
+        )
+        return 0
+
+    def turned(b, _):
+        start = pl.multiple_of(b * rows, 128)
+        for d in range(1, 4):
+            total[lax.rem(b + d, BLOCKS)] += lax.dot_general(
+                source[:, pl.ds(start, rows)],
+                tiles[b, d].reshape(rows, rows),
+                (((1,), (1,)), ((), ())),
+                preferred_element_type=F32,
+            )
+        return 0
+
+    lax.fori_loop(0, BLOCKS, straight, 0)
+    lax.fori_loop(0, BLOCKS, turned, 0)
+
+
 def apply_far(source, fours, total):
     rows = total.shape[2]
 
@@ -262,8 +287,7 @@
     for b in range(BLOCKS + 3):
         source[:, b * rows : (b + 1) * rows] = total[b % BLOCKS].astype(BF16)
     out.wait()
-    total[...] = jnp.zeros_like(total)
-    apply_near(source, tiles, total, (0, BLOCKS), 0, 4)
+    apply_all(source, tiles, total)
     apply_far(source, fours, total)
     out = pltpu.make_async_copy(total, z_ref, out_sem)
     out.start()

time: 723 us -> 724 us (level)
  no operation moved by 1% of the time
where the time goes in v4:
time: 724 us; the launch traced here: 717 us
  waiting for transfers between devices  422 us (58%)
  Pallas kernels  107 us (15%)
  starting transfers between devices  62.8 us (9%)
  local copies, waits for them, and re-layouts  59.1 us (8%)
  other arithmetic  33.5 us (5%)
  matrix products  30.8 us (4%)
    ppermute x49, waiting for transfers between devices, swap(): return lax.ppermute(value, axis, [(i, i ^ bit) for i in range(size)])  266 us
    ppermute x20, waiting for transfers between devices, row_shift(): lax.ppermute(value, 'row', [(i, (i + step) % BLOCKS) for i in range(BLOCK...  155 us
    pallas_call x1, Pallas kernels, products(): pl.pallas_call(product_kernel, out_shape=(whole, whole, jax.ShapeDtypeStr...  90 us
    ppermute x49, starting transfers between devices, swap(): return lax.ppermute(value, axis, [(i, i ^ bit) for i in range(size)])  36.2 us
    dot_general x18, matrix products, tile(): lax.dot_general(deep[i], deep[j], (((0,), (0,)), ((), ())), preferred_ele...  30.8 us
    ppermute x20, starting transfers between devices, row_shift(): lax.ppermute(value, 'row', [(i, (i + step) % BLOCKS) for i in range(BLOCK...  19.1 us
    unnamed x64, local copies, waits for them, and re-layouts  15 us
    dynamic_update_slice x14, local copies, waits for them, and re-layouts, fast_body(): panel = lax.dynamic_update_slice(panel, value[None], (j, start, 0))  15 us
  transfers between devices with their start and end apart: 75, of which 31 were waited for; matrix products, arithmetic and copies ran while one was open for 12% of the time, Pallas kernels for 1%

profile of v4, /device:TPU:27, one launch (start us, length us, event | category | flops | bytes accessed | tf_op | source)
XLA Modules:
  0.0 717.3 jit_solution(5413762926808293496)
XLA Ops:
  9.1 7.3 %collective-permute-done.11.refs_2_ = bf16[64,1536]{1,0:T(8,128)(2,1)S(1)} collective-permute-done((bf16[64,1536]{1,0:T(8,128)(2,1)S(1)}, bf16[64,1536]{1,0:T(8,128)(2,1)S(1)}, u32[]{:S(2)}, u32[]{:S(2)}) %collective-permute-start.11) | collective-permute-done | bytes 196640 | tf_op jit(solution)/shard_map/ppermute | solution.py:61
  19.5 7.9 %collective-permute-done.12.refs_3_ = bf16[64,1536]{1,0:T(8,128)(2,1)S(1)} collective-permute-done((bf16[64,1536]{1,0:T(8,128)(2,1)S(1)}, bf16[64,1536]{1,0:T(8,128)(2,1)S(1)}, u32[]{:S(2)}, u32[]{:S(2)}) %collective-permute-start.12) | collective-permute-done | bytes 196640 | tf_op jit(solution)/shard_map/ppermute | solution.py:61
  40.8 3.5 copy-done
  45.3 4.8 shard_map.67
  56.3 12.3 %collective-permute-done.9.refs_7_ = bf16[64,1920]{1,0:T(8,128)(2,1)S(1)} collective-permute-done((bf16[64,1920]{1,0:T(8,128)(2,1)S(1)}, bf16[64,1920]{1,0:T(8,128)(2,1)S(1)}, u32[]{:S(2)}, u32[]{:S(2)}) %collective-permute-start.9) | collective-permute-done | bytes 245792 | tf_op jit(solution)/shard_map/ppermute | solution.py:61
  68.6 3.5 copy-done.1
  72.1 4.8 shard_map.68
  77.2 18.4 %collective-permute-done.20 = bf16[384,640]{1,0:T(8,128)(2,1)} collective-permute-done((bf16[384,640]{1,0:T(8,128)(2,1)}, bf16[384,640]{1,0:T(8,128)(2,1)}, u32[]{:S(2)}, u32[]{:S(2)}) %collective-permute-start.20) | collective-permute-done | bytes 491552 | tf_op jit(solution)/shard_map/ppermute | solution.py:55
  107.0 8.9 %collective-permute-done.23 = bf16[384,640]{1,0:T(8,128)(2,1)S(1)} collective-permute-done((bf16[384,640]{1,0:T(8,128)(2,1)S(1)}, bf16[384,640]{1,0:T(8,128)(2,1)S(1)}, u32[]{:S(2)}, u32[]{:S(2)}) %collective-permute-start.23) | collective-permute-done | bytes 491552 | tf_op jit(solution)/shard_map/ppermute | solution.py:61
  122.1 7.3 %collective-permute-done.25 = bf16[480,640]{1,0:T(8,128)(2,1)S(1)} collective-permute-done((bf16[480,640]{1,0:T(8,128)(2,1)S(1)}, bf16[480,640]{1,0:T(8,128)(2,1)S(1)}, u32[]{:S(2)}, u32[]{:S(2)}) %collective-permute-start.25) | collective-permute-done | bytes 614432 | tf_op jit(solution)/shard_map/ppermute | solution.py:55
  129.5 39.9 %collective-permute-done.27 = bf16[480,640]{1,0:T(8,128)(2,1)S(1)} collective-permute-done((bf16[480,640]{1,0:T(8,128)(2,1)}, bf16[480,640]{1,0:T(8,128)(2,1)S(1)}, u32[]{:S(2)}, u32[]{:S(2)}) %collective-permute-start.27) | collective-permute-done | bytes 614432 | tf_op jit(solution)/shard_map/ppermute | solution.py:55
  174.3 5.5 collective-permute-done.28
  181.6 11.4 %collective-permute-done.30 = bf16[480,640]{1,0:T(8,128)(2,1)S(1)} collective-permute-done((bf16[480,640]{1,0:T(8,128)(2,1)S(1)}, bf16[480,640]{1,0:T(8,128)(2,1)S(1)}, u32[]{:S(2)}, u32[]{:S(2)}) %collective-permute-start.30) | collective-permute-done | bytes 614432 | tf_op jit(solution)/shard_map/ppermute | solution.py:61
  207.0 5.8 collective-permute-start.31
  249.6 21.5 %collective-permute-done.33 = bf16[3,2,160,640]{3,2,0,1:T(8,128)(2,1)} collective-permute-done((bf16[3,2,160,640]{3,2,0,1:T(8,128)(2,1)}, bf16[3,2,160,640]{3,2,0,1:T(8,128)(2,1)}, u32[]{:S(2)}, u32[]{:S(2)}) %collective-permute-start.33) | collective-permute-done | bytes 1228832 | tf_op jit(solution)/shard_map/ppermute | solution.py:61
  280.6 12.4 %collective-permute-done.43 = bf16[3,160,640]{2,1,0:T(8,128)(2,1)S(1)} collective-permute-done((bf16[3,160,640]{2,1,0:T(8,128)(2,1)S(1)}, bf16[3,160,640]{2,1,0:T(8,128)(2,1)S(1)}, u32[]{:S(2)}, u32[]{:S(2)}) %collective-permute-start.43) | collective-permute-done | bytes 614432 | tf_op jit(solution)/shard_map/ppermute | solution.py:61
  295.6 21.0 %collective-permute-done.50 = bf16[3,2,160,640]{3,2,0,1:T(8,128)(2,1)S(1)} collective-permute-done((bf16[3,2,160,640]{3,2,0,1:T(8,128)(2,1)S(1)}, bf16[3,2,160,640]{3,2,0,1:T(8,128)(2,1)S(1)}, u32[]{:S(2)}, u32[]{:S(2)}) %collective-permute-start.50) | collective-permute-done | bytes 1228832 | tf_op jit(solution)/shard_map/ppermute | solution.py:61
  318.2 11.6 %collective-permute-done.34 = bf16[3,160,640]{2,1,0:T(8,128)(2,1)S(1)} collective-permute-done((bf16[3,160,640]{2,1,0:T(8,128)(2,1)S(1)}, bf16[3,160,640]{2,1,0:T(8,128)(2,1)S(1)}, u32[]{:S(2)}, u32[]{:S(2)}) %collective-permute-start.34) | collective-permute-done | bytes 614432 | tf_op jit(solution)/shard_map/ppermute | solution.py:61
  333.2 28.7 %collective-permute-done.35 = bf16[3,160,640]{2,1,0:T(8,128)(2,1)S(1)} collective-permute-done((bf16[3,160,640]{2,1,0:T(8,128)(2,1)S(1)}, bf16[3,160,640]{2,1,0:T(8,128)(2,1)S(1)}, u32[]{:S(2)}, u32[]{:S(2)}) %collective-permute-start.35) | collective-permute-done | bytes 614432 | tf_op jit(solution)/shard_map/ppermute | solution.py:61
  363.8 22.5 %collective-permute-done.52 = bf16[3,160,640]{2,1,0:T(8,128)(2,1)S(1)} collective-permute-done((bf16[3,160,640]{2,1,0:T(8,128)(2,1)S(1)}, bf16[3,160,640]{2,1,0:T(8,128)(2,1)S(1)}, u32[]{:S(2)}, u32[]{:S(2)}) %collective-permute-start.52) | collective-permute-done | bytes 614432 | tf_op jit(solution)/shard_map/ppermute | solution.py:61
  388.1 13.3 %collective-permute-done.53 = bf16[3,160,640]{2,1,0:T(8,128)(2,1)S(1)} collective-permute-done((bf16[3,160,640]{2,1,0:T(8,128)(2,1)S(1)}, bf16[3,160,640]{2,1,0:T(8,128)(2,1)S(1)}, u32[]{:S(2)}, u32[]{:S(2)}) %collective-permute-start.53) | collective-permute-done | bytes 614432 | tf_op jit(solution)/shard_map/ppermute | solution.py:61
  403.5 13.2 %collective-permute-done.37.refs_1_ = bf16[2,3,160,640]{3,2,1,0:T(8,128)(2,1)S(1)} collective-permute-done((bf16[2,3,160,640]{3,2,1,0:T(8,128)(2,1)S(1)}, bf16[2,3,160,640]{3,2,1,0:T(8,128)(2,1)S(1)}, u32[]{:S(2)}, u32[]{:S(2)}) %collective-permute-start.37) | collective-permute-done | bytes 1228832 | tf_op jit(solution)/shard_map/ppermute | solution.py:61
  417.7 24.3 %collective-permute-done.54.refs_11_ = bf16[2,3,160,640]{3,2,1,0:T(8,128)(2,1)S(1)} collective-permute-done((bf16[2,3,160,640]{3,2,1,0:T(8,128)(2,1)S(1)}, bf16[2,3,160,640]{3,2,1,0:T(8,128)(2,1)S(1)}, u32[]{:S(2)}, u32[]{:S(2)}) %collective-permute-start.54) | collective-permute-done | bytes 1228832 | tf_op jit(solution)/shard_map/ppermute | solution.py:61
  442.4 25.9 %collective-permute-done.48.refs_8_ = bf16[2,3,160,640]{3,2,1,0:T(8,128)(2,1)S(1)} collective-permute-done((bf16[2,3,160,640]{3,2,1,0:T(8,128)(2,1)S(1)}, bf16[2,3,160,640]{3,2,1,0:T(8,128)(2,1)S(1)}, u32[]{:S(2)}, u32[]{:S(2)}) %collective-permute-start.48) | collective-permute-done | bytes 1228832 | tf_op jit(solution)/shard_map/ppermute | solution.py:61
  481.3 7.0 collective-permute-done.40.refs_4_
  488.3 7.0 collective-permute-done.57.refs_14_
  495.4 90.0 %shard_map.69 = (f32[8,432,640]{2,1,0:T(8,128)}, f32[8,432,640]{2,1,0:T(8,128)}, f32[8,640]{1,0:T(8,128)}) custom-call(s32[5]{0:T(128)} %stack.158.place_ref, bf16[8,864,640]{2,1,0:T(8,128)(2,1)} %bitcast_dynamic-update-slice_fusion.panel_ref, bf16[2,3,160,640]{3,2,1,0:T(8,128)(2,1)} %copy-done.13, bf16[2,3,160,640]{3,2,1,0:T(8,128)(2,1)} %copy-done.16, ...), custom_call_target="tpu_custom_call" | custom-call | flops 45298483200 | bytes 29491200 | tf_op jit(solution)/shard_map/pallas_call | solution.py:307
  622.9 16.8 %collective-permute-done.68 = bf16[432,640]{1,0:T(8,128)(2,1)S(1)} collective-permute-done((bf16[432,640]{1,0:T(8,128)(2,1)S(1)}, bf16[432,640]{1,0:T(8,128)(2,1)S(1)}, u32[]{:S(2)}, u32[]{:S(2)}) %collective-permute-start.68) | collective-permute-done | bytes 552992 | tf_op jit(solution)/shard_map/ppermute | solution.py:55
  639.8 10.5 %collective-permute-done.69 = bf16[432,640]{1,0:T(8,128)(2,1)S(1)} collective-permute-done((bf16[432,640]{1,0:T(8,128)(2,1)S(1)}, bf16[432,640]{1,0:T(8,128)(2,1)S(1)}, u32[]{:S(2)}, u32[]{:S(2)}) %collective-permute-start.69) | collective-permute-done | bytes 552992 | tf_op jit(solution)/shard_map/ppermute | solution.py:55
  650.4 9.0 %collective-permute-done.70 = bf16[432,640]{1,0:T(8,128)(2,1)S(1)} collective-permute-done((bf16[432,640]{1,0:T(8,128)(2,1)S(1)}, bf16[432,640]{1,0:T(8,128)(2,1)S(1)}, u32[]{:S(2)}, u32[]{:S(2)}) %collective-permute-start.70) | collective-permute-done | bytes 552992 | tf_op jit(solution)/shard_map/ppermute | solution.py:55
  659.5 50.1 %collective-permute-done.71 = bf16[432,640]{1,0:T(8,128)(2,1)S(1)} collective-permute-done((bf16[432,640]{1,0:T(8,128)(2,1)S(1)}, bf16[432,640]{1,0:T(8,128)(2,1)S(1)}, u32[]{:S(2)}, u32[]{:S(2)}) %collective-permute-start.71) | collective-permute-done | bytes 552992 | tf_op jit(solution)/shard_map/ppermute | solution.py:55
  710.0 7.1 shard_map.70
  (296 shorter events, 181.1 us)
Async XLA Ops:
  7.4 30.0 %collective-permute-start.4 = (bf16[64,1920]{1,0:T(8,128)(2,1)S(1)}, bf16[64,1920]{1,0:T(8,128)(2,1)S(1)}, u32[]{:S(2)}, u32[]{:S(2)}) collective-permute-start(bf16[64,1920]{1,0:T(8,128)(2,1)S(1)} %slice.124.refs_0_), channel_id=1, source_target_pairs={{0,16},{4,20},{8,24},{12,28},{16,0},{20,4},{24,8},{28,12},{1,17},{... | collective-permute-start | bytes 737288 | tf_op jit(solution)/shard_map/ppermute | solution.py:61
  52.2 43.5 %collective-permute-start.20 = (bf16[384,640]{1,0:T(8,128)(2,1)}, bf16[384,640]{1,0:T(8,128)(2,1)}, u32[]{:S(2)}, u32[]{:S(2)}) collective-permute-start(bf16[384,640]{1,0:T(8,128)(2,1)} %get-tuple-element.54), channel_id=1, source_target_pairs={{0,16},{4,20},{8,24},{12,28},{16,0},{20,4},{24,8},{28,12},{1,17},{... | collective-permute-start | bytes 1474568 | tf_op jit(solution)/shard_map/ppermute | solution.py:55
  54.8 41.0 %collective-permute-start.22 = (bf16[384,640]{1,0:T(8,128)(2,1)}, bf16[384,640]{1,0:T(8,128)(2,1)S(1)}, u32[]{:S(2)}, u32[]{:S(2)}) collective-permute-start(bf16[384,640]{1,0:T(8,128)(2,1)} %get-tuple-element.52), channel_id=1, source_target_pairs={{0,24},{4,28},{8,0},{12,4},{16,8},{20,12},{24,16},{28,20},{1,25},{... | collective-permute-start | bytes 1474568 | tf_op jit(solution)/shard_map/ppermute | solution.py:55
  54.8 42.3 %collective-permute-start.17 = (bf16[384,640]{1,0:T(8,128)(2,1)}, bf16[384,640]{1,0:T(8,128)(2,1)}, u32[]{:S(2)}, u32[]{:S(2)}) collective-permute-start(bf16[384,640]{1,0:T(8,128)(2,1)} %get-tuple-element.53), channel_id=1, source_target_pairs={{0,4},{4,0},{8,12},{12,8},{16,20},{20,16},{24,28},{28,24},{1,5},{5... | collective-permute-start | bytes 1474568 | tf_op jit(solution)/shard_map/ppermute | solution.py:61
  118.2 51.1 %collective-permute-start.27 = (bf16[480,640]{1,0:T(8,128)(2,1)}, bf16[480,640]{1,0:T(8,128)(2,1)S(1)}, u32[]{:S(2)}, u32[]{:S(2)}) collective-permute-start(bf16[480,640]{1,0:T(8,128)(2,1)} %get-tuple-element.49), channel_id=1, source_target_pairs={{0,16},{4,20},{8,24},{12,28},{16,0},{20,4},{24,8},{28,12},{1,17},{... | collective-permute-start | bytes 1843208 | tf_op jit(solution)/shard_map/ppermute | solution.py:55
  119.9 50.6 %collective-permute-start.24 = (bf16[480,640]{1,0:T(8,128)(2,1)}, bf16[480,640]{1,0:T(8,128)(2,1)S(1)}, u32[]{:S(2)}, u32[]{:S(2)}) collective-permute-start(bf16[480,640]{1,0:T(8,128)(2,1)} %get-tuple-element.48), channel_id=1, source_target_pairs={{0,4},{4,0},{8,12},{12,8},{16,20},{20,16},{24,28},{28,24},{1,5},{5... | collective-permute-start | bytes 1843208 | tf_op jit(solution)/shard_map/ppermute | solution.py:61
  120.5 51.7 %collective-permute-start.29 = (bf16[480,640]{1,0:T(8,128)(2,1)}, bf16[480,640]{1,0:T(8,128)(2,1)S(1)}, u32[]{:S(2)}, u32[]{:S(2)}) collective-permute-start(bf16[480,640]{1,0:T(8,128)(2,1)} %get-tuple-element.47), channel_id=1, source_target_pairs={{0,24},{4,28},{8,0},{12,4},{16,8},{20,12},{24,16},{28,20},{1,25},{... | collective-permute-start | bytes 1843208 | tf_op jit(solution)/shard_map/ppermute | solution.py:55
  129.5 43.1 %collective-permute-start.26 = (bf16[480,640]{1,0:T(8,128)(2,1)S(1)}, bf16[480,640]{1,0:T(8,128)(2,1)S(1)}, u32[]{:S(2)}, u32[]{:S(2)}) collective-permute-start(bf16[480,640]{1,0:T(8,128)(2,1)S(1)} %collective-permute-done.25), channel_id=1, source_target_pairs={{0,4},{4,0},{8,12},{12,8},{16,20},{20,16},{24,28},{28,24},{1,5},{5... | collective-permute-start | bytes 1843208 | tf_op jit(solution)/shard_map/ppermute | solution.py:61
  241.5 31.2 %collective-permute-start.32 = (bf16[3,2,2,160,640]{4,3,0,1,2:T(8,128)(2,1)}, bf16[3,2,2,160,640]{4,3,0,1,2:T(8,128)(2,1)}, u32[]{:S(2)}, u32[]{:S(2)}) collective-permute-start(bf16[3,2,2,160,640]{4,3,0,1,2:T(8,128)(2,1)} %copy_bitcast_fusion.1), channel_id=1, source_target_pairs={{0,1},{1,0},{2,3},{3,2},{4,5},{5,4},{6,7},{7,6},{8,9},{9,8},{10,11... | collective-permute-start | bytes 7372808 | tf_op jit(solution)/shard_map/ppermute | solution.py:61
  242.7 28.4 %collective-permute-start.33 = (bf16[3,2,160,640]{3,2,0,1:T(8,128)(2,1)}, bf16[3,2,160,640]{3,2,0,1:T(8,128)(2,1)}, u32[]{:S(2)}, u32[]{:S(2)}) collective-permute-start(bf16[3,2,160,640]{3,2,0,1:T(8,128)(2,1)} %dynamic-slice_bitcast_fusion.2), channel_id=1, source_target_pairs={{0,2},{1,3},{2,0},{3,1},{4,6},{5,7},{6,4},{7,5},{8,10},{9,11},{10,... | collective-permute-start | bytes 3686408 | tf_op jit(solution)/shard_map/ppermute | solution.py:61
  249.6 28.1 %collective-permute-start.42 = (bf16[3,2,160,640]{3,2,0,1:T(8,128)(2,1)}, bf16[3,2,160,640]{3,2,0,1:T(8,128)(2,1)}, u32[]{:S(2)}, u32[]{:S(2)}) collective-permute-start(bf16[3,2,160,640]{3,2,0,1:T(8,128)(2,1)} %dynamic-slice_bitcast_fusion.1), channel_id=1, source_target_pairs={{0,8},{4,12},{8,0},{12,4},{16,24},{20,28},{24,16},{28,20},{1,9},{5... | collective-permute-start | bytes 3686408 | tf_op jit(solution)/shard_map/ppermute | solution.py:61
  275.9 40.7 %collective-permute-start.50 = (bf16[3,2,160,640]{3,2,0,1:T(8,128)(2,1)S(1)}, bf16[3,2,160,640]{3,2,0,1:T(8,128)(2,1)S(1)}, u32[]{:S(2)}, u32[]{:S(2)}) collective-permute-start(bf16[3,2,160,640]{3,2,0,1:T(8,128)(2,1)S(1)} %dynamic-slice_bitcast_fusion), channel_id=1, source_target_pairs={{0,8},{4,12},{8,0},{12,4},{16,24},{20,28},{24,16},{28,20},{1,9},{5... | collective-permute-start | bytes 3686408 | tf_op jit(solution)/shard_map/ppermute | solution.py:61
  280.5 49.3 %collective-permute-start.34 = (bf16[3,160,640]{2,1,0:T(8,128)(2,1)S(1)}, bf16[3,160,640]{2,1,0:T(8,128)(2,1)S(1)}, u32[]{:S(2)}, u32[]{:S(2)}) collective-permute-start(bf16[3,160,640]{2,1,0:T(8,128)(2,1)S(1)} %dynamic-slice_bitcast_fusion.5), channel_id=1, source_target_pairs={{0,8},{4,12},{8,0},{12,4},{16,24},{20,28},{24,16},{28,20},{1,9},{5... | collective-permute-start | bytes 1843208 | tf_op jit(solution)/shard_map/ppermute | solution.py:61
  293.1 37.4 %collective-permute-start.44 = (bf16[3,160,640]{2,1,0:T(8,128)(2,1)S(1)}, bf16[3,160,640]{2,1,0:T(8,128)(2,1)S(1)}, u32[]{:S(2)}, u32[]{:S(2)}) collective-permute-start(bf16[3,160,640]{2,1,0:T(8,128)(2,1)S(1)} %fusion.43), channel_id=1, source_target_pairs={{0,16},{4,20},{8,24},{12,28},{16,0},{20,4},{24,8},{28,12},{1,17},{... | collective-permute-start | bytes 1843208 | tf_op jit(solution)/shard_map/ppermute | solution.py:61
  330.0 32.0 %collective-permute-start.35 = (bf16[3,160,640]{2,1,0:T(8,128)(2,1)S(1)}, bf16[3,160,640]{2,1,0:T(8,128)(2,1)S(1)}, u32[]{:S(2)}, u32[]{:S(2)}) collective-permute-start(bf16[3,160,640]{2,1,0:T(8,128)(2,1)S(1)} %fusion.44), channel_id=1, source_target_pairs={{0,16},{4,20},{8,24},{12,28},{16,0},{20,4},{24,8},{28,12},{1,17},{... | collective-permute-start | bytes 1843208 | tf_op jit(solution)/shard_map/ppermute | solution.py:61
  330.7 31.9 %collective-permute-start.45 = (bf16[3,160,640]{2,1,0:T(8,128)(2,1)S(1)}, bf16[3,160,640]{2,1,0:T(8,128)(2,1)S(1)}, u32[]{:S(2)}, u32[]{:S(2)}) collective-permute-start(bf16[3,160,640]{2,1,0:T(8,128)(2,1)S(1)} %add_convert_fusion.1), channel_id=1, source_target_pairs={{0,8},{4,12},{8,0},{12,4},{16,24},{20,28},{24,16},{28,20},{1,9},{5... | collective-permute-start | bytes 1843208 | tf_op jit(solution)/shard_map/ppermute | solution.py:61
  333.1 53.2 %collective-permute-start.52 = (bf16[3,160,640]{2,1,0:T(8,128)(2,1)S(1)}, bf16[3,160,640]{2,1,0:T(8,128)(2,1)S(1)}, u32[]{:S(2)}, u32[]{:S(2)}) collective-permute-start(bf16[3,160,640]{2,1,0:T(8,128)(2,1)S(1)} %fusion.42), channel_id=1, source_target_pairs={{0,16},{4,20},{8,24},{12,28},{16,0},{20,4},{24,8},{28,12},{1,17},{... | collective-permute-start | bytes 1843208 | tf_op jit(solution)/shard_map/ppermute | solution.py:61
  362.8 39.4 %collective-permute-start.46 = (bf16[2,3,160,640]{3,2,1,0:T(8,128)(2,1)S(1)}, bf16[2,3,160,640]{3,2,1,0:T(8,128)(2,1)S(1)}, u32[]{:S(2)}, u32[]{:S(2)}) collective-permute-start(bf16[2,3,160,640]{3,2,1,0:T(8,128)(2,1)S(1)} %get-tuple-element.60.refs_5_), channel_id=1, source_target_pairs={{0,2},{1,3},{2,0},{3,1},{4,6},{5,7},{6,4},{7,5},{8,10},{9,11},{10,... | collective-permute-start | bytes 3686408 | tf_op jit(solution)/shard_map/ppermute | solution.py:61
  386.7 30.0 %collective-permute-start.37 = (bf16[2,3,160,640]{3,2,1,0:T(8,128)(2,1)S(1)}, bf16[2,3,160,640]{3,2,1,0:T(8,128)(2,1)S(1)}, u32[]{:S(2)}, u32[]{:S(2)}) collective-permute-start(bf16[2,3,160,640]{3,2,1,0:T(8,128)(2,1)S(1)} %get-tuple-element.62.refs_0_), channel_id=1, source_target_pairs={{0,2},{1,3},{2,0},{3,1},{4,6},{5,7},{6,4},{7,5},{8,10},{9,11},{10,... | collective-permute-start | bytes 3686408 | tf_op jit(solution)/shard_map/ppermute | solution.py:61
  387.9 28.9 %collective-permute-start.47 = (bf16[2,3,160,640]{3,2,1,0:T(8,128)(2,1)S(1)}, bf16[2,3,160,640]{3,2,1,0:T(8,128)(2,1)S(1)}, u32[]{:S(2)}, u32[]{:S(2)}) collective-permute-start(bf16[2,3,160,640]{3,2,1,0:T(8,128)(2,1)S(1)} %get-tuple-element.60.refs_5_), channel_id=1, source_target_pairs={{0,4},{4,0},{8,12},{12,8},{16,20},{20,16},{24,28},{28,24},{1,5},{5... | collective-permute-start | bytes 3686408 | tf_op jit(solution)/shard_map/ppermute | solution.py:61
  401.6 40.3 %collective-permute-start.54 = (bf16[2,3,160,640]{3,2,1,0:T(8,128)(2,1)S(1)}, bf16[2,3,160,640]{3,2,1,0:T(8,128)(2,1)S(1)}, u32[]{:S(2)}, u32[]{:S(2)}) collective-permute-start(bf16[2,3,160,640]{3,2,1,0:T(8,128)(2,1)S(1)} %get-tuple-element.58.refs_10_), channel_id=1, source_target_pairs={{0,4},{4,0},{8,12},{12,8},{16,20},{20,16},{24,28},{28,24},{1,5},{5... | collective-permute-start | bytes 3686408 | tf_op jit(solution)/shard_map/ppermute | solution.py:61
  402.2 66.2 %collective-permute-start.48 = (bf16[2,3,160,640]{3,2,1,0:T(8,128)(2,1)S(1)}, bf16[2,3,160,640]{3,2,1,0:T(8,128)(2,1)S(1)}, u32[]{:S(2)}, u32[]{:S(2)}) collective-permute-start(bf16[2,3,160,640]{3,2,1,0:T(8,128)(2,1)S(1)} %collective-permute-done.46.refs_6_), channel_id=1, source_target_pairs={{0,4},{4,0},{8,12},{12,8},{16,20},{20,16},{24,28},{28,24},{1,5},{5... | collective-permute-start | bytes 3686408 | tf_op jit(solution)/shard_map/ppermute | solution.py:61
  403.2 70.0 %collective-permute-start.38 = (bf16[2,3,160,640]{3,2,1,0:T(8,128)(2,1)S(1)}, bf16[2,3,160,640]{3,2,1,0:T(8,128)(2,1)S(1)}, u32[]{:S(2)}, u32[]{:S(2)}) collective-permute-start(bf16[2,3,160,640]{3,2,1,0:T(8,128)(2,1)S(1)} %get-tuple-element.62.refs_0_), channel_id=1, source_target_pairs={{0,8},{4,12},{8,0},{12,4},{16,24},{20,28},{24,16},{28,20},{1,9},{5... | collective-permute-start | bytes 3686408 | tf_op jit(solution)/shard_map/ppermute | solution.py:61
  416.7 56.4 %collective-permute-start.39 = (bf16[2,3,160,640]{3,2,1,0:T(8,128)(2,1)S(1)}, bf16[2,3,160,640]{3,2,1,0:T(8,128)(2,1)S(1)}, u32[]{:S(2)}, u32[]{:S(2)}) collective-permute-start(bf16[2,3,160,640]{3,2,1,0:T(8,128)(2,1)S(1)} %collective-permute-done.37.refs_1_), channel_id=1, source_target_pairs={{0,8},{4,12},{8,0},{12,4},{16,24},{20,28},{24,16},{28,20},{1,9},{5... | collective-permute-start | bytes 3686408 | tf_op jit(solution)/shard_map/ppermute | solution.py:61
  416.7 59.6 %collective-permute-start.55 = (bf16[2,3,160,640]{3,2,1,0:T(8,128)(2,1)S(1)}, bf16[2,3,160,640]{3,2,1,0:T(8,128)(2,1)S(1)}, u32[]{:S(2)}, u32[]{:S(2)}) collective-permute-start(bf16[2,3,160,640]{3,2,1,0:T(8,128)(2,1)S(1)} %get-tuple-element.58.refs_10_), channel_id=1, source_target_pairs={{0,2},{1,3},{2,0},{3,1},{4,6},{5,7},{6,4},{7,5},{8,10},{9,11},{10,... | collective-permute-start | bytes 3686408 | tf_op jit(solution)/shard_map/ppermute | solution.py:61
  442.0 34.4 %collective-permute-start.56 = (bf16[2,3,160,640]{3,2,1,0:T(8,128)(2,1)S(1)}, bf16[2,3,160,640]{3,2,1,0:T(8,128)(2,1)S(1)}, u32[]{:S(2)}, u32[]{:S(2)}) collective-permute-start(bf16[2,3,160,640]{3,2,1,0:T(8,128)(2,1)S(1)} %collective-permute-done.54.refs_11_), channel_id=1, source_target_pairs={{0,2},{1,3},{2,0},{3,1},{4,6},{5,7},{6,4},{7,5},{8,10},{9,11},{10,... | collective-permute-start | bytes 3686408 | tf_op jit(solution)/shard_map/ppermute | solution.py:61
  611.7 97.9 %collective-permute-start.72 = (bf16[432,640]{1,0:T(8,128)(2,1)S(1)}, bf16[432,640]{1,0:T(8,128)(2,1)S(1)}, u32[]{:S(2)}, u32[]{:S(2)}) collective-permute-start(bf16[432,640]{1,0:T(8,128)(2,1)S(1)} %get-tuple-element.41), channel_id=1, source_target_pairs={{0,20},{4,24},{8,28},{12,0},{16,4},{20,8},{24,12},{28,16},{1,21},{... | collective-permute-start | bytes 1658888 | tf_op jit(solution)/shard_map/ppermute | solution.py:55
  618.6 31.7 %collective-permute-start.69 = (bf16[432,640]{1,0:T(8,128)(2,1)S(1)}, bf16[432,640]{1,0:T(8,128)(2,1)S(1)}, u32[]{:S(2)}, u32[]{:S(2)}) collective-permute-start(bf16[432,640]{1,0:T(8,128)(2,1)S(1)} %get-tuple-element.44), channel_id=1, source_target_pairs={{0,8},{4,12},{8,16},{12,20},{16,24},{20,28},{24,0},{28,4},{1,9},{5... | collective-permute-start | bytes 1658888 | tf_op jit(solution)/shard_map/ppermute | solution.py:55
  621.5 37.9 %collective-permute-start.70 = (bf16[432,640]{1,0:T(8,128)(2,1)S(1)}, bf16[432,640]{1,0:T(8,128)(2,1)S(1)}, u32[]{:S(2)}, u32[]{:S(2)}) collective-permute-start(bf16[432,640]{1,0:T(8,128)(2,1)S(1)} %get-tuple-element.43), channel_id=1, source_target_pairs={{0,12},{4,16},{8,20},{12,24},{16,28},{20,0},{24,4},{28,8},{1,13},{... | collective-permute-start | bytes 1658888 | tf_op jit(solution)/shard_map/ppermute | solution.py:55
  621.5 88.0 %collective-permute-start.71 = (bf16[432,640]{1,0:T(8,128)(2,1)S(1)}, bf16[432,640]{1,0:T(8,128)(2,1)S(1)}, u32[]{:S(2)}, u32[]{:S(2)}) collective-permute-start(bf16[432,640]{1,0:T(8,128)(2,1)S(1)} %get-tuple-element.42), channel_id=1, source_target_pairs={{0,16},{4,20},{8,24},{12,28},{16,0},{20,4},{24,8},{28,12},{1,17},{... | collective-permute-start | bytes 1658888 | tf_op jit(solution)/shard_map/ppermute | solution.py:55
  639.7 70.0 %collective-permute-start.73 = (bf16[432,640]{1,0:T(8,128)(2,1)S(1)}, bf16[432,640]{1,0:T(8,128)(2,1)S(1)}, u32[]{:S(2)}, u32[]{:S(2)}) collective-permute-start(bf16[432,640]{1,0:T(8,128)(2,1)S(1)} %get-tuple-element.40), channel_id=1, source_target_pairs={{0,24},{4,28},{8,0},{12,4},{16,8},{20,12},{24,16},{28,20},{1,25},{... | collective-permute-start | bytes 1658888 | tf_op jit(solution)/shard_map/ppermute | solution.py:55
  650.3 59.6 %collective-permute-start.74 = (bf16[432,640]{1,0:T(8,128)(2,1)S(1)}, bf16[432,640]{1,0:T(8,128)(2,1)S(1)}, u32[]{:S(2)}, u32[]{:S(2)}) collective-permute-start(bf16[432,640]{1,0:T(8,128)(2,1)S(1)} %get-tuple-element.39), channel_id=1, source_target_pairs={{0,28},{4,0},{8,4},{12,8},{16,12},{20,16},{24,20},{28,24},{1,29},{... | collective-permute-start | bytes 1658888 | tf_op jit(solution)/shard_map/ppermute | solution.py:55
  (75 other events, 1340.1 us)
